TPU v7x, 32 devices: a whole 2x2x4 slice. The times are simulated.
32 devices in a mesh: tok: 16 (over z, y, x), head: 2 (over core).
Axes of the slice: x: 2, y: 2, z: 4, core: 2. Of those that a mesh axis runs over, the one named last changes fastest.
Arguments:
- source_keys: bfloat16 [4096, 2048], P('tok', 'head'), may hold values from -6 to 6
- source_values: bfloat16 [4096, 2048], P('tok', 'head'), may hold values from -6 to 6
- queries: bfloat16 [4096, 2048], P('tok', 'head'), may hold values from -6 to 6
- fast_weights: float32 [3, 16, 128, 512], P(None, 'head'), may hold values from -0.5 to 0.5
- step_size: float32 [16], P('head'), may hold values from 0.3 to 3
- edit_mask: int32 [16], P('tok'), may hold values 0 or 1
- out_proj: bfloat16 [2048, 2048], P(None, 'head'), may hold values from -0.125 to 0.125
Outputs:
- layer_out: bfloat16 [4096, 2048], P('tok', 'head')
Inputs may be any that keep to these rules, and one draw needn't show every extreme that they name: `edit_mask`: 1 marks a block of source frames whose keys and values update the fast weights, 0 a block of edited frames.
All inputs are finite; a program needn't handle non-finite values.
Results may differ from a plain program's by a relative error of at most 0.0087.
Values may be sent and summed in bfloat16 or wider, within the bound.
No kernel may reach another device: no remote copies, remote signals or barrier semaphores. Data moves between devices by JAX's collectives and lax.ppermute only.
A program may use at most 128 MiB of HBM per device.

v0:
```python
import jax
import jax.numpy as jnp
from jax import lax
from jax.sharding import PartitionSpec as P

ITERS = 5


coef_a = 3.4445
coef_b = -4.775
coef_c = 2.0315
highest = lax.Precision.HIGHEST


def silu_grad(preact):
    sigmoid_value = jax.nn.sigmoid(preact)
    return sigmoid_value * (1.0 + preact * (1.0 - sigmoid_value))


def newton_steps(iterate, gram_matrix, gram_source):
    for sweeps in range(ITERS):
        if sweeps > 0:
            gram_matrix = gram_source(iterate)
        polynomial = coef_b * gram_matrix + coef_c * jnp.einsum(
            "...ij,...jk->...ik", gram_matrix, gram_matrix, precision=highest
        )
        iterate = coef_a * iterate + jnp.einsum(
            "...ij,...jf->...if", polynomial, iterate, precision=highest
        )
    return iterate


def local_gram(iterate):
    return jnp.einsum("...if,...jf->...ij", iterate, iterate, precision=highest)


def orthogonalize(gradients):
    scaling = lax.rsqrt(jnp.sum(gradients * gradients, axis=(-2, -1), keepdims=True) + 1e-06)
    iterate = gradients * scaling
    return newton_steps(iterate, local_gram(iterate), local_gram)


def renormalize(previous, proposed):
    old_norm = jnp.sqrt(jnp.sum(previous * previous, axis=-2, keepdims=True) + 1e-06)
    new_norm = jnp.sqrt(jnp.sum(proposed * proposed, axis=-2, keepdims=True) + 1e-06)
    return proposed * (old_norm / new_norm)


def on_device(source_keys, source_values, queries, fast_weights, step_size, edit_mask, out_proj):
    tok_rows = source_keys.shape[0]
    local_heads = fast_weights.shape[1]
    head_size = fast_weights.shape[2]
    blocks = edit_mask.shape[0]
    token_mask = jnp.repeat(edit_mask, tok_rows // blocks).astype(jnp.bfloat16)
    keys_heads = source_keys.reshape(tok_rows, local_heads, head_size)
    masked_values = (
        source_values.reshape(tok_rows, local_heads, head_size) * token_mask[:, None, None]
    )
    weights_low = fast_weights.astype(jnp.bfloat16)
    gate_pre = jnp.einsum(
        "thd,hdf->htf", keys_heads, weights_low[0], preferred_element_type=jnp.float32
    )
    up_pre = jnp.einsum(
        "thd,hdf->htf", keys_heads, weights_low[2], preferred_element_type=jnp.float32
    )
    hidden = (jax.nn.silu(gate_pre) * up_pre).astype(jnp.bfloat16)
    back_grad = jnp.einsum(
        "thd,hdf->htf", masked_values, weights_low[1], preferred_element_type=jnp.float32
    )
    gate_grad = (back_grad * up_pre * silu_grad(gate_pre)).astype(jnp.bfloat16)
    up_grad = (back_grad * jax.nn.silu(gate_pre)).astype(jnp.bfloat16)
    grad_gate = jnp.einsum(
        "thd,htf->hdf", keys_heads, gate_grad, preferred_element_type=jnp.float32
    )
    grad_down = jnp.einsum(
        "thd,htf->hdf", masked_values, hidden, preferred_element_type=jnp.float32
    )
    grad_up = jnp.einsum("thd,htf->hdf", keys_heads, up_grad, preferred_element_type=jnp.float32)
    partial_value = jnp.stack([grad_gate, grad_down, grad_up])
    head_rates = step_size[None, :, None, None]
    summed = lax.psum(partial_value, "tok")
    directions = orthogonalize(summed)
    updated = renormalize(fast_weights, fast_weights + head_rates * directions).astype(jnp.bfloat16)
    query_heads = queries.reshape(tok_rows, local_heads, head_size)
    read_gate = jnp.einsum(
        "thd,hdf->htf", query_heads, updated[0], preferred_element_type=jnp.float32
    )
    read_up = jnp.einsum(
        "thd,hdf->htf", query_heads, updated[2], preferred_element_type=jnp.float32
    )
    read_hidden = (jax.nn.silu(read_gate) * read_up).astype(jnp.bfloat16)
    read_out = jnp.einsum(
        "htf,hdf->thd", read_hidden, updated[1], preferred_element_type=jnp.float32
    )
    read_out = read_out.astype(jnp.bfloat16).reshape(tok_rows, local_heads * head_size)
    projected = jnp.dot(
        lax.all_gather(read_out, "head", axis=1, tiled=True),
        out_proj,
        preferred_element_type=jnp.float32,
    )
    return jax.nn.silu(projected).astype(jnp.bfloat16)


def solution(mesh):
    in_specs = (
        P("tok", "head"),
        P("tok", "head"),
        P("tok", "head"),
        P(None, "head", None, None),
        P("head"),
        P("tok"),
        P(None, "head"),
    )
    out_specs = P("tok", "head")
    return jax.shard_map(
        on_device, mesh=mesh, in_specs=in_specs, out_specs=out_specs, check_vma=False
    )
```

profile of v0, /device:TPU:0, one launch (start us, length us, event | category | flops | bytes accessed | tf_op | source)
XLA Modules:
  0.0 387.1 jit_solution(8915672703002302425)
XLA Ops:
  6.5 0.0 copy-start
  6.5 6.1 %multiply_reduce_fusion.1 = (f32[3,8,512]{2,1,0:T(8,128)S(1)}, bf16[3,8,128,512]{3,2,1,0:T(8,128)(2,1)S(1)}) fusion(f32[3,8,128,512]{3,2,1,0:T(8,128)} %param.10), kind=kLoop, calls=%fused_computation.3 | loop fusion | flops 4706304 | bytes 9486336 | tf_op jit(solution)/shard_map/reduce_sum | solution.py:44
  12.6 2.9 fusion.37
  15.5 2.7 fusion.38
  18.2 0.0 copy-done.3
  18.9 0.2 copy.67
  19.1 2.1 fusion.39
  21.3 0.4 copy-done.5
  21.6 3.9 %fusion.17 = f32[1,8,128,512]{2,3,1,0:T(8,128)S(1)} fusion(bf16[256,8,128]{0,2,1:T(8,128)(2,1)S(1)} %bitcast.115, f32[8,256,512]{2,1,0:T(8,128)} %fusion.38, f32[8,256,512]{2,1,0:T(8,128)S(1)} %copy-done.5), kind=kOutput, calls=%fused_computation.32 | convolution fusion | flops 274726912 | bytes 11010048 | tf_op jit(solution)/shard_map/thd,htf->hdf/dot_general | solution.py:75
  25.6 0.0 copy-done.6
  25.6 2.2 fusion.18
  27.8 1.9 fusion.16
  29.7 3.2 pad_maximum_fusion
  32.9 0.0 all-reduce.2.cloned.1.call-update
  32.9 0.0 copy-start.7
  32.9 0.0 all-gather.2.cloned.1.call-start
  33.0 6.8 %copy.37 = f32[3,8,128,512]{2,3,1,0:T(8,128)} copy(f32[3,8,128,512]{3,2,1,0:T(8,128)} %param.10) | data formatting | bytes 12582912 | tf_op args[3]
  39.8 0.2 copy.68
  40.0 206.0 %all-reduce.2.cloned.1.call-done = f32[3,8,128,512]{2,3,1,0:T(8,128)} async-done(((f32[3,8,128,512]{2,3,1,0:T(8,128)}), f32[3,8,128,512]{2,3,1,0:T(8,128)}) %all-reduce.2.cloned.1.call-update) | async-done | bytes 6291472 | tf_op jit(solution)/shard_map/psum | solution.py:81
  246.0 3.5 multiply_reduce_fusion.2
  249.5 1.1 copy-done.2
  250.6 10.7 %fusion.2 = f32[3,8,128,128]{3,2,1,0:T(8,128)S(1)} fusion(f32[3,8,128,512]{2,3,1,0:T(8,128)S(1)} %copy-done.2, f32[3,8]{1,0:T(4,128)S(1)} %add_rsqrt_fusion), kind=kOutput, calls=%fused_computation.12 | convolution fusion | flops 2417491968 | bytes 7864416 | tf_op jit(solution)/shard_map/...if,...jf->...ij/dot_general | solution.py:34
  261.3 2.0 fusion.74
  263.4 7.3 %multiply_add_fusion.4 = f32[3,8,128,512]{2,3,1,0:T(8,128)S(1)} fusion(f32[3,8,128,512]{2,3,1,0:T(8,128)S(1)} %copy-done.2, f32[3,8]{1,0:T(4,128)S(1)} %add_rsqrt_fusion, f32[3,8,128,128]{3,2,1,0:T(8,128)S(1)} %fusion.74, f32[3,8,128,128]{3,2,1,0:T(8,128)S(1)} %fusion.2), kind=kOutput, calls=%fused_computation.8 | convolution fusion | flops 2423390208 | bytes 15728736 | tf_op jit(solution)/shard_map/...ij,...jf->...if/dot_general | solution.py:27
  270.7 10.6 %fusion.75 = f32[3,8,128,128]{3,2,1,0:T(8,128)S(1)} fusion(f32[3,8,128,512]{2,3,1,0:T(8,128)S(1)} %multiply_add_fusion.4), kind=kOutput, calls=%fused_computation.98 | convolution fusion | flops 2415919104 | bytes 7864320 | tf_op jit(solution)/shard_map/...if,...jf->...ij/dot_general | solution.py:34
  281.3 1.6 fusion.76
  283.0 7.5 %multiply_add_fusion.3 = f32[3,8,128,512]{2,3,1,0:T(8,128)S(1)} fusion(f32[3,8,128,512]{2,3,1,0:T(8,128)S(1)} %multiply_add_fusion.4, f32[3,8,128,128]{3,2,1,0:T(8,128)S(1)} %fusion.76, f32[3,8,128,128]{3,2,1,0:T(8,128)S(1)} %fusion.75), kind=kOutput, calls=%fused_computation.7 | convolution fusion | flops 2420244480 | bytes 15728640 | tf_op jit(solution)/shard_map/...ij,...jf->...if/dot_general | solution.py:27
  290.5 10.9 %fusion.77 = f32[3,8,128,128]{3,2,1,0:T(8,128)S(1)} fusion(f32[3,8,128,512]{2,3,1,0:T(8,128)S(1)} %multiply_add_fusion.3), kind=kOutput, calls=%fused_computation.100 | convolution fusion | flops 2415919104 | bytes 7864320 | tf_op jit(solution)/shard_map/...if,...jf->...ij/dot_general | solution.py:34
  301.4 1.6 fusion.78
  303.0 7.5 %multiply_add_fusion.2 = f32[3,8,128,512]{2,3,1,0:T(8,128)S(1)} fusion(f32[3,8,128,512]{2,3,1,0:T(8,128)S(1)} %multiply_add_fusion.3, f32[3,8,128,128]{3,2,1,0:T(8,128)S(1)} %fusion.78, f32[3,8,128,128]{3,2,1,0:T(8,128)S(1)} %fusion.77), kind=kOutput, calls=%fused_computation.6 | convolution fusion | flops 2420244480 | bytes 15728640 | tf_op jit(solution)/shard_map/...ij,...jf->...if/dot_general | solution.py:27
  310.5 10.8 %fusion.79 = f32[3,8,128,128]{3,2,1,0:T(8,128)S(1)} fusion(f32[3,8,128,512]{2,3,1,0:T(8,128)S(1)} %multiply_add_fusion.2), kind=kOutput, calls=%fused_computation.102 | convolution fusion | flops 2415919104 | bytes 7864320 | tf_op jit(solution)/shard_map/...if,...jf->...ij/dot_general | solution.py:34
  321.3 1.6 fusion.80
  322.9 0.0 slice-start
  322.9 7.7 %multiply_add_fusion.1 = f32[3,8,128,512]{2,3,1,0:T(8,128)S(1)} fusion(f32[3,8,128,512]{2,3,1,0:T(8,128)S(1)} %multiply_add_fusion.2, f32[3,8,128,128]{3,2,1,0:T(8,128)S(1)} %fusion.80, f32[3,8,128,128]{3,2,1,0:T(8,128)S(1)} %fusion.79), kind=kOutput, calls=%fused_computation.5 | convolution fusion | flops 2420244480 | bytes 15728640 | tf_op jit(solution)/shard_map/...ij,...jf->...if/dot_general | solution.py:27
  330.6 0.0 slice-start.1
  330.6 10.7 %fusion.81 = f32[3,8,128,128]{3,2,1,0:T(8,128)S(1)} fusion(f32[3,8,128,512]{2,3,1,0:T(8,128)S(1)} %multiply_add_fusion.1), kind=kOutput, calls=%fused_computation.104 | convolution fusion | flops 2415919104 | bytes 7864320 | tf_op jit(solution)/shard_map/...if,...jf->...ij/dot_general | solution.py:34
  341.3 0.0 copy-start.9
  341.3 1.7 fusion.82
  343.0 9.4 %multiply_reduce_fusion = (f32[3,8,512]{2,1,0:T(8,128)S(1)}, f32[3,8,128,512]{2,3,1,0:T(8,128)}) fusion(f32[3,8,128,512]{2,3,1,0:T(8,128)S(1)} %bitcast.111, f32[3,8,128,512]{2,3,1,0:T(8,128)S(1)} %multiply_add_fusion.1, f32[3,8,128,128]{3,2,1,0:T(8,128)S(1)} %fusion.82, f32[3,8,128,128]{3,2,1,0:T(8,128)S(1)} %fusion.81, f32[8]{0:T(128)S(1)} %copy-done.9), kind=kOutput, calls=%fused_computation.2 | convolution fusion | flops 2426523648 | bytes 22069280 | tf_op jit(solution)/shard_map/...ij,...jf->...if/dot_general | solution.py:27
  352.4 4.4 %multiply_convert_fusion = bf16[3,8,128,512]{2,3,1,0:T(8,128)(2,1)S(1)} fusion(f32[3,8,128,512]{2,3,1,0:T(8,128)} %get-tuple-element.8, f32[3,8,512]{2,1,0:T(8,128)S(1)} %rsqrt_multiply_fusion), kind=kLoop, calls=%fused_computation.1 | loop fusion | flops 3145728 | bytes 9486336 | tf_op jit(solution)/shard_map/convert_element_type | solution.py:83
  356.9 1.6 copy-done.4
  358.5 2.7 fusion.36
  361.2 5.6 %fusion.35 = bf16[8,128,256]{2,1,0:T(8,128)(2,1)} fusion(f32[8,512,256]{1,2,0:T(8,128)} %fusion.36, bf16[256,8,128]{0,2,1:T(8,128)(2,1)S(1)} %bitcast.113, bf16[3,8,128,512]{2,3,1,0:T(8,128)(2,1)} %copy-done.4), kind=kOutput, calls=%fused_computation.50 | convolution fusion | flops 543424512 | bytes 7340032 | tf_op jit(solution)/shard_map/htf,hdf->thd/dot_general | solution.py:92
  366.8 0.0 all-gather.2.cloned.1.call-update
  366.8 0.0 copy-start.1
  366.8 8.2 %all-gather.2.cloned.1.call-done = bf16[256,2048]{0,1:T(8,128)(2,1)} async-done(((bf16[256,1024]{0,1:T(8,128)(2,1)}), bf16[256,2048]{0,1:T(8,128)(2,1)}) %all-gather.2.cloned.1.call-update) | async-done | bytes 1048592 | tf_op jit(solution)/shard_map/all_gather | solution.py:97
  375.1 4.7 %multiply_convert_fusion.13 = bf16[256,1024]{1,0:T(8,128)(2,1)} fusion(bf16[256,2048]{0,1:T(8,128)(2,1)} %all-gather.2.cloned.1.call-done, bf16[2048,1024]{1,0:T(8,128)(2,1)} %param.13), kind=kOutput, calls=%fused_computation.61 | convolution fusion | flops 1075052544 | bytes 5767168 | tf_op jit(solution)/shard_map/dot_general | solution.py:96
  379.8 0.0 copy-done.1
  (17 shorter events, 0.1 us)
Async XLA Ops:
  6.5 6.1 %copy-start = (bf16[256,1024]{1,0:T(8,128)(2,1)S(1)}, bf16[256,1024]{1,0:T(8,128)(2,1)}, u32[]{:S(2)}) copy-start(bf16[256,1024]{1,0:T(8,128)(2,1)} %param.7) | copy-start | bytes 1572868
  6.5 239.4 %all-reduce.2.cloned.1.call-start = ((), (), s32[]{:S(2)}) async-start(), calls=%async_computation | async-start | bytes 12582912 | tf_op jit(solution)/shard_map/psum | solution.py:81
  12.6 5.6 %copy-start.3 = (bf16[3,8,128,512]{3,2,1,0:T(8,128)(2,1)}, bf16[3,8,128,512]{3,2,1,0:T(8,128)(2,1)S(1)}, u32[]{:S(2)}) copy-start(bf16[3,8,128,512]{3,2,1,0:T(8,128)(2,1)S(1)} %get-tuple-element.6) | copy-start | bytes 9437188
  15.5 3.3 copy-start.8
  19.1 2.5 copy-start.5
  21.6 3.9 %copy-start.6 = (f32[8,256,512]{2,1,0:T(8,128)S(1)}, f32[8,256,512]{2,1,0:T(8,128)}, u32[]{:S(2)}) copy-start(f32[8,256,512]{2,1,0:T(8,128)} %fusion.38) | copy-start | bytes 12582916
  32.9 6.9 %copy-start.7 = (bf16[256,1024]{1,0:T(8,128)(2,1)S(1)}, bf16[256,1024]{1,0:T(8,128)(2,1)}, u32[]{:S(2)}) copy-start(bf16[256,1024]{1,0:T(8,128)(2,1)} %param.9) | copy-start | bytes 1572868
  32.9 342.2 %all-gather.2.cloned.1.call-start = ((), (), s32[]{:S(2)}) async-start(), calls=%async_computation.1 | async-start | bytes 1572864 | tf_op jit(solution)/shard_map/all_gather | solution.py:97
  246.0 4.6 %copy-start.2 = (f32[3,8,128,512]{2,3,1,0:T(8,128)S(1)}, f32[3,8,128,512]{2,3,1,0:T(8,128)}, u32[]{:S(2)}) copy-start(f32[3,8,128,512]{2,3,1,0:T(8,128)} %all-reduce.2.cloned.1.call-done) | copy-start | bytes 18874372
  322.9 20.1 %slice-start = ((s8[6291456]{0:T(1024)(128)(4,1)}), s8[2097152]{0:T(1024)(128)(4,1)S(1)}, s32[]{:S(2)}) async-start(s8[6291456]{0:T(1024)(128)(4,1)} %bitcast.110), calls=%async_computation.2 | async-start | bytes 4194304
  330.6 12.4 %slice-start.1 = ((s8[6291456]{0:T(1024)(128)(4,1)}), s8[4194304]{0:T(1024)(128)(4,1)S(1)}, s32[]{:S(2)}) async-start(s8[6291456]{0:T(1024)(128)(4,1)} %bitcast.110), calls=%async_computation.3 | async-start | bytes 8388608
  341.3 1.7 copy-start.9
  356.8 1.7 copy-start.4
  366.8 13.0 %copy-start.1 = (bf16[256,1024]{1,0:T(8,128)(2,1)S(1)}, bf16[256,1024]{1,0:T(8,128)(2,1)}, u32[]{:S(2)}) copy-start(bf16[256,1024]{1,0:T(8,128)(2,1)} %param.7) | copy-start | bytes 1572868
Sparse Core Ops, SparseCore 0:
  33.0 212.9 all-reduce.1
  366.9 8.0 all-gather.1
where the time goes:
time: 393 us; the launch traced here: 387 us
  waiting for transfers between devices  214 us (54%)
  matrix products  130 us (33%)
  other arithmetic  17.3 us (4%)
  between operations  14.8 us (4%)
  local copies, waits for them, and re-layouts  10.4 us (3%)
    psum x1, waiting for transfers between devices, on_device(): summed = lax.psum(partial_value, 'tok')  206 us
    dot_general x5, matrix products, local_gram(): return jnp.einsum('...if,...jf->...ij', iterate, iterate, precision=highest)  53.7 us
    dot_general x5, matrix products, newton_steps(): jnp.einsum('...ij,...jf->...if', polynomial, iterate, precision=highest)  39.4 us
    unnamed x25, local copies, waits for them, and re-layouts  9.96 us
    dot_general x5, matrix products, newton_steps(): jnp.einsum('...ij,...jk->...ik', gram_matrix, gram_matrix, precision=high...  8.61 us
    all_gather x1, waiting for transfers between devices, on_device(): lax.all_gather(read_out, 'head', axis=1, tiled=True)  8.23 us
  transfers between devices with their start and end apart: 2, of which 2 were waited for; matrix products, arithmetic and copies ran while one was open for 2% of the time, Pallas kernels for 0%

commit v1 on v0

v1 whole, which is shorter than its diff:
```python
import functools

import jax
import jax.numpy as jnp
from jax import lax
from jax.experimental import pallas as pl
from jax.experimental.pallas import tpu as pltpu
from jax.sharding import PartitionSpec as P

ITERS = 5
COEF_A = 3.4445
COEF_B = -4.775
COEF_C = 2.0315
BF16 = jnp.bfloat16
F32 = jnp.float32
NN = (((1,), (0,)), ((), ()))
NT = (((1,), (1,)), ((), ()))
TN = (((0,), (0,)), ((), ()))


def dot(a, b, dims=NN):
    return lax.dot_general(a, b, dims, preferred_element_type=F32)


def halves(x):
    high = x.astype(BF16)
    return high, (x - high.astype(F32)).astype(BF16)


def dot3(a, b, dims=NN):
    (ah, al), (bh, bl) = a, b
    return dot(ah, bh, dims) + (dot(ah, bl, dims) + dot(al, bh, dims))


def sigmoid(x):
    return 0.5 + 0.5 * jnp.tanh(0.5 * x)


def gradient_kernel(chunk, recv_ref, weights_ref, grads_ref):
    sources, _, sub, dh = recv_ref.shape
    ff = weights_ref.shape[-1]
    gate_up = jnp.concatenate([weights_ref[0], weights_ref[2]], axis=1).astype(BF16)
    down = weights_ref[1].astype(BF16)
    grads_ref[...] = jnp.zeros_like(grads_ref)

    def step(i, _):
        rows = pl.ds(i * chunk, chunk)
        keys = recv_ref[rows, 0].reshape(chunk * sub, dh)
        values = recv_ref[rows, 1].reshape(chunk * sub, dh)
        pre = dot(keys, gate_up)
        gate, up = pre[:, :ff], pre[:, ff:]
        back = dot(values, down)
        sig = sigmoid(gate)
        act = gate * sig
        hidden = (act * up).astype(BF16)
        gate_grad = (back * up * (sig + act * (1.0 - sig))).astype(BF16)
        up_grad = (back * act).astype(BF16)
        grads_ref[0] += dot(keys, gate_grad, TN)
        grads_ref[1] += dot(values, hidden, TN)
        grads_ref[2] += dot(keys, up_grad, TN)
        return 0

    lax.fori_loop(0, sources // chunk, step, 0)


def update_kernel(chunk, iters, *refs):
    parts, (weights_ref, rate_ref, query_ref, read_ref, new_ref) = refs[:-5], refs[-5:]
    sources, sub, dh = query_ref.shape
    kinds, _, ff = weights_ref.shape
    rate = rate_ref[0:1, :]
    iterates = []
    for m in range(kinds):
        grad = parts[0][m]
        for part in parts[1:]:
            grad = grad + part[m]
        iterates.append(grad * lax.rsqrt(jnp.sum(grad * grad) + 1e-06))
    for _ in range(iters):
        split = [halves(x) for x in iterates]
        gram = [dot3(s, s, NT) for s in split]
        gram_split = [halves(a) for a in gram]
        square = [dot3(s, s) for s in gram_split]
        poly = [halves(COEF_B * a + COEF_C * b) for a, b in zip(gram, square)]
        iterates = [COEF_A * x + dot3(p, s) for x, p, s in zip(iterates, poly, split)]
    for m in range(kinds):
        old = weights_ref[m]
        new = old + rate * iterates[m]
        old_norm = jnp.sqrt(jnp.sum(old * old, axis=0, keepdims=True) + 1e-06)
        new_norm = jnp.sqrt(jnp.sum(new * new, axis=0, keepdims=True) + 1e-06)
        new_ref[m] = (new * (old_norm / new_norm)).astype(BF16)
    gate_up = jnp.concatenate([new_ref[0], new_ref[2]], axis=1)
    down = new_ref[1]

    def step(i, _):
        rows = pl.ds(i * chunk, chunk)
        pre = dot(query_ref[rows].reshape(chunk * sub, dh), gate_up)
        gate, up = pre[:, :ff], pre[:, ff:]
        hidden = (gate * sigmoid(gate) * up).astype(BF16)
        read = dot(hidden, down, NT).astype(BF16)
        read_ref[rows] = read.reshape(chunk, sub, dh)
        return 0

    lax.fori_loop(0, sources // chunk, step, 0)


def project_kernel(place_ref, *refs):
    reads, (weight_ref, out_ref) = refs[:-2], refs[-2:]
    heads, sub, _ = reads[0].shape
    for s, read in enumerate(reads):
        flat = jnp.concatenate([read[i] for i in range(heads)], axis=1)
        value = dot(flat, weight_ref[...])
        out_ref[pl.ds(pl.multiple_of(place_ref[s] * sub, sub), sub), :] = (
            value * sigmoid(value)
        ).astype(BF16)


def call(kernel, out_shape, args, scalars=0, scratch=(), limit=32):
    specs = [pl.BlockSpec(memory_space=pltpu.SMEM)] * scalars
    specs += [pl.BlockSpec(memory_space=pltpu.VMEM)] * (len(args) - scalars)
    return pl.pallas_call(
        kernel,
        out_shape=out_shape,
        in_specs=specs,
        out_specs=pl.BlockSpec(memory_space=pltpu.VMEM),
        scratch_shapes=list(scratch),
        compiler_params=pltpu.CompilerParams(vmem_limit_bytes=limit * 2**20),
    )(*args)


def on_device(tok_size, head_size, keys, values, queries, fast_weights, step_size, edit_mask, out_proj):
    tokens = keys.shape[0]
    kinds, local_heads, dh, ff = fast_weights.shape
    heads = local_heads * head_size
    sub = tokens // head_size
    column = lax.axis_index("head")
    my_head = lax.axis_index("tok") % heads
    groups = [[g * heads + i for i in range(heads)] for g in range(tok_size // heads)]
    whole = len(groups) == 1

    def send(x, shift):
        return lax.ppermute(x, "head", [(i, (i + shift) % head_size) for i in range(head_size)])

    def shuffle(x):
        if whole:
            return lax.all_to_all(x, "tok", 0, 0, tiled=True)
        return lax.all_to_all(x, "tok", 0, 0, tiled=True, axis_index_groups=groups)

    def by_owner(pieces):
        ordered = []
        for owner in range(head_size):
            value = pieces[0]
            for s in range(1, head_size):
                value = jnp.where((column - owner) % head_size == s, pieces[s], value)
            ordered.append(value)
        return jnp.concatenate(ordered, axis=0)

    def swap(x):
        pieces = []
        for s in range(head_size):
            piece = lax.dynamic_index_in_dim(x, (column + s) % head_size, 0, keepdims=False)
            pieces.append(send(piece, s) if s else piece)
        return by_owner(pieces)

    def by_part(x):
        return x.reshape(head_size, sub, local_heads, dh).transpose(0, 2, 1, 3)

    mask = jnp.repeat(edit_mask, tokens // edit_mask.shape[0]).astype(BF16)
    pairs = jnp.stack([by_part(keys), by_part(values * mask[:, None])], axis=2)
    received = shuffle(swap(pairs))
    asked = shuffle(swap(by_part(queries)))

    slot = my_head % local_heads
    own = lax.dynamic_index_in_dim(fast_weights, slot, 1, keepdims=False).reshape(kinds * dh, ff)
    rate = jnp.broadcast_to(lax.dynamic_index_in_dim(step_size, slot, 0, keepdims=False), (8, ff))
    own = jnp.concatenate([own, rate], axis=0)
    mine = own
    for s in range(1, head_size):
        mine = jnp.where((column - my_head // local_heads) % head_size == s, send(own, s), mine)
    weights = mine[: kinds * dh].reshape(kinds, dh, ff)
    rate = mine[kinds * dh :]

    chunk = 4 if heads % 4 == 0 else 1
    partial = call(
        functools.partial(gradient_kernel, chunk),
        jax.ShapeDtypeStruct((kinds, dh, ff), F32),
        (received, weights),
    )
    if not whole:
        others = [[g * heads + i for g in range(tok_size // heads)] for i in range(heads)]
        partial = lax.psum(partial, "tok", axis_index_groups=others)
    if head_size == 2:
        partials = [partial, send(partial, 1)]
    else:
        partials = [lax.psum(partial, "head")]
    read = call(
        functools.partial(update_kernel, chunk, ITERS),
        jax.ShapeDtypeStruct((heads, sub, dh), BF16),
        (*partials, weights, rate, asked),
        scratch=[pltpu.VMEM((kinds, dh, ff), BF16)],
    )
    reads = shuffle(read)
    pieces = [send(reads, s) if s else reads for s in range(head_size)]
    places = (column - jnp.arange(head_size, dtype=jnp.int32)) % head_size
    return call(
        project_kernel,
        jax.ShapeDtypeStruct((tokens, out_proj.shape[1]), BF16),
        (places, *pieces, out_proj),
        scalars=1,
    )


def solution(mesh):
    sizes = dict(mesh.shape)
    in_specs = (
        P("tok", "head"),
        P("tok", "head"),
        P("tok", "head"),
        P(None, "head", None, None),
        P("head"),
        P("tok"),
        P(None, "head"),
    )
    return jax.shard_map(
        functools.partial(on_device, sizes["tok"], sizes["head"]),
        mesh=mesh,
        in_specs=in_specs,
        out_specs=P("tok", "head"),
        check_vma=False,
    )
```

time: 393 us -> 89.8 us (0.23); the launches traced: 387 us -> 89.4 us
  waiting for transfers between devices: 214 us -> 31.9 us
  matrix products: 130 us -> 0 us
  blocking collectives: 0 us -> 17.6 us
  starting transfers between devices: 0.04 us -> 15.5 us
  Pallas kernels: 0 us -> 14.4 us
  between operations: 14.8 us -> 0.87 us
  other arithmetic: 17.3 us -> 3.96 us
  local copies, waits for them, and re-layouts: 10.4 us -> 5.14 us
    psum x1 -> x0, waiting for transfers between devices: 206 us -> none  [on_device(): summed = lax.psum(partial_value, 'tok')]
    dot_general x24 -> x0, matrix products: 130 us -> none  [the longest x5 53.7 us: local_gram(): return jnp.einsum('...if,...jf->...ij', iterate, iterate, precision=highest)]
    all_to_all x0 -> x2, waiting for transfers between devices: none -> 26.5 us  [shuffle(): return lax.all_to_all(x, 'tok', 0, 0, tiled=True)]
    all_to_all x0 -> x1, blocking collectives: none -> 17.6 us  [shuffle(): return lax.all_to_all(x, 'tok', 0, 0, tiled=True)]
    pallas_call x0 -> x3, Pallas kernels: none -> 14.4 us  [call(): pl.pallas_call(kernel, out_shape=out_shape, in_specs=specs, out_specs=pl....]
    all_to_all x0 -> x2, starting transfers between devices: none -> 14.3 us  [shuffle(): return lax.all_to_all(x, 'tok', 0, 0, tiled=True)]
    reduce_sum x2 -> x0, other arithmetic: 9.57 us -> none  [the longest x1 6.08 us: renormalize(): jnp.sum(previous * previous, axis=-2, keepdims=True) + 1e-06]
    unnamed x25 -> x10, local copies, waits for them, and re-layouts: 9.96 us -> 1.37 us
  transfers between devices with their start and end apart: 2 -> 7, of which waited for: 2 -> 5; matrix products, arithmetic and copies ran while one was open for 2% -> 6% of each run, Pallas kernels for 0% -> 5%
where the time goes in v1:
time: 89.8 us; the launch traced here: 89.4 us
  waiting for transfers between devices  31.9 us (36%)
  blocking collectives  17.6 us (20%)
  starting transfers between devices  15.5 us (17%)
  Pallas kernels  14.4 us (16%)
  local copies, waits for them, and re-layouts  5.14 us (6%)
  other arithmetic  3.96 us (4%)
    all_to_all x2, waiting for transfers between devices, shuffle(): return lax.all_to_all(x, 'tok', 0, 0, tiled=True)  26.5 us
    all_to_all x1, blocking collectives, shuffle(): return lax.all_to_all(x, 'tok', 0, 0, tiled=True)  17.6 us
    pallas_call x3, Pallas kernels, call(): pl.pallas_call(kernel, out_shape=out_shape, in_specs=specs, out_specs=pl....  14.4 us
    all_to_all x2, starting transfers between devices, shuffle(): return lax.all_to_all(x, 'tok', 0, 0, tiled=True)  14.3 us
    ppermute x5, waiting for transfers between devices, send(): lax.ppermute(x, 'head', [(i, (i + shift) % head_size) for i in range(head...  5.35 us
    concatenate x2, other arithmetic, by_owner(): return jnp.concatenate(ordered, axis=0)  1.91 us
  transfers between devices with their start and end apart: 7, of which 5 were waited for; matrix products, arithmetic and copies ran while one was open for 6% of the time, Pallas kernels for 5%

profile of v1, /device:TPU:0, one launch (start us, length us, event | category | flops | bytes accessed | tf_op | source)
XLA Modules:
  0.0 89.4 jit_solution(15698284903951024771)
XLA Ops:
  0.7 1.1 %multiply_bitcast_fusion = bf16[32,8,8,128]{3,1,2,0:T(8,128)(2,1)S(1)} fusion(bf16[256,1024]{1,0:T(8,128)(2,1)} %param.8, bf16[]{:T(256)} %bitcast.2), kind=kLoop, calls=%fused_computation.12 | loop fusion | flops 262144 | bytes 1048578
  1.7 0.0 copy-start.2
  1.8 0.1 copy.17
  1.9 1.1 %copy.16 = bf16[32,8,8,128]{3,2,1,0:T(8,128)(2,1)S(1)} copy(bf16[32,8,8,128]{3,1,2,0:T(8,128)(2,1)} %bitcast.50) | data formatting | bytes 1048576
  3.0 0.2 copy_bitcast_fusion
  3.2 0.0 copy-start.1
  3.3 0.1 fusion.3
  3.3 0.5 collective-permute-start
  3.8 1.5 %collective-permute-done = bf16[8,2,128,128]{3,2,1,0:T(8,128)(2,1)S(1)} collective-permute-done((bf16[8,2,128,128]{3,2,1,0:T(8,128)(2,1)S(1)}, bf16[8,2,128,128]{3,2,1,0:T(8,128)(2,1)S(1)}, u32[]{:S(2)}, u32[]{:S(2)}) %collective-permute-start) | collective-permute-done | bytes 524320 | tf_op jit(solution)/shard_map/ppermute | solution.py:140
  5.4 0.1 broadcast_select_fusion.1
  5.5 1.1 %pad_maximum_fusion = bf16[16,2,128,128]{3,2,1,0:T(8,128)(2,1)} fusion(bf16[8,2,128,128]{3,2,1,0:T(8,128)(2,1)S(1)} %get-tuple-element.6, bf16[8,2,128,128]{3,2,1,0:T(8,128)(2,1)S(1)} %get-tuple-element.5), kind=kLoop, calls=%fused_computation.4 | loop fusion | flops 524288 | bytes 2097152 | tf_op jit(solution)/shard_map/concatenate | solution.py:154
  6.5 8.2 %all-to-all-start = ((bf16[16,2,128,128]{3,2,1,0:T(8,128)(2,1)}), bf16[16,2,128,128]{3,2,1,0:T(8,128)(2,1)S(1)}, u32[]{:S(2)}, u32[]{:S(2)}) async-start(bf16[16,2,128,128]{3,2,1,0:T(8,128)(2,1)} %pad_maximum_fusion), calls=%async_computation | async-start | bytes 2097152 | tf_op jit(solution)/shard_map/all_to_all | solution.py:144
  14.8 0.0 copy-done.2
  14.8 0.6 dynamic_slice.25
  15.5 1.2 %constant_dynamic-slice_fusion.2 = f32[3,1,128,512]{3,2,1,0:T(8,128)S(1)} fusion(f32[3,8,128,512]{3,2,1,0:T(8,128)} %param.10, s32[]{:T(128)S(6)} %select_n.114), kind=kLoop, calls=%fused_computation.25 | loop fusion | bytes 1572868 | tf_op jit(solution)/shard_map/jit(dynamic_index_in_dim)/dynamic_slice | solution.py:172
  16.7 1.6 %concatenate.10 = f32[392,512]{1,0:T(8,128)} pad(f32[384,512]{1,0:T(8,128)S(1)} %bitcast.45, f32[]{:T(128)} %bitcast.8), padding=0_8x0_0 | pad | bytes 1589252 | tf_op jit(solution)/shard_map/concatenate | solution.py:174
  18.3 0.0 collective-permute-start.1
  18.3 0.0 copy-done.1
  18.3 0.1 copy.18
  18.5 0.6 collective-permute-start.3
  19.0 1.9 %collective-permute-done.3 = bf16[8,128,128]{2,1,0:T(8,128)(2,1)S(1)} collective-permute-done((bf16[8,128,128]{2,1,0:T(8,128)(2,1)S(1)}, bf16[8,128,128]{2,1,0:T(8,128)(2,1)S(1)}, u32[]{:S(2)}, u32[]{:S(2)}) %collective-permute-start.3) | collective-permute-done | bytes 262176 | tf_op jit(solution)/shard_map/ppermute | solution.py:140
  21.0 0.8 pad_maximum_fusion.1
  21.8 17.6 %all-to-all-done.recv_ref = bf16[16,2,128,128]{3,2,1,0:T(8,128)(2,1)S(1)} async-done(((bf16[16,2,128,128]{3,2,1,0:T(8,128)(2,1)}), bf16[16,2,128,128]{3,2,1,0:T(8,128)(2,1)S(1)}, u32[]{:S(2)}, u32[]{:S(2)}) %all-to-all-start) | async-done | bytes 1048608 | tf_op jit(solution)/shard_map/all_to_all | solution.py:144
  39.4 6.1 %all-to-all-start.1 = ((bf16[16,128,128]{2,1,0:T(8,128)(2,1)}), bf16[16,128,128]{2,1,0:T(8,128)(2,1)S(1)}, u32[]{:S(2)}, u32[]{:S(2)}) async-start(bf16[16,128,128]{2,1,0:T(8,128)(2,1)} %pad_maximum_fusion.1), calls=%async_computation.1 | async-start | bytes 1048576 | tf_op jit(solution)/shard_map/all_to_all | solution.py:144
  45.5 0.0 collective-permute-done.1
  45.5 0.8 broadcast_select_fusion.2
  46.3 0.1 slice.8
  46.3 4.1 %shard_map.73.refs_0_ = f32[3,128,512]{2,1,0:T(8,128)S(1)} custom-call(bf16[16,2,128,128]{3,2,1,0:T(8,128)(2,1)S(1)} %all-to-all-done.recv_ref, f32[3,128,512]{2,1,0:T(8,128)S(1)} %bitcast.43), custom_call_target="tpu_custom_call" | custom-call | tf_op jit(solution)/shard_map/pallas_call | solution.py:119
  50.5 0.1 collective-permute-start.2
  50.5 9.0 %all-to-all-done.1.refs_4_ = bf16[16,128,128]{2,1,0:T(8,128)(2,1)S(1)} async-done(((bf16[16,128,128]{2,1,0:T(8,128)(2,1)}), bf16[16,128,128]{2,1,0:T(8,128)(2,1)S(1)}, u32[]{:S(2)}, u32[]{:S(2)}) %all-to-all-start.1) | async-done | bytes 524320 | tf_op jit(solution)/shard_map/all_to_all | solution.py:144
  59.5 0.0 copy-start
  59.5 0.0 collective-permute-done.2.refs_1_
  59.5 7.7 %shard_map.74 = bf16[16,128,128]{2,1,0:T(8,128)(2,1)S(1)} custom-call(f32[3,128,512]{2,1,0:T(8,128)S(1)} %shard_map.73.refs_0_, f32[3,128,512]{2,1,0:T(8,128)S(1)} %collective-permute-done.2.refs_1_, f32[3,128,512]{2,1,0:T(8,128)S(1)} %bitcast.44, f32[8,512]{1,0:T(8,128)S(1)} %slice.9.refs_3_, bf16[16,128,128]{2,1,0:T(8,128)(2,1)S(1)} %all-to-all-done.1.refs_4_), custom_call_target="tpu_custom_call" | custom-call | tf_op jit(solution)/shard_map/pallas_call | solution.py:119
  67.2 17.6 %all_to_all.15.refs_0_ = bf16[16,128,128]{2,1,0:T(8,128)(2,1)S(1)} all-to-all(bf16[16,128,128]{2,1,0:T(8,128)(2,1)S(1)} %shard_map.74), channel_id=1, replica_groups=mesh['tok'=16,'head'=2] {'tok'}, dimensions={0} | all-to-all | bytes 1048576 | tf_op jit(solution)/shard_map/all_to_all | solution.py:144
  84.8 0.0 collective-permute-start.4
  84.8 1.9 %collective-permute-done.4.refs_1_ = bf16[16,128,128]{2,1,0:T(8,128)(2,1)S(1)} collective-permute-done((bf16[16,128,128]{2,1,0:T(8,128)(2,1)S(1)}, bf16[16,128,128]{2,1,0:T(8,128)(2,1)S(1)}, u32[]{:S(2)}, u32[]{:S(2)}) %collective-permute-start.4) | collective-permute-done | bytes 524320 | tf_op jit(solution)/shard_map/ppermute | solution.py:140
  86.7 0.0 copy-done
  86.7 2.7 %shard_map.75 = bf16[256,1024]{1,0:T(8,128)(2,1)} custom-call(s32[2]{0:T(128)S(1)} %and_select_fusion.place_ref, bf16[16,128,128]{2,1,0:T(8,128)(2,1)S(1)} %all_to_all.15.refs_0_, bf16[16,128,128]{2,1,0:T(8,128)(2,1)S(1)} %collective-permute-done.4.refs_1_, bf16[2048,1024]{1,0:T(8,128)(2,1)S(1)} %copy-done), custom_call_target="tpu_custom_call" | custom-call | tf_op jit(solution)/shard_map/pallas_call | solution.py:119
  (5 shorter events, 0.1 us)
Async XLA Ops:
  1.7 13.1 %copy-start.2 = (f32[8]{0:T(128)S(1)}, f32[8]{0:T(128)}, u32[]{:S(2)}) copy-start(f32[8]{0:T(128)} %param.11) | copy-start | bytes 100
  3.2 15.0 %copy-start.1 = (bf16[256,1024]{1,0:T(8,128)(2,1)S(1)}, bf16[256,1024]{1,0:T(8,128)(2,1)}, u32[]{:S(2)}) copy-start(bf16[256,1024]{1,0:T(8,128)(2,1)} %param.9) | copy-start | bytes 1572868
  3.3 2.1 %collective-permute-start = (bf16[8,2,128,128]{3,2,1,0:T(8,128)(2,1)S(1)}, bf16[8,2,128,128]{3,2,1,0:T(8,128)(2,1)S(1)}, u32[]{:S(2)}, u32[]{:S(2)}) collective-permute-start(bf16[8,2,128,128]{3,2,1,0:T(8,128)(2,1)S(1)} %fusion.3), channel_id=1, source_target_pairs={{0,1},{1,0},{2,3},{3,2},{4,5},{5,4},{6,7},{7,6},{8,9},{9,8},{10,11... | collective-permute-start | bytes 1572872 | tf_op jit(solution)/shard_map/ppermute | solution.py:140
  6.5 32.9 %all-to-all-start = ((bf16[16,2,128,128]{3,2,1,0:T(8,128)(2,1)}), bf16[16,2,128,128]{3,2,1,0:T(8,128)(2,1)S(1)}, u32[]{:S(2)}, u32[]{:S(2)}) async-start(bf16[16,2,128,128]{3,2,1,0:T(8,128)(2,1)} %pad_maximum_fusion), calls=%async_computation | async-start | bytes 2097152 | tf_op jit(solution)/shard_map/all_to_all | solution.py:144
  18.3 27.2 %collective-permute-start.1 = (f32[392,512]{1,0:T(8,128)}, f32[392,512]{1,0:T(8,128)}, u32[]{:S(2)}, u32[]{:S(2)}) collective-permute-start(f32[392,512]{1,0:T(8,128)} %concatenate.10), channel_id=1, source_target_pairs={{0,1},{1,0},{2,3},{3,2},{4,5},{5,4},{6,7},{7,6},{8,9},{9,8},{10,11... | collective-permute-start | bytes 2408456 | tf_op jit(solution)/shard_map/ppermute | solution.py:140
  18.5 2.5 %collective-permute-start.3 = (bf16[8,128,128]{2,1,0:T(8,128)(2,1)S(1)}, bf16[8,128,128]{2,1,0:T(8,128)(2,1)S(1)}, u32[]{:S(2)}, u32[]{:S(2)}) collective-permute-start(bf16[8,128,128]{2,1,0:T(8,128)(2,1)S(1)} %bitcast.52), channel_id=1, source_target_pairs={{0,1},{1,0},{2,3},{3,2},{4,5},{5,4},{6,7},{7,6},{8,9},{9,8},{10,11... | collective-permute-start | bytes 786440 | tf_op jit(solution)/shard_map/ppermute | solution.py:140
  39.4 20.1 %all-to-all-start.1 = ((bf16[16,128,128]{2,1,0:T(8,128)(2,1)}), bf16[16,128,128]{2,1,0:T(8,128)(2,1)S(1)}, u32[]{:S(2)}, u32[]{:S(2)}) async-start(bf16[16,128,128]{2,1,0:T(8,128)(2,1)} %pad_maximum_fusion.1), calls=%async_computation.1 | async-start | bytes 1048576 | tf_op jit(solution)/shard_map/all_to_all | solution.py:144
  50.5 9.1 %collective-permute-start.2 = (f32[3,128,512]{2,1,0:T(8,128)S(1)}, f32[3,128,512]{2,1,0:T(8,128)S(1)}, u32[]{:S(2)}, u32[]{:S(2)}) collective-permute-start(f32[3,128,512]{2,1,0:T(8,128)S(1)} %shard_map.73.refs_0_), channel_id=1, source_target_pairs={{0,1},{1,0},{2,3},{3,2},{4,5},{5,4},{6,7},{7,6},{8,9},{9,8},{10,11... | collective-permute-start | bytes 2359304 | tf_op jit(solution)/shard_map/ppermute | solution.py:140
  59.5 27.2 %copy-start = (bf16[2048,1024]{1,0:T(8,128)(2,1)S(1)}, bf16[2048,1024]{1,0:T(8,128)(2,1)}, u32[]{:S(2)}) copy-start(bf16[2048,1024]{1,0:T(8,128)(2,1)} %refs_2_.1) | copy-start | bytes 12582916
  84.8 1.9 %collective-permute-start.4 = (bf16[16,128,128]{2,1,0:T(8,128)(2,1)S(1)}, bf16[16,128,128]{2,1,0:T(8,128)(2,1)S(1)}, u32[]{:S(2)}, u32[]{:S(2)}) collective-permute-start(bf16[16,128,128]{2,1,0:T(8,128)(2,1)S(1)} %all_to_all.15.refs_0_), channel_id=1, source_target_pairs={{0,1},{1,0},{2,3},{3,2},{4,5},{5,4},{6,7},{7,6},{8,9},{9,8},{10,11... | collective-permute-start | bytes 1572872 | tf_op jit(solution)/shard_map/ppermute | solution.py:140

commit v2 on v1

v2 whole, which is shorter than its diff:
```python
import functools

import jax
import jax.numpy as jnp
from jax import lax
from jax.experimental import pallas as pl
from jax.experimental.pallas import tpu as pltpu
from jax.sharding import PartitionSpec as P

ITERS = 5
COEF_A = 3.4445
COEF_B = -4.775
COEF_C = 2.0315
BF16 = jnp.bfloat16
F32 = jnp.float32
NN = (((1,), (0,)), ((), ()))
NT = (((1,), (1,)), ((), ()))
TN = (((0,), (0,)), ((), ()))


def dot(a, b, dims=NN):
    return lax.dot_general(a, b, dims, preferred_element_type=F32)


def halves(x):
    high = x.astype(BF16)
    return high, (x - high.astype(F32)).astype(BF16)


def dot3(a, b, dims=NN):
    (ah, al), (bh, bl) = a, b
    return dot(ah, bh, dims) + (dot(ah, bl, dims) + dot(al, bh, dims))


def sigmoid(x):
    return 0.5 + 0.5 * jnp.tanh(0.5 * x)


def gradient_kernel(chunk, recv_ref, weights_ref, grads_ref, low_ref):
    sources, _, sub, dh = recv_ref.shape
    ff = weights_ref.shape[-1]
    gate_up = jnp.concatenate([weights_ref[0], weights_ref[2]], axis=1).astype(BF16)
    down = weights_ref[1].astype(BF16)
    grads_ref[...] = jnp.zeros_like(grads_ref)

    def step(i, _):
        rows = pl.ds(i * chunk, chunk)
        keys = recv_ref[rows, 0].reshape(chunk * sub, dh)
        values = recv_ref[rows, 1].reshape(chunk * sub, dh)
        pre = dot(keys, gate_up)
        gate, up = pre[:, :ff], pre[:, ff:]
        back = dot(values, down)
        sig = sigmoid(gate)
        act = gate * sig
        hidden = (act * up).astype(BF16)
        gate_grad = (back * up * (sig + act * (1.0 - sig))).astype(BF16)
        up_grad = (back * act).astype(BF16)
        grads_ref[0] += dot(keys, gate_grad, TN)
        grads_ref[1] += dot(values, hidden, TN)
        grads_ref[2] += dot(keys, up_grad, TN)
        return 0

    lax.fori_loop(0, sources // chunk, step, 0)
    low_ref[...] = grads_ref[...].astype(BF16)


def update_kernel(chunk, iters, rate_ref, *refs):
    parts, (weights_ref, query_ref, read_ref, new_ref) = refs[:-4], refs[-4:]
    sources, sub, dh = query_ref.shape
    kinds, _, ff = weights_ref.shape
    rate = rate_ref[0]
    iterates = []
    for m in range(kinds):
        grad = parts[0][m]
        for part in parts[1:]:
            grad = grad + part[m].astype(F32)
        iterates.append(grad * lax.rsqrt(jnp.sum(grad * grad) + 1e-06))
    for _ in range(iters):
        split = [halves(x) for x in iterates]
        gram = [dot3(s, s, NT) for s in split]
        gram_split = [halves(a) for a in gram]
        square = [dot3(s, s) for s in gram_split]
        poly = [halves(COEF_B * a + COEF_C * b) for a, b in zip(gram, square)]
        iterates = [COEF_A * x + dot3(p, s) for x, p, s in zip(iterates, poly, split)]
    for m in range(kinds):
        old = weights_ref[m]
        new = old + rate * iterates[m]
        old_norm = jnp.sqrt(jnp.sum(old * old, axis=0, keepdims=True) + 1e-06)
        new_norm = jnp.sqrt(jnp.sum(new * new, axis=0, keepdims=True) + 1e-06)
        new_ref[m] = (new * (old_norm / new_norm)).astype(BF16)
    gate_up = jnp.concatenate([new_ref[0], new_ref[2]], axis=1)
    down = new_ref[1]

    def step(i, _):
        rows = pl.ds(i * chunk, chunk)
        pre = dot(query_ref[rows].reshape(chunk * sub, dh), gate_up)
        gate, up = pre[:, :ff], pre[:, ff:]
        hidden = (gate * sigmoid(gate) * up).astype(BF16)
        read = dot(hidden, down, NT).astype(BF16)
        read_ref[rows] = read.reshape(chunk, sub, dh)
        return 0

    lax.fori_loop(0, sources // chunk, step, 0)


def project_own_kernel(place_ref, read_ref, weight_ref, sum_ref):
    heads = read_ref.shape[0]
    flat = jnp.concatenate([read_ref[i] for i in range(heads)], axis=1)
    depth = flat.shape[1]
    rows = pl.ds(pl.multiple_of(place_ref[0] * depth, depth), depth)
    sum_ref[...] = dot(flat, weight_ref[rows, :])


def project_rest_kernel(place_ref, sum_ref, *refs):
    reads, (weight_ref, out_ref) = refs[:-2], refs[-2:]
    heads = reads[0].shape[0]
    value = sum_ref[...]
    for s, read in enumerate(reads):
        flat = jnp.concatenate([read[i] for i in range(heads)], axis=1)
        depth = flat.shape[1]
        rows = pl.ds(pl.multiple_of(place_ref[s + 1] * depth, depth), depth)
        value = value + dot(flat, weight_ref[rows, :])
    out_ref[...] = (value * sigmoid(value)).astype(BF16)


def call(kernel, out_shape, args, scalars=0, scratch=(), limit=32):
    specs = [pl.BlockSpec(memory_space=pltpu.SMEM)] * scalars
    specs += [pl.BlockSpec(memory_space=pltpu.VMEM)] * (len(args) - scalars)
    return pl.pallas_call(
        kernel,
        out_shape=out_shape,
        in_specs=specs,
        out_specs=jax.tree.map(lambda _: pl.BlockSpec(memory_space=pltpu.VMEM), out_shape),
        scratch_shapes=list(scratch),
        compiler_params=pltpu.CompilerParams(vmem_limit_bytes=limit * 2**20),
    )(*args)


def on_device(tok_size, head_size, keys, values, queries, fast_weights, step_size, edit_mask, out_proj):
    tokens = keys.shape[0]
    kinds, heads, dh, ff = fast_weights.shape
    column = lax.axis_index("head")
    slot = lax.axis_index("tok") % heads
    count = tok_size // heads
    groups = [[g * heads + i for i in range(heads)] for g in range(count)]

    def shuffle(x):
        return lax.all_to_all(x, "tok", 0, 0, tiled=True, axis_index_groups=groups)

    def by_head(x):
        return x.reshape(tokens, heads, dh).transpose(1, 0, 2)

    mask = jnp.repeat(edit_mask, tokens // edit_mask.shape[0]).astype(BF16)
    received = shuffle(jnp.stack([by_head(keys), by_head(values * mask[:, None])], axis=1))
    weights = lax.dynamic_index_in_dim(fast_weights, slot, 1, keepdims=False)
    rate = lax.dynamic_slice_in_dim(step_size, slot, 1)

    chunk = 2 if heads % 2 == 0 else 1
    partial, low = call(
        functools.partial(gradient_kernel, chunk),
        (jax.ShapeDtypeStruct((kinds, dh, ff), F32), jax.ShapeDtypeStruct((kinds, dh, ff), BF16)),
        (received, weights),
    )
    low, packed = lax.optimization_barrier((low, by_head(queries)))
    if count == 1:
        partials = [partial]
    elif count == 2:
        partials = [partial, lax.ppermute(low, "tok", [(i, (i + heads) % tok_size) for i in range(tok_size)])]
    else:
        others = [[g * heads + i for g in range(count)] for i in range(heads)]
        partials = [lax.psum(partial, "tok", axis_index_groups=others)]
    asked = shuffle(packed)
    read = call(
        functools.partial(update_kernel, chunk, ITERS),
        jax.ShapeDtypeStruct((heads, tokens, dh), BF16),
        (rate, *partials, weights, asked),
        scalars=1,
        scratch=[pltpu.VMEM((kinds, dh, ff), BF16)],
    )
    reads = shuffle(read)
    pieces = [
        lax.ppermute(reads, "head", [(i, (i + s) % head_size) for i in range(head_size)])
        for s in range(1, head_size)
    ]
    places = (column - jnp.arange(head_size, dtype=jnp.int32)) % head_size
    columns = out_proj.shape[1]
    own = call(
        project_own_kernel,
        jax.ShapeDtypeStruct((tokens, columns), F32),
        (places, reads, out_proj),
        scalars=1,
    )
    return call(
        project_rest_kernel,
        jax.ShapeDtypeStruct((tokens, columns), BF16),
        (places, own, *pieces, out_proj),
        scalars=1,
    )


def solution(mesh):
    sizes = dict(mesh.shape)
    in_specs = (
        P("tok", "head"),
        P("tok", "head"),
        P("tok", "head"),
        P(None, "head", None, None),
        P("head"),
        P("tok"),
        P(None, "head"),
    )
    return jax.shard_map(
        functools.partial(on_device, sizes["tok"], sizes["head"]),
        mesh=mesh,
        in_specs=in_specs,
        out_specs=P("tok", "head"),
        check_vma=False,
    )
```

time: 89.8 us -> 80.6 us (0.90)
  blocking collectives: 17.6 us -> 11.9 us
  local copies, waits for them, and re-layouts: 5.14 us -> 9.2 us
  starting transfers between devices: 15.5 us -> 12.3 us
  waiting for transfers between devices: 31.9 us -> 28.9 us
  other arithmetic: 3.96 us -> 1.12 us
  Pallas kernels: 14.4 us -> 15.9 us
    all_to_all x2, waiting for transfers between devices: 26.5 us -> 12.3 us  [shuffle(): return lax.all_to_all(x, 'tok', 0, 0, tiled=True, axis_index_groups=groups)]
    ppermute x5 -> x2, waiting for transfers between devices: 5.35 us -> 16.6 us  [the longest x1 16.6 us: on_device(): lax.ppermute(low, 'tok', [(i, (i + heads) % tok_size) for i in range(tok_...]
    all_to_all x1, blocking collectives: 17.6 us -> 11.9 us  [shuffle(): return lax.all_to_all(x, 'tok', 0, 0, tiled=True, axis_index_groups=groups)]
    all_to_all x2, starting transfers between devices: 14.3 us -> 9.69 us  [shuffle(): return lax.all_to_all(x, 'tok', 0, 0, tiled=True, axis_index_groups=groups)]
    unnamed x10 -> x11, local copies, waits for them, and re-layouts: 1.37 us -> 5.87 us
    concatenate x2 -> x0, other arithmetic: 1.91 us -> none  [by_owner(): return jnp.concatenate(ordered, axis=0)]
    concatenate x1 -> x0, local copies, waits for them, and re-layouts: 1.6 us -> none  [on_device(): own = jnp.concatenate([own, rate], axis=0)]
    reshape x0 -> x3, local copies, waits for them, and re-layouts: none -> 1.55 us  [by_head(): return x.reshape(tokens, heads, dh).transpose(1, 0, 2)]
  transfers between devices with their start and end apart: 7 -> 4, of which waited for: 5 -> 2; matrix products, arithmetic and copies ran while one was open for 6% -> 4% of each run, Pallas kernels for 5% -> 2%
where the time goes in v2:
time: 80.6 us; the launch traced here: 80.1 us
  waiting for transfers between devices  28.9 us (36%)
  Pallas kernels  15.9 us (20%)
  starting transfers between devices  12.3 us (15%)
  blocking collectives  11.9 us (15%)
  local copies, waits for them, and re-layouts  9.2 us (11%)
  other arithmetic  1.12 us (1%)
    ppermute x1, waiting for transfers between devices, on_device(): lax.ppermute(low, 'tok', [(i, (i + heads) % tok_size) for i in range(tok_...  16.6 us
    pallas_call x4, Pallas kernels, call(): pl.pallas_call(kernel, out_shape=out_shape, in_specs=specs, out_specs=jax...  15.9 us
    all_to_all x2, waiting for transfers between devices, shuffle(): return lax.all_to_all(x, 'tok', 0, 0, tiled=True, axis_index_groups=groups)  12.3 us
    all_to_all x1, blocking collectives, shuffle(): return lax.all_to_all(x, 'tok', 0, 0, tiled=True, axis_index_groups=groups)  11.9 us
    all_to_all x2, starting transfers between devices, shuffle(): return lax.all_to_all(x, 'tok', 0, 0, tiled=True, axis_index_groups=groups)  9.69 us
    unnamed x11, local copies, waits for them, and re-layouts  5.87 us
    ppermute x1, starting transfers between devices, on_device(): lax.ppermute(low, 'tok', [(i, (i + heads) % tok_size) for i in range(tok_...  2.66 us
  transfers between devices with their start and end apart: 4, of which 2 were waited for; matrix products, arithmetic and copies ran while one was open for 4% of the time, Pallas kernels for 2%

profile of v2, /device:TPU:0, one launch (start us, length us, event | category | flops | bytes accessed | tf_op | source)
XLA Modules:
  0.0 80.1 jit_solution(2454167556975433572)
XLA Ops:
  0.0 0.0 copy-start.2
  0.0 1.3 %copy.10 = bf16[256,1024]{0,1:T(8,128)(2,1)S(1)} copy(bf16[256,1024]{1,0:T(8,128)(2,1)} %param.8) | data formatting | bytes 1048576 | tf_op args[1]
  2.0 0.3 copy.11
  2.3 0.0 copy-start.3
  2.3 1.3 %copy.8 = bf16[256,1024]{0,1:T(8,128)(2,1)S(1)} copy(bf16[256,1024]{1,0:T(8,128)(2,1)} %param.7) | data formatting | bytes 1048576 | tf_op args[0]
  3.6 0.3 copy.9
  3.8 1.1 %pad_maximum_fusion = bf16[8,2,256,128]{3,2,1,0:T(8,128)(2,1)} fusion(bf16[8,1,256,128]{3,2,1,0:T(8,128)(2,1)S(1)} %bitcast.16, bf16[8,1,256,128]{3,2,1,0:T(8,128)(2,1)S(1)} %bitcast.17), kind=kLoop, calls=%fused_computation | loop fusion | flops 524288 | bytes 2097152 | tf_op jit(solution)/shard_map/stack | solution.py:154
  4.9 6.2 %all-to-all-start = ((bf16[8,2,256,128]{3,2,1,0:T(8,128)(2,1)}), bf16[8,2,256,128]{3,2,1,0:T(8,128)(2,1)S(1)}, u32[]{:S(2)}, u32[]{:S(2)}) async-start(bf16[8,2,256,128]{3,2,1,0:T(8,128)(2,1)} %pad_maximum_fusion), calls=%async_computation | async-start | bytes 2097152 | tf_op jit(solution)/shard_map/all_to_all | solution.py:148
  11.1 0.0 copy-done.2
  11.1 0.2 copy.12
  11.3 1.0 %copy.13 = bf16[256,8,128]{2,0,1:T(8,128)(2,1)} copy(bf16[256,8,128]{0,2,1:T(8,128)(2,1)S(1)} %bitcast.15) | data formatting | bytes 1048576 | tf_op jit(solution)/shard_map/reshape | solution.py:151
  12.3 1.2 %dynamic-slice_bitcast_fusion.weights_ref.refs_2_ = f32[3,128,512]{2,1,0:T(8,128)S(1)} fusion(f32[3,8,128,512]{3,2,1,0:T(8,128)} %param.10, s32[]{:T(128)S(6)} %select_n.20), kind=kLoop, calls=%fused_computation.1 | loop fusion | bytes 1572868 | tf_op jit(solution)/shard_map/jit(dynamic_index_in_dim)/squeeze | solution.py:155
  13.5 12.3 %all-to-all-done.recv_ref = bf16[8,2,256,128]{3,2,1,0:T(8,128)(2,1)S(1)} async-done(((bf16[8,2,256,128]{3,2,1,0:T(8,128)(2,1)}), bf16[8,2,256,128]{3,2,1,0:T(8,128)(2,1)S(1)}, u32[]{:S(2)}, u32[]{:S(2)}) %all-to-all-start) | async-done | bytes 1048608 | tf_op jit(solution)/shard_map/all_to_all | solution.py:148
  25.8 4.1 %shard_map.73 = (f32[3,128,512]{2,1,0:T(8,128)S(1)}, bf16[3,128,512]{2,1,0:T(8,128)(2,1)S(1)}) custom-call(bf16[8,2,256,128]{3,2,1,0:T(8,128)(2,1)S(1)} %all-to-all-done.recv_ref, f32[3,128,512]{2,1,0:T(8,128)S(1)} %dynamic-slice_bitcast_fusion.weights_ref.refs_2_), custom_call_target="tpu_custom_call" | custom-call | tf_op jit(solution)/shard_map/pallas_call | solution.py:129
  29.9 3.5 %all-to-all-start.1 = ((bf16[8,256,128]{2,1,0:T(8,128)(2,1)}), bf16[8,256,128]{2,1,0:T(8,128)(2,1)S(1)}, u32[]{:S(2)}, u32[]{:S(2)}) async-start(bf16[8,256,128]{2,1,0:T(8,128)(2,1)} %bitcast.9), calls=%async_computation.1 | async-start | bytes 1048576 | tf_op jit(solution)/shard_map/all_to_all | solution.py:148
  33.4 2.7 %collective-permute-start = (bf16[3,128,512]{2,1,0:T(8,128)(2,1)S(1)}, bf16[3,128,512]{2,1,0:T(8,128)(2,1)S(1)}, u32[]{:S(2)}, u32[]{:S(2)}) collective-permute-start(bf16[3,128,512]{2,1,0:T(8,128)(2,1)S(1)} %get-tuple-element.11), channel_id=1, source_target_pairs={{0,16},{2,18},{4,20},{6,22},{8,24},{10,26},{12,28},{14,30},{16,0},... | collective-permute-start | bytes 1179656 | tf_op jit(solution)/shard_map/ppermute | solution.py:168
  36.1 0.0 copy-done.3
  36.1 0.6 dynamic_slice.7.rate_ref
  36.7 16.6 %collective-permute-done.refs_1_ = bf16[3,128,512]{2,1,0:T(8,128)(2,1)S(1)} collective-permute-done((bf16[3,128,512]{2,1,0:T(8,128)(2,1)S(1)}, bf16[3,128,512]{2,1,0:T(8,128)(2,1)S(1)}, u32[]{:S(2)}, u32[]{:S(2)}) %collective-permute-start) | collective-permute-done | bytes 393248 | tf_op jit(solution)/shard_map/ppermute | solution.py:168
  53.3 0.0 all-to-all-done.1.refs_3_
  53.3 8.3 %shard_map.74 = bf16[8,256,128]{2,1,0:T(8,128)(2,1)S(1)} custom-call(f32[1]{0:T(128)} %dynamic_slice.7.rate_ref, f32[3,128,512]{2,1,0:T(8,128)S(1)} %get-tuple-element.9.refs_0_, bf16[3,128,512]{2,1,0:T(8,128)(2,1)S(1)} %collective-permute-done.refs_1_, f32[3,128,512]{2,1,0:T(8,128)S(1)} %dynamic-slice_bitcast_fusion.weights_ref.refs_2_, ...), custom_call_target="tpu_custom_call" | custom-call | tf_op jit(solution)/shard_map/pallas_call | solution.py:129
  61.6 11.9 %all_to_all.15.read_ref = bf16[8,256,128]{2,1,0:T(8,128)(2,1)S(1)} all-to-all(bf16[8,256,128]{2,1,0:T(8,128)(2,1)S(1)} %shard_map.74), channel_id=1, replica_groups={{0,2,4,6,8,10,12,14},{16,18,20,22,24,26,28,30},{1,3,5,7,9,11,13,15},{17..., dimensions={0} | all-to-all | bytes 1048576 | tf_op jit(solution)/shard_map/all_to_all | solution.py:148
  73.5 0.0 collective-permute-start.1
  73.5 0.0 copy-start
  73.5 2.2 %copy-done = bf16[2048,1024]{1,0:T(8,128)(2,1)S(1)} copy-done((bf16[2048,1024]{1,0:T(8,128)(2,1)S(1)}, bf16[2048,1024]{1,0:T(8,128)(2,1)}, u32[]{:S(2)}) %copy-start) | copy-done | bytes 4194328
  75.7 0.0 copy-start.1
  75.7 1.3 %shard_map.75.sum_ref = f32[256,1024]{1,0:T(8,128)S(1)} custom-call(s32[2]{0:T(128)S(1)} %and_select_fusion.place_ref, bf16[8,256,128]{2,1,0:T(8,128)(2,1)S(1)} %all_to_all.15.read_ref, bf16[2048,1024]{1,0:T(8,128)(2,1)S(1)} %copy-done), custom_call_target="tpu_custom_call" | custom-call | tf_op jit(solution)/shard_map/pallas_call | solution.py:129
  77.0 0.0 collective-permute-done.1.refs_0_
  77.0 0.9 %copy-done.1 = bf16[2048,1024]{1,0:T(8,128)(2,1)S(1)} copy-done((bf16[2048,1024]{1,0:T(8,128)(2,1)S(1)}, bf16[2048,1024]{1,0:T(8,128)(2,1)}, u32[]{:S(2)}) %copy-start.1) | copy-done | bytes 4194328
  77.9 2.2 %shard_map.76 = bf16[256,1024]{1,0:T(8,128)(2,1)} custom-call(s32[2]{0:T(128)S(1)} %and_select_fusion.place_ref, f32[256,1024]{1,0:T(8,128)S(1)} %shard_map.75.sum_ref, bf16[8,256,128]{2,1,0:T(8,128)(2,1)S(1)} %collective-permute-done.1.refs_0_, bf16[2048,1024]{1,0:T(8,128)(2,1)S(1)} %copy-done.1), custom_call_target="tpu_custom_call" | custom-call | tf_op jit(solution)/shard_map/pallas_call | solution.py:129
  (2 shorter events, 0.0 us)
Async XLA Ops:
  0.0 11.1 %copy-start.2 = (bf16[256,1024]{1,0:T(8,128)(2,1)S(1)}, bf16[256,1024]{1,0:T(8,128)(2,1)}, u32[]{:S(2)}) copy-start(bf16[256,1024]{1,0:T(8,128)(2,1)} %param.9) | copy-start | bytes 1572868
  2.3 33.8 %copy-start.3 = (f32[8]{0:T(128)S(1)}, f32[8]{0:T(128)}, u32[]{:S(2)}) copy-start(f32[8]{0:T(128)} %param.11) | copy-start | bytes 100
  4.9 20.9 %all-to-all-start = ((bf16[8,2,256,128]{3,2,1,0:T(8,128)(2,1)}), bf16[8,2,256,128]{3,2,1,0:T(8,128)(2,1)S(1)}, u32[]{:S(2)}, u32[]{:S(2)}) async-start(bf16[8,2,256,128]{3,2,1,0:T(8,128)(2,1)} %pad_maximum_fusion), calls=%async_computation | async-start | bytes 2097152 | tf_op jit(solution)/shard_map/all_to_all | solution.py:148
  29.9 23.4 %all-to-all-start.1 = ((bf16[8,256,128]{2,1,0:T(8,128)(2,1)}), bf16[8,256,128]{2,1,0:T(8,128)(2,1)S(1)}, u32[]{:S(2)}, u32[]{:S(2)}) async-start(bf16[8,256,128]{2,1,0:T(8,128)(2,1)} %bitcast.9), calls=%async_computation.1 | async-start | bytes 1048576 | tf_op jit(solution)/shard_map/all_to_all | solution.py:148
  33.4 19.9 %collective-permute-start = (bf16[3,128,512]{2,1,0:T(8,128)(2,1)S(1)}, bf16[3,128,512]{2,1,0:T(8,128)(2,1)S(1)}, u32[]{:S(2)}, u32[]{:S(2)}) collective-permute-start(bf16[3,128,512]{2,1,0:T(8,128)(2,1)S(1)} %get-tuple-element.11), channel_id=1, source_target_pairs={{0,16},{2,18},{4,20},{6,22},{8,24},{10,26},{12,28},{14,30},{16,0},... | collective-permute-start | bytes 1179656 | tf_op jit(solution)/shard_map/ppermute | solution.py:168
  73.5 3.5 %collective-permute-start.1 = (bf16[8,256,128]{2,1,0:T(8,128)(2,1)S(1)}, bf16[8,256,128]{2,1,0:T(8,128)(2,1)S(1)}, u32[]{:S(2)}, u32[]{:S(2)}) collective-permute-start(bf16[8,256,128]{2,1,0:T(8,128)(2,1)S(1)} %all_to_all.15.read_ref), channel_id=1, source_target_pairs={{0,1},{1,0},{2,3},{3,2},{4,5},{5,4},{6,7},{7,6},{8,9},{9,8},{10,11... | collective-permute-start | bytes 1572872 | tf_op jit(solution)/shard_map/ppermute | solution.py:182
  73.5 2.2 %copy-start = (bf16[2048,1024]{1,0:T(8,128)(2,1)S(1)}, bf16[2048,1024]{1,0:T(8,128)(2,1)}, u32[]{:S(2)}) copy-start(bf16[2048,1024]{1,0:T(8,128)(2,1)} %refs_1_.1) | copy-start | bytes 12582916
  75.7 2.2 %copy-start.1 = (bf16[2048,1024]{1,0:T(8,128)(2,1)S(1)}, bf16[2048,1024]{1,0:T(8,128)(2,1)}, u32[]{:S(2)}) copy-start(bf16[2048,1024]{1,0:T(8,128)(2,1)} %refs_1_.1) | copy-start | bytes 12582916

commit v3 on v2

v3 whole, which is shorter than its diff:
```python
import functools

import jax
import jax.numpy as jnp
from jax import lax
from jax.experimental import pallas as pl
from jax.experimental.pallas import tpu as pltpu
from jax.sharding import PartitionSpec as P

ITERS = 5
COEF_A = 3.4445
COEF_B = -4.775
COEF_C = 2.0315
BF16 = jnp.bfloat16
F32 = jnp.float32
LANES = 128
KINDS = 3
NN = (((1,), (0,)), ((), ()))
NT = (((1,), (1,)), ((), ()))
TN = (((0,), (0,)), ((), ()))


def dot(a, b, dims=NN):
    return lax.dot_general(a, b, dims, preferred_element_type=F32)


def halves(x):
    high = x.astype(BF16)
    return high, (x - high.astype(F32)).astype(BF16)


def sigmoid(x):
    return 0.5 + 0.5 * jnp.tanh(0.5 * x)


def pack_kernel(mask_ref, keys_ref, values_ref, pairs_ref, kept_ref, mask_kept, in_sem, out_sem, mask_sem):
    heads, _, tokens, dh = pairs_ref.shape
    blocks = mask_ref.shape[1]
    length = tokens // blocks
    sources = (keys_ref, values_ref)
    mask_copy = pltpu.make_async_copy(mask_ref, mask_kept, mask_sem)
    mask_copy.start()
    loads, stores = [], []
    for i in range(heads):
        for p in range(2):
            loads.append(
                pltpu.make_async_copy(
                    sources[p].at[:, pl.ds(i * dh, dh)], kept_ref.at[i, p], in_sem.at[i, p]
                )
            )
            stores.append(
                pltpu.make_async_copy(kept_ref.at[i, p], pairs_ref.at[i, p], out_sem.at[i, p])
            )
    for load in loads:
        load.start()
    mask_copy.wait()
    for i in range(heads):
        for p in range(2):
            loads[2 * i + p].wait()
            if p == 1:
                for b in range(blocks):
                    rows = pl.ds(b * length, length)
                    kept = kept_ref[i, 1, rows].astype(F32) * mask_kept[:, b : b + 1].astype(F32)
                    kept_ref[i, 1, rows] = kept.astype(BF16)
            stores[2 * i + p].start()
    for store in stores:
        store.wait()


def gradient_kernel(chunk, start, recv_ref, weights_ref, grads_ref, coded_ref):
    sources, _, sub, dh = recv_ref.shape
    ff = grads_ref.shape[-1]
    units = pl.ds(start, ff)
    gate_up = jnp.concatenate([weights_ref[0, :, units], weights_ref[2, :, units]], axis=1).astype(BF16)
    down = weights_ref[1, :, units].astype(BF16)
    for i in range(0, sources, chunk):
        rows = pl.ds(i, chunk)
        keys = recv_ref[rows, 0].reshape(chunk * sub, dh)
        values = recv_ref[rows, 1].reshape(chunk * sub, dh)
        pre = dot(keys, gate_up)
        gate, up = pre[:, :ff], pre[:, ff:]
        back = dot(values, down)
        sig = sigmoid(gate)
        act = gate * sig
        hidden = (act * up).astype(BF16)
        gate_grad = (back * up * (sig + act * (1.0 - sig))).astype(BF16)
        up_grad = (back * act).astype(BF16)
        sums = dot(keys.T, jnp.concatenate([gate_grad, up_grad], axis=1))
        sums = (sums[:, :ff], dot(values.T, hidden), sums[:, ff:])
        for m, value in enumerate(sums):
            grads_ref[m] = value if i == 0 else grads_ref[m] + value
    encode(grads_ref, coded_ref)


def encode(grads_ref, coded_ref):
    kinds, dh, ff = grads_ref.shape
    powers = []
    for m in range(kinds):
        for c in range(ff // LANES):
            block = grads_ref[m, :, c * LANES : (c + 1) * LANES]
            top = jnp.max(jnp.abs(block), axis=0, keepdims=True)
            power = jnp.floor(jnp.log2(jnp.maximum(top, 1e-30))) - 14.0
            code = jnp.clip(jnp.round(block * jnp.exp2(-power)), -32767.0, 32767.0)
            coded_ref[pl.ds(len(powers) * dh, dh)] = code.astype(jnp.int32).astype(jnp.int16)
            powers.append(power)
    rest = coded_ref.shape[0] - len(powers) * dh
    powers += [jnp.zeros_like(powers[0])] * (rest - len(powers))
    power = jnp.concatenate(powers, axis=0)
    coded_ref[pl.ds(coded_ref.shape[0] - rest, rest)] = power.astype(jnp.int32).astype(jnp.int16)


def decode(coded_ref, m, dh, ff):
    width = ff // LANES
    rest = code_rows(KINDS * width)
    power = coded_ref[pl.ds(coded_ref.shape[0] - rest, rest)].astype(jnp.int32).astype(F32)
    blocks = []
    for c in range(width):
        i = m * width + c
        code = coded_ref[pl.ds(i * dh, dh)].astype(jnp.int32).astype(F32)
        blocks.append(code * jnp.exp2(power[i : i + 1]))
    return jnp.concatenate(blocks, axis=1)


def code_rows(columns):
    return -(-columns // 16) * 16


def product(a, b):
    (ah, al), (bh, bl) = a, b
    return dot(jnp.concatenate([ah, al], axis=1), jnp.concatenate([bh, bh], axis=0)) + dot(ah, bl)


def newton_schulz(iterates, iters):
    for _ in range(iters):
        split = [halves(x) for x in iterates]
        gram = []
        for high, low in split:
            both = dot(high, jnp.concatenate([high, low], axis=0), NT)
            size = high.shape[0]
            cross = both[:, size:]
            gram.append(both[:, :size] + (cross + cross.T))
        gram_split = [halves(a) for a in gram]
        square = []
        for high, low in gram_split:
            wide = jnp.concatenate([high, low], axis=1)
            under = jnp.concatenate([high, jnp.zeros_like(high)], axis=1)
            both = dot(wide, jnp.concatenate([wide, under], axis=0))
            size = high.shape[0]
            square.append(both[:, :size] + both[:, size:])
        poly = [halves(COEF_B * a + COEF_C * b) for a, b in zip(gram, square)]
        iterates = [COEF_A * x + product(p, s) for x, p, s in zip(iterates, poly, split)]
    return iterates


def update_kernel(iters, coded, slot_ref, rate_ref, *refs):
    weights_ref, new_ref = refs[-2:]
    kinds, dh, ff = weights_ref.shape
    rate = rate_ref[slot_ref[0]]
    partials, others = refs[:-2], ()
    if coded:
        partials, others = refs[: len(refs) // 2 - 1], refs[len(refs) // 2 - 1 : -2]
    iterates = []
    for m in range(kinds):
        blocks = [partial[m] for partial in partials]
        if coded:
            blocks = [
                block + decode(other, m, dh, block.shape[-1])
                for block, other in zip(blocks, others)
            ]
        grad = jnp.concatenate(blocks, axis=1)
        iterates.append(grad * lax.rsqrt(jnp.sum(grad * grad) + 1e-06))
    iterates = newton_schulz(iterates, iters)
    for m in range(kinds):
        old = weights_ref[m]
        new = old + rate * iterates[m]
        old_norm = jnp.sqrt(jnp.sum(old * old, axis=0, keepdims=True) + 1e-06)
        new_norm = jnp.sqrt(jnp.sum(new * new, axis=0, keepdims=True) + 1e-06)
        new_ref[m] = (new * (old_norm / new_norm)).astype(BF16)


def read_kernel(chunk, new_ref, query_ref, read_ref):
    sources, sub, dh = query_ref.shape
    ff = new_ref.shape[-1]
    gate_up = jnp.concatenate([new_ref[0], new_ref[2]], axis=1)
    down = new_ref[1]

    def step(i, _):
        rows = pl.ds(i * chunk, chunk)
        pre = dot(query_ref[rows].reshape(chunk * sub, dh), gate_up)
        gate, up = pre[:, :ff], pre[:, ff:]
        hidden = (gate * sigmoid(gate) * up).astype(BF16)
        read = dot(hidden, down, NT).astype(BF16)
        read_ref[rows] = read.reshape(chunk, sub, dh)
        return 0

    lax.fori_loop(0, sources // chunk, step, 0)


def flat_heads(read_ref):
    return jnp.concatenate([read_ref[i] for i in range(read_ref.shape[0])], axis=1)


def project_own_kernel(column_ref, read_ref, weight_ref, sum_ref, *refs):
    rest_refs, (own_ref, sems) = refs[:-2], refs[-2:]
    depth, columns = own_ref.shape
    size = weight_ref.shape[0] // depth
    copies = []
    for s, target in enumerate((own_ref, *rest_refs)):
        rows = pl.ds(pl.multiple_of(lax.rem(column_ref[0] + size - s, size) * depth, depth), depth)
        copies.append(pltpu.make_async_copy(weight_ref.at[rows], target, sems.at[s]))
        copies[-1].start()
    copies[0].wait()
    sum_ref[...] = dot(flat_heads(read_ref), own_ref[...])
    for copy in copies[1:]:
        copy.wait()


def project_rest_kernel(sum_ref, *refs):
    reads, weights, out_ref = refs[: len(refs) // 2], refs[len(refs) // 2 : -1], refs[-1]
    value = sum_ref[...]
    for read, weight in zip(reads, weights):
        value = value + dot(flat_heads(read), weight[...])
    out_ref[...] = (value * sigmoid(value)).astype(BF16)


def call(kernel, out_shape, args, scalars=0, flops=None, limit=12, hbm=(), scratch=()):
    specs = [pl.BlockSpec(memory_space=pltpu.SMEM)] * scalars
    specs += [
        pl.BlockSpec(memory_space=pl.ANY if i in hbm else pltpu.VMEM)
        for i in range(scalars, len(args))
    ]
    cost = None
    if flops is not None:
        cost = pl.CostEstimate(flops=flops, bytes_accessed=2**20, transcendentals=0)
    return pl.pallas_call(
        kernel,
        out_shape=out_shape,
        in_specs=specs,
        out_specs=jax.tree.map(
            lambda _: pl.BlockSpec(memory_space=pl.ANY if -1 in hbm else pltpu.VMEM), out_shape
        ),
        scratch_shapes=list(scratch),
        compiler_params=pltpu.CompilerParams(vmem_limit_bytes=limit * 2**20),
        cost_estimate=cost,
    )(*args)


def on_device(tok_size, head_size, keys, values, queries, fast_weights, step_size, edit_mask, out_proj):
    tokens = keys.shape[0]
    kinds, heads, dh, ff = fast_weights.shape
    column = lax.axis_index("head")
    slot = lax.axis_index("tok") % heads
    count = tok_size // heads
    groups = [[g * heads + i for i in range(heads)] for g in range(count)]
    struct = jax.ShapeDtypeStruct

    def shuffle(x):
        return lax.all_to_all(x, "tok", 0, 0, tiled=True, axis_index_groups=groups)

    pairs = call(
        pack_kernel,
        struct((heads, 2, tokens, dh), BF16),
        (edit_mask[None], keys, values),
        hbm=(-1, 0, 1, 2),
        limit=60,
        scratch=[
            pltpu.VMEM((heads, 2, tokens, dh), BF16),
            pltpu.VMEM((1, *edit_mask.shape), edit_mask.dtype),
            pltpu.SemaphoreType.DMA((heads, 2)),
            pltpu.SemaphoreType.DMA((heads, 2)),
            pltpu.SemaphoreType.DMA,
        ],
    )
    received = shuffle(pairs)
    weights = lax.dynamic_index_in_dim(fast_weights, slot, 1, keepdims=False)
    chunk = max(c for c in (1, 2, 4) if heads % c == 0)
    split = 2 if ff % (2 * LANES) == 0 else 1
    width = ff // split
    partials, coded = [], []
    for start in range(0, ff, width):
        rows = kinds * dh * width // LANES + code_rows(kinds * width // LANES)
        partial, code = call(
            functools.partial(gradient_kernel, max(1, chunk // 2), start),
            (struct((kinds, dh, width), F32), struct((rows, LANES), jnp.int16)),
            (received, weights),
            flops=2**32,
            limit=16,
        )
        partials.append(partial)
        code, received = lax.optimization_barrier((code, received))
        coded.append(code)

    packed = queries.reshape(tokens, heads, dh).transpose(1, 0, 2)
    coded[-1], packed = lax.optimization_barrier((coded[-1], packed))
    if count == 2:
        turn = [(i, (i + heads) % tok_size) for i in range(tok_size)]
        parts = (*partials, *[lax.ppermute(code, "tok", turn) for code in coded])
    else:
        others = [[g * heads + i for g in range(count)] for i in range(heads)]
        parts = lax.psum(tuple(partials), "tok", axis_index_groups=others)
    asked = shuffle(packed)
    new = call(
        functools.partial(update_kernel, ITERS, count == 2),
        struct((kinds, dh, ff), BF16),
        (slot.reshape(1), step_size, *parts, weights),
        scalars=2,
        flops=2**33,
    )
    read = call(
        functools.partial(read_kernel, chunk), struct((heads, tokens, dh), BF16), (new, asked), limit=16
    )

    reads = shuffle(read)
    pieces = [
        lax.ppermute(reads, "head", [(i, (i + s) % head_size) for i in range(head_size)])
        for s in range(1, head_size)
    ]
    columns = out_proj.shape[1]
    depth = heads * dh
    own, *rest = call(
        project_own_kernel,
        (
            struct((tokens, columns), F32),
            *[struct((depth, columns), BF16) for _ in range(1, head_size)],
        ),
        (column.reshape(1), reads, out_proj),
        scalars=1,
        hbm=(2,),
        limit=49,
        scratch=[pltpu.VMEM((depth, columns), BF16), pltpu.SemaphoreType.DMA((head_size,))],
    )
    return call(
        project_rest_kernel, struct((tokens, columns), BF16), (own, *pieces, *rest)
    )


def solution(mesh):
    sizes = dict(mesh.shape)
    in_specs = (
        P("tok", "head"),
        P("tok", "head"),
        P("tok", "head"),
        P(None, "head", None, None),
        P("head"),
        P("tok"),
        P(None, "head"),
    )
    return jax.shard_map(
        functools.partial(on_device, sizes["tok"], sizes["head"]),
        mesh=mesh,
        in_specs=in_specs,
        out_specs=P("tok", "head"),
        check_vma=False,
    )
```

time: 80.6 us -> 69.5 us (0.86)
  waiting for transfers between devices: 28.9 us -> 22.1 us
  local copies, waits for them, and re-layouts: 9.2 us -> 3.43 us
  Pallas kernels: 15.9 us -> 17.4 us
  other arithmetic: 1.12 us -> 0 us
    ppermute x1 -> x2, waiting for transfers between devices: 16.6 us -> 10.9 us  [on_device(): parts = (*partials, *[lax.ppermute(code, 'tok', turn) for code in coded])]
    unnamed x11 -> x3, local copies, waits for them, and re-layouts: 5.87 us -> 1.25 us
    pallas_call x4 -> x7, Pallas kernels: 15.9 us -> 17.4 us  [call(): pl.pallas_call(kernel, out_shape=out_shape, in_specs=specs, out_specs=jax...]
    another operation x1 -> x0, other arithmetic: 1.07 us -> none  [on_device(): jnp.stack([by_head(keys), by_head(values * mask[:, None])], axis=1)]
    all_to_all x2, waiting for transfers between devices: 12.3 us -> 11.3 us  [shuffle(): return lax.all_to_all(x, 'tok', 0, 0, tiled=True, axis_index_groups=groups)]
    ppermute x1 -> x2, starting transfers between devices: 2.66 us -> 3.06 us  [on_device(): parts = (*partials, *[lax.ppermute(code, 'tok', turn) for code in coded])]
  transfers between devices with their start and end apart: 4 -> 5, of which waited for: 2 -> 3; matrix products, arithmetic and copies ran while one was open for 4% -> 5% of each run, Pallas kernels for 2% -> 13%
where the time goes in v3:
time: 69.5 us; the launch traced here: 69 us
  waiting for transfers between devices  22.1 us (32%)
  Pallas kernels  17.4 us (25%)
  starting transfers between devices  12.7 us (18%)
  blocking collectives  12.5 us (18%)
  local copies, waits for them, and re-layouts  3.43 us (5%)
  between operations  0.74 us (1%)
    pallas_call x7, Pallas kernels, call(): pl.pallas_call(kernel, out_shape=out_shape, in_specs=specs, out_specs=jax...  17.4 us
    all_to_all x1, blocking collectives, shuffle(): return lax.all_to_all(x, 'tok', 0, 0, tiled=True, axis_index_groups=groups)  12.5 us
    all_to_all x2, waiting for transfers between devices, shuffle(): return lax.all_to_all(x, 'tok', 0, 0, tiled=True, axis_index_groups=groups)  11.3 us
    ppermute x2, waiting for transfers between devices, on_device(): parts = (*partials, *[lax.ppermute(code, 'tok', turn) for code in coded])  10.9 us
    all_to_all x2, starting transfers between devices, shuffle(): return lax.all_to_all(x, 'tok', 0, 0, tiled=True, axis_index_groups=groups)  9.69 us
    ppermute x2, starting transfers between devices, on_device(): parts = (*partials, *[lax.ppermute(code, 'tok', turn) for code in coded])  3.06 us
  transfers between devices with their start and end apart: 5, of which 3 were waited for; matrix products, arithmetic and copies ran while one was open for 5% of the time, Pallas kernels for 13%

profile of v3, /device:TPU:0, one launch (start us, length us, event | category | flops | bytes accessed | tf_op | source)
XLA Modules:
  0.0 69.0 jit_solution(17894680576523669172)
XLA Ops:
  0.7 2.5 %shard_map.73 = bf16[8,2,256,128]{3,2,1,0:T(8,128)(2,1)} custom-call(s32[1,1]{1,0:T(1,128)} %bitcast.7.mask_ref, bf16[256,1024]{1,0:T(8,128)(2,1)} %keys_ref.1, bf16[256,1024]{1,0:T(8,128)(2,1)} %values_ref.1), custom_call_target="tpu_custom_call" | custom-call | tf_op jit(solution)/shard_map/pallas_call | solution.py:235
  3.1 6.2 %all-to-all-start = ((bf16[8,2,256,128]{3,2,1,0:T(8,128)(2,1)}), bf16[8,2,256,128]{3,2,1,0:T(8,128)(2,1)S(1)}, u32[]{:S(2)}, u32[]{:S(2)}) async-start(bf16[8,2,256,128]{3,2,1,0:T(8,128)(2,1)} %shard_map.73), calls=%async_computation | async-start | bytes 2097152 | tf_op jit(solution)/shard_map/all_to_all | solution.py:258
  9.3 1.2 %copy.8 = bf16[256,1024]{0,1:T(8,128)(2,1)S(1)} copy(bf16[256,1024]{1,0:T(8,128)(2,1)} %param.9) | data formatting | bytes 1048576 | tf_op args[2]
  10.6 1.0 %copy.9 = bf16[256,8,128]{2,0,1:T(8,128)(2,1)} copy(bf16[256,8,128]{0,2,1:T(8,128)(2,1)S(1)} %bitcast.9) | data formatting | bytes 1048576 | tf_op jit(solution)/shard_map/reshape | solution.py:293
  11.6 1.2 %dynamic-slice_bitcast_fusion.weights_ref.refs_4_ = f32[3,128,512]{2,1,0:T(8,128)S(1)} fusion(f32[3,8,128,512]{3,2,1,0:T(8,128)} %param.10, s32[]{:T(128)S(6)} %select_n.12), kind=kLoop, calls=%fused_computation | loop fusion | bytes 1572868 | tf_op jit(solution)/shard_map/jit(dynamic_index_in_dim)/squeeze | solution.py:275
  12.7 11.2 %all-to-all-done.recv_ref = bf16[8,2,256,128]{3,2,1,0:T(8,128)(2,1)S(1)} async-done(((bf16[8,2,256,128]{3,2,1,0:T(8,128)(2,1)}), bf16[8,2,256,128]{3,2,1,0:T(8,128)(2,1)S(1)}, u32[]{:S(2)}, u32[]{:S(2)}) %all-to-all-start) | async-done | bytes 1048608 | tf_op jit(solution)/shard_map/all_to_all | solution.py:258
  24.0 2.0 %shard_map.74 = (f32[3,128,256]{2,1,0:T(8,128)S(1)}, s16[784,128]{1,0:T(8,128)(2,1)S(1)}) custom-call(bf16[8,2,256,128]{3,2,1,0:T(8,128)(2,1)S(1)} %all-to-all-done.recv_ref, f32[3,128,512]{2,1,0:T(8,128)S(1)} %dynamic-slice_bitcast_fusion.weights_ref.refs_4_), custom_call_target="tpu_custom_call" | custom-call | flops 4294967296 | bytes 1048576 | tf_op jit(solution)/shard_map/pallas_call | solution.py:235
  26.0 0.0 copy-start
  26.0 2.7 %collective-permute-start = (s16[784,128]{1,0:T(8,128)(2,1)S(1)}, s16[784,128]{1,0:T(8,128)(2,1)S(1)}, u32[]{:S(2)}, u32[]{:S(2)}) collective-permute-start(s16[784,128]{1,0:T(8,128)(2,1)S(1)} %get-tuple-element.20), channel_id=1, source_target_pairs={{0,16},{2,18},{4,20},{6,22},{8,24},{10,26},{12,28},{14,30},{16,0},... | collective-permute-start | bytes 602120 | tf_op jit(solution)/shard_map/ppermute | solution.py:297
  28.6 2.0 %shard_map.75 = (f32[3,128,256]{2,1,0:T(8,128)S(1)}, s16[784,128]{1,0:T(8,128)(2,1)S(1)}) custom-call(bf16[8,2,256,128]{3,2,1,0:T(8,128)(2,1)S(1)} %all-to-all-done.recv_ref, f32[3,128,512]{2,1,0:T(8,128)S(1)} %dynamic-slice_bitcast_fusion.weights_ref.refs_4_), custom_call_target="tpu_custom_call" | custom-call | flops 4294967296 | bytes 1048576 | tf_op jit(solution)/shard_map/pallas_call | solution.py:235
  30.6 0.4 collective-permute-start.1
  31.0 3.5 %all-to-all-start.1 = ((bf16[8,256,128]{2,1,0:T(8,128)(2,1)}), bf16[8,256,128]{2,1,0:T(8,128)(2,1)S(1)}, u32[]{:S(2)}, u32[]{:S(2)}) async-start(bf16[8,256,128]{2,1,0:T(8,128)(2,1)} %bitcast.8), calls=%async_computation.1 | async-start | bytes 1048576 | tf_op jit(solution)/shard_map/all_to_all | solution.py:258
  34.5 8.6 %collective-permute-done.refs_2_ = s16[784,128]{1,0:T(8,128)(2,1)S(1)} collective-permute-done((s16[784,128]{1,0:T(8,128)(2,1)S(1)}, s16[784,128]{1,0:T(8,128)(2,1)S(1)}, u32[]{:S(2)}, u32[]{:S(2)}) %collective-permute-start) | collective-permute-done | bytes 200736 | tf_op jit(solution)/shard_map/ppermute | solution.py:297
  43.2 2.2 %collective-permute-done.1.refs_3_ = s16[784,128]{1,0:T(8,128)(2,1)S(1)} collective-permute-done((s16[784,128]{1,0:T(8,128)(2,1)S(1)}, s16[784,128]{1,0:T(8,128)(2,1)S(1)}, u32[]{:S(2)}, u32[]{:S(2)}) %collective-permute-start.1) | collective-permute-done | bytes 200736 | tf_op jit(solution)/shard_map/ppermute | solution.py:297
  45.4 0.0 copy-done
  45.4 4.8 %shard_map.76.new_ref = bf16[3,128,512]{2,1,0:T(8,128)(2,1)S(1)} custom-call(s32[1]{0:T(128)} %bitcast.1.slot_ref, f32[8]{0:T(128)S(1)} %copy-done, f32[3,128,256]{2,1,0:T(8,128)S(1)} %get-tuple-element.16.refs_0_, f32[3,128,256]{2,1,0:T(8,128)S(1)} %get-tuple-element.19.refs_1_, s16[784,128]{1,0:T(8,128)(2,1)S(1)} %collective-permute-done.refs_2_, ...), custom_call_target="tpu_custom_call" | custom-call | flops 8589934592 | bytes 1048576 | tf_op jit(solution)/shard_map/pallas_call | solution.py:235
  50.2 0.0 all-to-all-done.1.query_ref
  50.3 2.2 %shard_map.77 = bf16[8,256,128]{2,1,0:T(8,128)(2,1)S(1)} custom-call(bf16[3,128,512]{2,1,0:T(8,128)(2,1)S(1)} %shard_map.76.new_ref, bf16[8,256,128]{2,1,0:T(8,128)(2,1)S(1)} %all-to-all-done.1.query_ref), custom_call_target="tpu_custom_call" | custom-call | tf_op jit(solution)/shard_map/pallas_call | solution.py:235
  52.5 12.5 %all_to_all.15.read_ref = bf16[8,256,128]{2,1,0:T(8,128)(2,1)S(1)} all-to-all(bf16[8,256,128]{2,1,0:T(8,128)(2,1)S(1)} %shard_map.77), channel_id=1, replica_groups={{0,2,4,6,8,10,12,14},{16,18,20,22,24,26,28,30},{1,3,5,7,9,11,13,15},{17..., dimensions={0} | all-to-all | bytes 1048576 | tf_op jit(solution)/shard_map/all_to_all | solution.py:258
  65.0 0.0 collective-permute-start.2
  65.0 2.3 %shard_map.78 = (f32[256,1024]{1,0:T(8,128)S(1)}, bf16[1024,1024]{1,0:T(8,128)(2,1)S(1)}) custom-call(s32[1]{0:T(128)} %bitcast.column_ref, bf16[8,256,128]{2,1,0:T(8,128)(2,1)S(1)} %all_to_all.15.read_ref, bf16[2048,1024]{1,0:T(8,128)(2,1)} %weight_ref.1), custom_call_target="tpu_custom_call" | custom-call | tf_op jit(solution)/shard_map/pallas_call | solution.py:235
  67.4 0.0 collective-permute-done.2.refs_0_
  67.4 1.6 %shard_map.79 = bf16[256,1024]{1,0:T(8,128)(2,1)} custom-call(f32[256,1024]{1,0:T(8,128)S(1)} %get-tuple-element.25.sum_ref, bf16[8,256,128]{2,1,0:T(8,128)(2,1)S(1)} %collective-permute-done.2.refs_0_, bf16[1024,1024]{1,0:T(8,128)(2,1)S(1)} %get-tuple-element.26.refs_1_), custom_call_target="tpu_custom_call" | custom-call | tf_op jit(solution)/shard_map/pallas_call | solution.py:235
Async XLA Ops:
  3.1 20.9 %all-to-all-start = ((bf16[8,2,256,128]{3,2,1,0:T(8,128)(2,1)}), bf16[8,2,256,128]{3,2,1,0:T(8,128)(2,1)S(1)}, u32[]{:S(2)}, u32[]{:S(2)}) async-start(bf16[8,2,256,128]{3,2,1,0:T(8,128)(2,1)} %shard_map.73), calls=%async_computation | async-start | bytes 2097152 | tf_op jit(solution)/shard_map/all_to_all | solution.py:258
  26.0 19.4 %copy-start = (f32[8]{0:T(128)S(1)}, f32[8]{0:T(128)}, u32[]{:S(2)}) copy-start(f32[8]{0:T(128)} %rate_ref.1) | copy-start | bytes 100
  26.0 17.2 %collective-permute-start = (s16[784,128]{1,0:T(8,128)(2,1)S(1)}, s16[784,128]{1,0:T(8,128)(2,1)S(1)}, u32[]{:S(2)}, u32[]{:S(2)}) collective-permute-start(s16[784,128]{1,0:T(8,128)(2,1)S(1)} %get-tuple-element.20), channel_id=1, source_target_pairs={{0,16},{2,18},{4,20},{6,22},{8,24},{10,26},{12,28},{14,30},{16,0},... | collective-permute-start | bytes 602120 | tf_op jit(solution)/shard_map/ppermute | solution.py:297
  30.6 14.8 %collective-permute-start.1 = (s16[784,128]{1,0:T(8,128)(2,1)S(1)}, s16[784,128]{1,0:T(8,128)(2,1)S(1)}, u32[]{:S(2)}, u32[]{:S(2)}) collective-permute-start(s16[784,128]{1,0:T(8,128)(2,1)S(1)} %get-tuple-element.23), channel_id=1, source_target_pairs={{0,16},{2,18},{4,20},{6,22},{8,24},{10,26},{12,28},{14,30},{16,0},... | collective-permute-start | bytes 602120 | tf_op jit(solution)/shard_map/ppermute | solution.py:297
  31.0 19.2 %all-to-all-start.1 = ((bf16[8,256,128]{2,1,0:T(8,128)(2,1)}), bf16[8,256,128]{2,1,0:T(8,128)(2,1)S(1)}, u32[]{:S(2)}, u32[]{:S(2)}) async-start(bf16[8,256,128]{2,1,0:T(8,128)(2,1)} %bitcast.8), calls=%async_computation.1 | async-start | bytes 1048576 | tf_op jit(solution)/shard_map/all_to_all | solution.py:258
  65.0 2.3 %collective-permute-start.2 = (bf16[8,256,128]{2,1,0:T(8,128)(2,1)S(1)}, bf16[8,256,128]{2,1,0:T(8,128)(2,1)S(1)}, u32[]{:S(2)}, u32[]{:S(2)}) collective-permute-start(bf16[8,256,128]{2,1,0:T(8,128)(2,1)S(1)} %all_to_all.15.read_ref), channel_id=1, source_target_pairs={{0,1},{1,0},{2,3},{3,2},{4,5},{5,4},{6,7},{7,6},{8,9},{9,8},{10,11... | collective-permute-start | bytes 1572872 | tf_op jit(solution)/shard_map/ppermute | solution.py:315

commit v4 on v3

--- a/solution.py
+++ b/solution.py
@@ -249,13 +249,31 @@
     tokens = keys.shape[0]
     kinds, heads, dh, ff = fast_weights.shape
     column = lax.axis_index("head")
-    slot = lax.axis_index("tok") % heads
+    place = lax.axis_index("tok")
     count = tok_size // heads
-    groups = [[g * heads + i for i in range(heads)] for g in range(count)]
     struct = jax.ShapeDtypeStruct
+    both = ("tok", "head")
+
+    quarter = tok_size // 4
+    mixed = count == 2 and quarter * 4 == tok_size and head_size % 2 == 0
+    slot = place % heads
+    groups, turn = [], []
+    for h in range(head_size):
+        if mixed and h % 2 == 1:
+            order = [q * quarter + i for q in (0, 2, 1, 3) for i in range(quarter)]
+            partners = [t + quarter if t // quarter % 2 == 0 else t - quarter for t in range(tok_size)]
+        else:
+            order = list(range(tok_size))
+            partners = [(t + heads) % tok_size for t in range(tok_size)]
+        for g in range(count):
+            groups.append([t * head_size + h for t in order[g * heads : (g + 1) * heads]])
+        turn += [(t * head_size + h, partners[t] * head_size + h) for t in range(tok_size)]
+    if mixed:
+        other = place % quarter + quarter * (place // (2 * quarter))
+        slot = jnp.where(column % 2 == 1, other, slot)
 
     def shuffle(x):
-        return lax.all_to_all(x, "tok", 0, 0, tiled=True, axis_index_groups=groups)
+        return lax.all_to_all(x, both, 0, 0, tiled=True, axis_index_groups=groups)
 
     pairs = call(
         pack_kernel,
@@ -290,14 +308,14 @@
         code, received = lax.optimization_barrier((code, received))
         coded.append(code)
 
+    coded[-1], queries = lax.optimization_barrier((coded[-1], queries))
     packed = queries.reshape(tokens, heads, dh).transpose(1, 0, 2)
-    coded[-1], packed = lax.optimization_barrier((coded[-1], packed))
     if count == 2:
-        turn = [(i, (i + heads) % tok_size) for i in range(tok_size)]
-        parts = (*partials, *[lax.ppermute(code, "tok", turn) for code in coded])
+        arrived = [lax.ppermute(code, both, turn) for code in coded]
+        parts = (*partials, *arrived)
     else:
-        others = [[g * heads + i for g in range(count)] for i in range(heads)]
-        parts = lax.psum(tuple(partials), "tok", axis_index_groups=others)
+        same = [[g * heads + i for g in range(count)] for i in range(heads)]
+        parts = lax.psum(tuple(partials), "tok", axis_index_groups=same)
     asked = shuffle(packed)
     new = call(
         functools.partial(update_kernel, ITERS, count == 2),

time: 69.5 us -> 66.8 us (0.961)
  waiting for transfers between devices: 22.1 us -> 18.8 us
  starting transfers between devices: 12.7 us -> 13.5 us
    ppermute x2, waiting for transfers between devices: 10.9 us -> 2.58 us  [on_device(): arrived = [lax.ppermute(code, both, turn) for code in coded]]
    all_to_all x2, waiting for transfers between devices: 11.3 us -> 16.2 us  [shuffle(): return lax.all_to_all(x, both, 0, 0, tiled=True, axis_index_groups=groups)]
    optimization_barrier x0 -> x1, local copies, waits for them, and re-layouts: none -> 1.24 us  [on_device(): coded[-1], queries = lax.optimization_barrier((coded[-1], queries))]
    unnamed x3 -> x2, local copies, waits for them, and re-layouts: 1.25 us -> 0.01 us
    ppermute x1, starting transfers between devices: 0.01 us -> 0.73 us  [on_device(): lax.ppermute(reads, 'head', [(i, (i + s) % head_size) for i in range(head...]
  transfers between devices with their start and end apart: 5 -> 5, of which waited for: 3 -> 3; matrix products, arithmetic and copies ran while one was open for 5% -> 5% of each run, Pallas kernels for 13% -> 14%
where the time goes in v4:
time: 66.8 us; the launch traced here: 66.4 us
  waiting for transfers between devices  18.8 us (28%)
  Pallas kernels  17.4 us (26%)
  starting transfers between devices  13.5 us (20%)
  blocking collectives  12.5 us (19%)
  local copies, waits for them, and re-layouts  3.43 us (5%)
  between operations  0.74 us (1%)
    pallas_call x7, Pallas kernels, call(): pl.pallas_call(kernel, out_shape=out_shape, in_specs=specs, out_specs=jax...  17.4 us
    all_to_all x2, waiting for transfers between devices, shuffle(): return lax.all_to_all(x, both, 0, 0, tiled=True, axis_index_groups=groups)  16.2 us
    all_to_all x1, blocking collectives, shuffle(): return lax.all_to_all(x, both, 0, 0, tiled=True, axis_index_groups=groups)  12.5 us
    all_to_all x2, starting transfers between devices, shuffle(): return lax.all_to_all(x, both, 0, 0, tiled=True, axis_index_groups=groups)  9.69 us
    ppermute x2, starting transfers between devices, on_device(): arrived = [lax.ppermute(code, both, turn) for code in coded]  3.05 us
    ppermute x2, waiting for transfers between devices, on_device(): arrived = [lax.ppermute(code, both, turn) for code in coded]  2.58 us
  transfers between devices with their start and end apart: 5, of which 3 were waited for; matrix products, arithmetic and copies ran while one was open for 5% of the time, Pallas kernels for 14%

profile of v4, /device:TPU:0, one launch (start us, length us, event | category | flops | bytes accessed | tf_op | source)
XLA Modules:
  0.0 66.4 jit_solution(3266864881594766863)
XLA Ops:
  0.7 2.5 %shard_map.73 = bf16[8,2,256,128]{3,2,1,0:T(8,128)(2,1)} custom-call(s32[1,1]{1,0:T(1,128)} %bitcast.7.mask_ref, bf16[256,1024]{1,0:T(8,128)(2,1)} %keys_ref.1, bf16[256,1024]{1,0:T(8,128)(2,1)} %values_ref.1), custom_call_target="tpu_custom_call" | custom-call | tf_op jit(solution)/shard_map/pallas_call | solution.py:235
  3.1 6.2 %all-to-all-start = ((bf16[8,2,256,128]{3,2,1,0:T(8,128)(2,1)}), bf16[8,2,256,128]{3,2,1,0:T(8,128)(2,1)S(1)}, u32[]{:S(2)}, u32[]{:S(2)}) async-start(bf16[8,2,256,128]{3,2,1,0:T(8,128)(2,1)} %shard_map.73), calls=%async_computation | async-start | bytes 2097152 | tf_op jit(solution)/shard_map/all_to_all | solution.py:276
  9.3 1.2 %dynamic-slice_bitcast_fusion.weights_ref.refs_4_ = f32[3,128,512]{2,1,0:T(8,128)S(1)} fusion(f32[3,8,128,512]{3,2,1,0:T(8,128)} %param.10, s32[]{:T(128)S(6)} %select_n.31), kind=kLoop, calls=%fused_computation | loop fusion | bytes 1572868 | tf_op jit(solution)/shard_map/jit(dynamic_index_in_dim)/squeeze | solution.py:293
  10.5 15.1 %all-to-all-done.recv_ref = bf16[8,2,256,128]{3,2,1,0:T(8,128)(2,1)S(1)} async-done(((bf16[8,2,256,128]{3,2,1,0:T(8,128)(2,1)}), bf16[8,2,256,128]{3,2,1,0:T(8,128)(2,1)S(1)}, u32[]{:S(2)}, u32[]{:S(2)}) %all-to-all-start) | async-done | bytes 1048608 | tf_op jit(solution)/shard_map/all_to_all | solution.py:276
  25.6 2.0 %shard_map.74 = (f32[3,128,256]{2,1,0:T(8,128)S(1)}, s16[784,128]{1,0:T(8,128)(2,1)S(1)}) custom-call(bf16[8,2,256,128]{3,2,1,0:T(8,128)(2,1)S(1)} %all-to-all-done.recv_ref, f32[3,128,512]{2,1,0:T(8,128)S(1)} %dynamic-slice_bitcast_fusion.weights_ref.refs_4_), custom_call_target="tpu_custom_call" | custom-call | flops 4294967296 | bytes 1048576 | tf_op jit(solution)/shard_map/pallas_call | solution.py:235
  27.6 0.0 copy-start
  27.6 1.7 %collective-permute-start = (s16[784,128]{1,0:T(8,128)(2,1)S(1)}, s16[784,128]{1,0:T(8,128)(2,1)S(1)}, u32[]{:S(2)}, u32[]{:S(2)}) collective-permute-start(s16[784,128]{1,0:T(8,128)(2,1)S(1)} %get-tuple-element.20), channel_id=1, source_target_pairs={{0,16},{2,18},{4,20},{6,22},{8,24},{10,26},{12,28},{14,30},{16,0},... | collective-permute-start | bytes 602120 | tf_op jit(solution)/shard_map/ppermute | solution.py:314
  29.4 2.0 %shard_map.75 = (f32[3,128,256]{2,1,0:T(8,128)S(1)}, s16[784,128]{1,0:T(8,128)(2,1)S(1)}) custom-call(bf16[8,2,256,128]{3,2,1,0:T(8,128)(2,1)S(1)} %all-to-all-done.recv_ref, f32[3,128,512]{2,1,0:T(8,128)S(1)} %dynamic-slice_bitcast_fusion.weights_ref.refs_4_), custom_call_target="tpu_custom_call" | custom-call | flops 4294967296 | bytes 1048576 | tf_op jit(solution)/shard_map/pallas_call | solution.py:235
  31.3 1.3 %collective-permute-start.1 = (s16[784,128]{1,0:T(8,128)(2,1)S(1)}, s16[784,128]{1,0:T(8,128)(2,1)S(1)}, u32[]{:S(2)}, u32[]{:S(2)}) collective-permute-start(s16[784,128]{1,0:T(8,128)(2,1)S(1)} %get-tuple-element.23), channel_id=1, source_target_pairs={{0,16},{2,18},{4,20},{6,22},{8,24},{10,26},{12,28},{14,30},{16,0},... | collective-permute-start | bytes 602120 | tf_op jit(solution)/shard_map/ppermute | solution.py:314
  32.7 1.2 %copy.8 = bf16[256,1024]{0,1:T(8,128)(2,1)S(1)} copy(bf16[256,1024]{1,0:T(8,128)(2,1)} %param.9) | data formatting | bytes 1048576 | tf_op jit(solution)/shard_map/optimization_barrier | solution.py:311
  33.9 1.0 %copy.9 = bf16[256,8,128]{2,0,1:T(8,128)(2,1)} copy(bf16[256,8,128]{0,2,1:T(8,128)(2,1)S(1)} %bitcast.9) | data formatting | bytes 1048576 | tf_op jit(solution)/shard_map/reshape | solution.py:312
  34.9 3.5 %all-to-all-start.1 = ((bf16[8,256,128]{2,1,0:T(8,128)(2,1)}), bf16[8,256,128]{2,1,0:T(8,128)(2,1)S(1)}, u32[]{:S(2)}, u32[]{:S(2)}) async-start(bf16[8,256,128]{2,1,0:T(8,128)(2,1)} %bitcast.8), calls=%async_computation.1 | async-start | bytes 1048576 | tf_op jit(solution)/shard_map/all_to_all | solution.py:276
  38.4 0.0 collective-permute-done.refs_2_
  38.4 2.6 %collective-permute-done.1.refs_3_ = s16[784,128]{1,0:T(8,128)(2,1)S(1)} collective-permute-done((s16[784,128]{1,0:T(8,128)(2,1)S(1)}, s16[784,128]{1,0:T(8,128)(2,1)S(1)}, u32[]{:S(2)}, u32[]{:S(2)}) %collective-permute-start.1) | collective-permute-done | bytes 200736 | tf_op jit(solution)/shard_map/ppermute | solution.py:314
  41.0 0.0 copy-done
  41.0 4.8 %shard_map.76.new_ref = bf16[3,128,512]{2,1,0:T(8,128)(2,1)S(1)} custom-call(s32[1]{0:T(128)} %bitcast.1.slot_ref, f32[8]{0:T(128)S(1)} %copy-done, f32[3,128,256]{2,1,0:T(8,128)S(1)} %get-tuple-element.16.refs_0_, f32[3,128,256]{2,1,0:T(8,128)S(1)} %get-tuple-element.19.refs_1_, s16[784,128]{1,0:T(8,128)(2,1)S(1)} %collective-permute-done.refs_2_, ...), custom_call_target="tpu_custom_call" | custom-call | flops 8589934592 | bytes 1048576 | tf_op jit(solution)/shard_map/pallas_call | solution.py:235
  45.8 1.1 %all-to-all-done.1.query_ref = bf16[8,256,128]{2,1,0:T(8,128)(2,1)S(1)} async-done(((bf16[8,256,128]{2,1,0:T(8,128)(2,1)}), bf16[8,256,128]{2,1,0:T(8,128)(2,1)S(1)}, u32[]{:S(2)}, u32[]{:S(2)}) %all-to-all-start.1) | async-done | bytes 524320 | tf_op jit(solution)/shard_map/all_to_all | solution.py:276
  46.9 2.2 %shard_map.77 = bf16[8,256,128]{2,1,0:T(8,128)(2,1)S(1)} custom-call(bf16[3,128,512]{2,1,0:T(8,128)(2,1)S(1)} %shard_map.76.new_ref, bf16[8,256,128]{2,1,0:T(8,128)(2,1)S(1)} %all-to-all-done.1.query_ref), custom_call_target="tpu_custom_call" | custom-call | tf_op jit(solution)/shard_map/pallas_call | solution.py:235
  49.2 12.5 %all_to_all.15.read_ref = bf16[8,256,128]{2,1,0:T(8,128)(2,1)S(1)} all-to-all(bf16[8,256,128]{2,1,0:T(8,128)(2,1)S(1)} %shard_map.77), channel_id=1, replica_groups={{0,2,4,6,8,10,12,14},{16,18,20,22,24,26,28,30},{1,3,5,7,17,19,21,23},{9..., dimensions={0} | all-to-all | bytes 1048576 | tf_op jit(solution)/shard_map/all_to_all | solution.py:276
  61.7 0.7 %collective-permute-start.2 = (bf16[8,256,128]{2,1,0:T(8,128)(2,1)S(1)}, bf16[8,256,128]{2,1,0:T(8,128)(2,1)S(1)}, u32[]{:S(2)}, u32[]{:S(2)}) collective-permute-start(bf16[8,256,128]{2,1,0:T(8,128)(2,1)S(1)} %all_to_all.15.read_ref), channel_id=1, source_target_pairs={{0,1},{1,0},{2,3},{3,2},{4,5},{5,4},{6,7},{7,6},{8,9},{9,8},{10,11... | collective-permute-start | bytes 1572872 | tf_op jit(solution)/shard_map/ppermute | solution.py:333
  62.4 2.3 %shard_map.78 = (f32[256,1024]{1,0:T(8,128)S(1)}, bf16[1024,1024]{1,0:T(8,128)(2,1)S(1)}) custom-call(s32[1]{0:T(128)} %bitcast.column_ref, bf16[8,256,128]{2,1,0:T(8,128)(2,1)S(1)} %all_to_all.15.read_ref, bf16[2048,1024]{1,0:T(8,128)(2,1)} %weight_ref.1), custom_call_target="tpu_custom_call" | custom-call | tf_op jit(solution)/shard_map/pallas_call | solution.py:235
  64.7 0.0 collective-permute-done.2.refs_0_
  64.7 1.6 %shard_map.79 = bf16[256,1024]{1,0:T(8,128)(2,1)} custom-call(f32[256,1024]{1,0:T(8,128)S(1)} %get-tuple-element.25.sum_ref, bf16[8,256,128]{2,1,0:T(8,128)(2,1)S(1)} %collective-permute-done.2.refs_0_, bf16[1024,1024]{1,0:T(8,128)(2,1)S(1)} %get-tuple-element.26.refs_1_), custom_call_target="tpu_custom_call" | custom-call | tf_op jit(solution)/shard_map/pallas_call | solution.py:235
Async XLA Ops:
  3.1 22.5 %all-to-all-start = ((bf16[8,2,256,128]{3,2,1,0:T(8,128)(2,1)}), bf16[8,2,256,128]{3,2,1,0:T(8,128)(2,1)S(1)}, u32[]{:S(2)}, u32[]{:S(2)}) async-start(bf16[8,2,256,128]{3,2,1,0:T(8,128)(2,1)} %shard_map.73), calls=%async_computation | async-start | bytes 2097152 | tf_op jit(solution)/shard_map/all_to_all | solution.py:276
  27.6 13.4 %copy-start = (f32[8]{0:T(128)S(1)}, f32[8]{0:T(128)}, u32[]{:S(2)}) copy-start(f32[8]{0:T(128)} %rate_ref.1) | copy-start | bytes 100
  27.6 10.8 %collective-permute-start = (s16[784,128]{1,0:T(8,128)(2,1)S(1)}, s16[784,128]{1,0:T(8,128)(2,1)S(1)}, u32[]{:S(2)}, u32[]{:S(2)}) collective-permute-start(s16[784,128]{1,0:T(8,128)(2,1)S(1)} %get-tuple-element.20), channel_id=1, source_target_pairs={{0,16},{2,18},{4,20},{6,22},{8,24},{10,26},{12,28},{14,30},{16,0},... | collective-permute-start | bytes 602120 | tf_op jit(solution)/shard_map/ppermute | solution.py:314
  31.3 9.7 %collective-permute-start.1 = (s16[784,128]{1,0:T(8,128)(2,1)S(1)}, s16[784,128]{1,0:T(8,128)(2,1)S(1)}, u32[]{:S(2)}, u32[]{:S(2)}) collective-permute-start(s16[784,128]{1,0:T(8,128)(2,1)S(1)} %get-tuple-element.23), channel_id=1, source_target_pairs={{0,16},{2,18},{4,20},{6,22},{8,24},{10,26},{12,28},{14,30},{16,0},... | collective-permute-start | bytes 602120 | tf_op jit(solution)/shard_map/ppermute | solution.py:314
  34.9 12.0 %all-to-all-start.1 = ((bf16[8,256,128]{2,1,0:T(8,128)(2,1)}), bf16[8,256,128]{2,1,0:T(8,128)(2,1)S(1)}, u32[]{:S(2)}, u32[]{:S(2)}) async-start(bf16[8,256,128]{2,1,0:T(8,128)(2,1)} %bitcast.8), calls=%async_computation.1 | async-start | bytes 1048576 | tf_op jit(solution)/shard_map/all_to_all | solution.py:276
  61.7 3.1 %collective-permute-start.2 = (bf16[8,256,128]{2,1,0:T(8,128)(2,1)S(1)}, bf16[8,256,128]{2,1,0:T(8,128)(2,1)S(1)}, u32[]{:S(2)}, u32[]{:S(2)}) collective-permute-start(bf16[8,256,128]{2,1,0:T(8,128)(2,1)S(1)} %all_to_all.15.read_ref), channel_id=1, source_target_pairs={{0,1},{1,0},{2,3},{3,2},{4,5},{5,4},{6,7},{7,6},{8,9},{9,8},{10,11... | collective-permute-start | bytes 1572872 | tf_op jit(solution)/shard_map/ppermute | solution.py:333

commit v5 on v4

--- a/solution.py
+++ b/solution.py
@@ -67,8 +67,9 @@
         store.wait()
 
 
-def gradient_kernel(chunk, start, recv_ref, weights_ref, grads_ref, coded_ref):
+def gradient_kernel(chunk, start, recv_ref, weights_ref, out_ref, *scratch):
     sources, _, sub, dh = recv_ref.shape
+    grads_ref = scratch[0] if scratch else out_ref
     ff = grads_ref.shape[-1]
     units = pl.ds(start, ff)
     gate_up = jnp.concatenate([weights_ref[0, :, units], weights_ref[2, :, units]], axis=1).astype(BF16)
@@ -89,7 +90,8 @@
         sums = (sums[:, :ff], dot(values.T, hidden), sums[:, ff:])
         for m, value in enumerate(sums):
             grads_ref[m] = value if i == 0 else grads_ref[m] + value
-    encode(grads_ref, coded_ref)
+    if scratch:
+        encode(grads_ref, out_ref)
 
 
 def encode(grads_ref, coded_ref):
@@ -125,50 +127,80 @@
     return -(-columns // 16) * 16
 
 
+def square_product(a, b):
+    (ah, al), (bh, bl) = a, b
+    size = bh.shape[1]
+    wide = jnp.concatenate([bh, bl], axis=1)
+    both = dot(jnp.concatenate([ah, al], axis=1), jnp.concatenate([wide, wide], axis=0))
+    return both[:, :size] + both[:, size:]
+
+
 def product(a, b):
     (ah, al), (bh, bl) = a, b
     return dot(jnp.concatenate([ah, al], axis=1), jnp.concatenate([bh, bh], axis=0)) + dot(ah, bl)
 
 
-def newton_schulz(iterates, iters):
-    for _ in range(iters):
-        split = [halves(x) for x in iterates]
-        gram = []
-        for high, low in split:
-            both = dot(high, jnp.concatenate([high, low], axis=0), NT)
-            size = high.shape[0]
-            cross = both[:, size:]
-            gram.append(both[:, :size] + (cross + cross.T))
-        gram_split = [halves(a) for a in gram]
-        square = []
-        for high, low in gram_split:
-            wide = jnp.concatenate([high, low], axis=1)
-            under = jnp.concatenate([high, jnp.zeros_like(high)], axis=1)
-            both = dot(wide, jnp.concatenate([wide, under], axis=0))
-            size = high.shape[0]
-            square.append(both[:, :size] + both[:, size:])
-        poly = [halves(COEF_B * a + COEF_C * b) for a, b in zip(gram, square)]
-        iterates = [COEF_A * x + product(p, s) for x, p, s in zip(iterates, poly, split)]
-    return iterates
+def gram(x):
+    high, low = x
+    size = high.shape[0]
+    both = dot(high, jnp.concatenate([high, low], axis=0), NT)
+    cross = both[:, size:]
+    return both[:, :size] + (cross + cross.T)
+
+
+def newton_schulz(grads, iters):
+    size = grads[0].shape[0]
+    lines = lax.broadcasted_iota(jnp.int32, (size, size), 0)
+    diagonal = lines == lax.broadcasted_iota(jnp.int32, (size, size), 1)
+    split = [halves(x) for x in grads]
+    grams = [gram(x) for x in split]
+    scales = [
+        1.0 / (jnp.sum(jnp.where(diagonal, a, 0.0), axis=(0, 1), keepdims=True) + 1e-06)
+        for a in grams
+    ]
+    grams = [a * scale for a, scale in zip(grams, scales)]
+    parts = [halves(a) for a in grams]
+    polys = [halves(COEF_B * a + COEF_C * square_product(p, p)) for a, p in zip(grams, parts)]
+    iterates = [
+        (COEF_A * x + product(p, s)) * jnp.sqrt(scale)
+        for x, p, s, scale in zip(grads, polys, split, scales)
+    ]
+    split = [halves(x) for x in iterates]
+    grams = [gram(x) for x in split]
+    steps = None
+    for left in range(iters - 2, -1, -1):
+        parts = [halves(a) for a in grams]
+        polys = [
+            halves(jnp.where(diagonal, COEF_A, 0.0) + (COEF_B * a + COEF_C * square_product(p, p)))
+            for a, p in zip(grams, parts)
+        ]
+        if left > 0:
+            inner = [halves(square_product(p, a)) for p, a in zip(polys, parts)]
+            grams = [square_product(a, p) for a, p in zip(inner, polys)]
+            if steps is None:
+                steps = polys
+            else:
+                steps = [halves(square_product(p, q)) for p, q in zip(polys, steps)]
+        if left == 1:
+            split = [halves(product(q, s)) for q, s in zip(steps, split)]
+    return [product(p, s) for p, s in zip(polys, split)]
 
 
 def update_kernel(iters, coded, slot_ref, rate_ref, *refs):
-    weights_ref, new_ref = refs[-2:]
+    parts, (weights_ref, new_ref) = refs[:-2], refs[-2:]
     kinds, dh, ff = weights_ref.shape
     rate = rate_ref[slot_ref[0]]
-    partials, others = refs[:-2], ()
-    if coded:
-        partials, others = refs[: len(refs) // 2 - 1], refs[len(refs) // 2 - 1 : -2]
     iterates = []
     for m in range(kinds):
-        blocks = [partial[m] for partial in partials]
         if coded:
+            width = ff // (len(parts) // 2)
             blocks = [
-                block + decode(other, m, dh, block.shape[-1])
-                for block, other in zip(blocks, others)
+                decode(own, m, dh, width) + decode(other, m, dh, width)
+                for own, other in zip(parts[::2], parts[1::2])
             ]
-        grad = jnp.concatenate(blocks, axis=1)
-        iterates.append(grad * lax.rsqrt(jnp.sum(grad * grad) + 1e-06))
+        else:
+            blocks = [part[m] for part in parts]
+        iterates.append(jnp.concatenate(blocks, axis=1))
     iterates = newton_schulz(iterates, iters)
     for m in range(kinds):
         old = weights_ref[m]
@@ -178,22 +210,29 @@
         new_ref[m] = (new * (old_norm / new_norm)).astype(BF16)
 
 
-def read_kernel(chunk, new_ref, query_ref, read_ref):
-    sources, sub, dh = query_ref.shape
+def merge_kernel(mine_ref, theirs_ref, both_ref):
+    both_ref[:, 0] = mine_ref[...]
+    both_ref[:, 1] = theirs_ref[...]
+
+
+def read_kernel(chunk, side_ref, new_ref, query_ref, read_ref):
+    half, sides, sub, dh = query_ref.shape
     ff = new_ref.shape[-1]
     gate_up = jnp.concatenate([new_ref[0], new_ref[2]], axis=1)
     down = new_ref[1]
 
     def step(i, _):
         rows = pl.ds(i * chunk, chunk)
-        pre = dot(query_ref[rows].reshape(chunk * sub, dh), gate_up)
+        pre = dot(query_ref[rows].reshape(chunk * sides * sub, dh), gate_up)
         gate, up = pre[:, :ff], pre[:, ff:]
         hidden = (gate * sigmoid(gate) * up).astype(BF16)
-        read = dot(hidden, down, NT).astype(BF16)
-        read_ref[rows] = read.reshape(chunk, sub, dh)
+        read = dot(hidden, down, NT).astype(BF16).reshape(chunk, sides, sub, dh)
+        for p in range(sides):
+            at = (side_ref[0] if p == 0 else 1 - side_ref[0]) * half + i * chunk
+            read_ref[pl.ds(at, chunk)] = read[:, p]
         return 0
 
-    lax.fori_loop(0, sources // chunk, step, 0)
+    lax.fori_loop(0, half // chunk, step, 0)
 
 
 def flat_heads(read_ref):
@@ -271,6 +310,9 @@
     if mixed:
         other = place % quarter + quarter * (place // (2 * quarter))
         slot = jnp.where(column % 2 == 1, other, slot)
+    turned = heads // 2
+    groups = [g[turned:] + g[:turned] for g in groups]
+    slot = (slot + heads - turned) % heads
 
     def shuffle(x):
         return lax.all_to_all(x, both, 0, 0, tiled=True, axis_index_groups=groups)
@@ -290,42 +332,53 @@
         ],
     )
     received = shuffle(pairs)
+    packed = queries.reshape(tokens, heads, dh).transpose(1, 0, 2)
+    half = max(1, heads // 2)
+    side = slot // half
+    halves_of = [g[i : i + half] for g in groups for i in range(0, heads, half)]
+    across = [(g[i], g[(i + half) % heads]) for g in groups for i in range(heads)]
+    theirs = lax.dynamic_slice_in_dim(packed, (1 - side) * half, half, 0)
+    theirs = lax.ppermute(theirs, both, across)
+    mine = lax.dynamic_slice_in_dim(packed, side * half, half, 0)
+    asked = call(merge_kernel, struct((half, 2, tokens, dh), BF16), (mine, theirs))
     weights = lax.dynamic_index_in_dim(fast_weights, slot, 1, keepdims=False)
     chunk = max(c for c in (1, 2, 4) if heads % c == 0)
     split = 2 if ff % (2 * LANES) == 0 else 1
     width = ff // split
-    partials, coded = [], []
+    coded = count == 2
+    partials = []
     for start in range(0, ff, width):
+        sums = struct((kinds, dh, width), F32)
         rows = kinds * dh * width // LANES + code_rows(kinds * width // LANES)
-        partial, code = call(
+        partial = call(
             functools.partial(gradient_kernel, max(1, chunk // 2), start),
-            (struct((kinds, dh, width), F32), struct((rows, LANES), jnp.int16)),
+            struct((rows, LANES), jnp.int16) if coded else sums,
             (received, weights),
             flops=2**32,
             limit=16,
+            scratch=[pltpu.VMEM(sums.shape, F32)] if coded else [],
         )
         partials.append(partial)
-        code, received = lax.optimization_barrier((code, received))
-        coded.append(code)
-
-    coded[-1], queries = lax.optimization_barrier((coded[-1], queries))
-    packed = queries.reshape(tokens, heads, dh).transpose(1, 0, 2)
-    if count == 2:
-        arrived = [lax.ppermute(code, both, turn) for code in coded]
-        parts = (*partials, *arrived)
+
+    asked = lax.all_to_all(asked, both, 0, 0, tiled=True, axis_index_groups=halves_of)
+    if coded:
+        parts = [x for code in partials for x in (code, lax.ppermute(code, both, turn))]
     else:
         same = [[g * heads + i for g in range(count)] for i in range(heads)]
         parts = lax.psum(tuple(partials), "tok", axis_index_groups=same)
-    asked = shuffle(packed)
     new = call(
-        functools.partial(update_kernel, ITERS, count == 2),
+        functools.partial(update_kernel, ITERS, coded),
         struct((kinds, dh, ff), BF16),
         (slot.reshape(1), step_size, *parts, weights),
         scalars=2,
         flops=2**33,
     )
     read = call(
-        functools.partial(read_kernel, chunk), struct((heads, tokens, dh), BF16), (new, asked), limit=16
+        functools.partial(read_kernel, max(1, chunk // 2)),
+        struct((heads, tokens, dh), BF16),
+        (side.reshape(1), new, asked),
+        scalars=1,
+        limit=16,
     )
 
     reads = shuffle(read)

time: 66.8 us -> 64.8 us (0.970)
  waiting for transfers between devices: 18.8 us -> 15.3 us
  blocking collectives: 12.5 us -> 14.1 us
    all_to_all x2 -> x1, waiting for transfers between devices: 16.2 us -> 12.2 us  [shuffle(): return lax.all_to_all(x, both, 0, 0, tiled=True, axis_index_groups=groups)]
    all_to_all x0 -> x1, starting transfers between devices: none -> 3.9 us  [on_device(): lax.all_to_all(asked, both, 0, 0, tiled=True, axis_index_groups=halves_of)]
    all_to_all x2 -> x1, starting transfers between devices: 9.69 us -> 6.76 us  [shuffle(): return lax.all_to_all(x, both, 0, 0, tiled=True, axis_index_groups=groups)]
    all_to_all x1, blocking collectives: 12.5 us -> 14.1 us  [shuffle(): return lax.all_to_all(x, both, 0, 0, tiled=True, axis_index_groups=groups)]
    unnamed x2 -> x5, local copies, waits for them, and re-layouts: 0.01 us -> 1.61 us
    optimization_barrier x1 -> x0, local copies, waits for them, and re-layouts: 1.24 us -> none  [on_device(): coded[-1], queries = lax.optimization_barrier((coded[-1], queries))]
    reshape x1 -> x0, local copies, waits for them, and re-layouts: 1 us -> none  [on_device(): packed = queries.reshape(tokens, heads, dh).transpose(1, 0, 2)]
    ppermute x1, starting transfers between devices: 0.73 us -> 0.01 us  [on_device(): lax.ppermute(reads, 'head', [(i, (i + s) % head_size) for i in range(head...]
  transfers between devices with their start and end apart: 5 -> 6, of which waited for: 3 -> 2; matrix products, arithmetic and copies ran while one was open for 5% -> 4% of each run, Pallas kernels for 14% -> 17%
where the time goes in v5:
time: 64.8 us; the launch traced here: 64.3 us
  Pallas kernels  17.5 us (27%)
  waiting for transfers between devices  15.3 us (24%)
  blocking collectives  14.1 us (22%)
  starting transfers between devices  13.8 us (21%)
  local copies, waits for them, and re-layouts  2.84 us (4%)
  between operations  0.79 us (1%)
    pallas_call x8, Pallas kernels, call(): pl.pallas_call(kernel, out_shape=out_shape, in_specs=specs, out_specs=jax...  17.5 us
    all_to_all x1, blocking collectives, shuffle(): return lax.all_to_all(x, both, 0, 0, tiled=True, axis_index_groups=groups)  14.1 us
    all_to_all x1, waiting for transfers between devices, shuffle(): return lax.all_to_all(x, both, 0, 0, tiled=True, axis_index_groups=groups)  12.2 us
    all_to_all x1, starting transfers between devices, shuffle(): return lax.all_to_all(x, both, 0, 0, tiled=True, axis_index_groups=groups)  6.76 us
    all_to_all x1, starting transfers between devices, on_device(): lax.all_to_all(asked, both, 0, 0, tiled=True, axis_index_groups=halves_of)  3.9 us
    ppermute x2, waiting for transfers between devices, on_device(): lax.ppermute(code, both, turn)  3.11 us
    ppermute x2, starting transfers between devices, on_device(): lax.ppermute(code, both, turn)  3.06 us
    unnamed x5, local copies, waits for them, and re-layouts  1.61 us
  transfers between devices with their start and end apart: 6, of which 2 were waited for; matrix products, arithmetic and copies ran while one was open for 4% of the time, Pallas kernels for 17%

profile of v5, /device:TPU:0, one launch (start us, length us, event | category | flops | bytes accessed | tf_op | source)
XLA Modules:
  0.0 64.3 jit_solution(13819946858562419233)
XLA Ops:
  0.7 2.5 %shard_map.73 = bf16[8,2,256,128]{3,2,1,0:T(8,128)(2,1)} custom-call(s32[1,1]{1,0:T(1,128)} %bitcast.9.mask_ref, bf16[256,1024]{1,0:T(8,128)(2,1)} %keys_ref.1, bf16[256,1024]{1,0:T(8,128)(2,1)} %values_ref.1), custom_call_target="tpu_custom_call" | custom-call | tf_op jit(solution)/shard_map/pallas_call | solution.py:274
  3.1 6.8 %all-to-all-start = ((bf16[8,2,256,128]{3,2,1,0:T(8,128)(2,1)}), bf16[8,2,256,128]{3,2,1,0:T(8,128)(2,1)S(1)}, u32[]{:S(2)}, u32[]{:S(2)}) async-start(bf16[8,2,256,128]{3,2,1,0:T(8,128)(2,1)} %shard_map.73), calls=%async_computation | async-start | bytes 2097152 | tf_op jit(solution)/shard_map/all_to_all | solution.py:318
  9.9 1.2 %copy.8 = bf16[256,1024]{0,1:T(8,128)(2,1)S(1)} copy(bf16[256,1024]{1,0:T(8,128)(2,1)} %param.9) | data formatting | bytes 1048576 | tf_op args[2]
  11.2 0.2 copy.12
  11.4 0.1 collective-permute-start.2
  11.4 1.2 %dynamic-slice_bitcast_fusion.weights_ref.refs_4_ = f32[3,128,512]{2,1,0:T(8,128)S(1)} fusion(f32[3,8,128,512]{3,2,1,0:T(8,128)} %param.10, s32[]{:T(128)S(6)} %select_n.46), kind=kLoop, calls=%fused_computation | loop fusion | bytes 1572868 | tf_op jit(solution)/shard_map/jit(dynamic_index_in_dim)/squeeze | solution.py:344
  12.6 12.2 %all-to-all-done.recv_ref = bf16[8,2,256,128]{3,2,1,0:T(8,128)(2,1)S(1)} async-done(((bf16[8,2,256,128]{3,2,1,0:T(8,128)(2,1)}), bf16[8,2,256,128]{3,2,1,0:T(8,128)(2,1)S(1)}, u32[]{:S(2)}, u32[]{:S(2)}) %all-to-all-start) | async-done | bytes 1048608 | tf_op jit(solution)/shard_map/all_to_all | solution.py:318
  24.8 2.0 %shard_map.74.refs_0_ = s16[784,128]{1,0:T(8,128)(2,1)S(1)} custom-call(bf16[8,2,256,128]{3,2,1,0:T(8,128)(2,1)S(1)} %all-to-all-done.recv_ref, f32[3,128,512]{2,1,0:T(8,128)S(1)} %dynamic-slice_bitcast_fusion.weights_ref.refs_4_), custom_call_target="tpu_custom_call" | custom-call | flops 4294967296 | bytes 1048576 | tf_op jit(solution)/shard_map/pallas_call | solution.py:274
  26.8 0.0 copy-start
  26.8 1.1 %collective-permute-start = (s16[784,128]{1,0:T(8,128)(2,1)S(1)}, s16[784,128]{1,0:T(8,128)(2,1)S(1)}, u32[]{:S(2)}, u32[]{:S(2)}) collective-permute-start(s16[784,128]{1,0:T(8,128)(2,1)S(1)} %shard_map.74.refs_0_), channel_id=1, source_target_pairs={{0,16},{2,18},{4,20},{6,22},{8,24},{10,26},{12,28},{14,30},{16,0},... | collective-permute-start | bytes 602120 | tf_op jit(solution)/shard_map/ppermute | solution.py:365
  28.0 2.0 %shard_map.75.refs_2_ = s16[784,128]{1,0:T(8,128)(2,1)S(1)} custom-call(bf16[8,2,256,128]{3,2,1,0:T(8,128)(2,1)S(1)} %all-to-all-done.recv_ref, f32[3,128,512]{2,1,0:T(8,128)S(1)} %dynamic-slice_bitcast_fusion.weights_ref.refs_4_), custom_call_target="tpu_custom_call" | custom-call | flops 4294967296 | bytes 1048576 | tf_op jit(solution)/shard_map/pallas_call | solution.py:274
  30.0 1.9 %collective-permute-start.1 = (s16[784,128]{1,0:T(8,128)(2,1)S(1)}, s16[784,128]{1,0:T(8,128)(2,1)S(1)}, u32[]{:S(2)}, u32[]{:S(2)}) collective-permute-start(s16[784,128]{1,0:T(8,128)(2,1)S(1)} %shard_map.75.refs_2_), channel_id=1, source_target_pairs={{0,16},{2,18},{4,20},{6,22},{8,24},{10,26},{12,28},{14,30},{16,0},... | collective-permute-start | bytes 602120 | tf_op jit(solution)/shard_map/ppermute | solution.py:365
  31.9 0.2 copy.11
  32.1 0.0 collective-permute-done.2.theirs_ref
  32.1 0.8 %shard_map.77 = bf16[4,2,256,128]{3,2,1,0:T(8,128)(2,1)} custom-call(bf16[4,256,128]{2,1,0:T(8,128)(2,1)S(1)} %bitcast.10, bf16[4,256,128]{2,1,0:T(8,128)(2,1)S(1)} %collective-permute-done.2.theirs_ref), custom_call_target="tpu_custom_call" | custom-call | tf_op jit(solution)/shard_map/pallas_call | solution.py:274
  32.9 3.9 %all-to-all-start.1 = ((bf16[4,2,256,128]{3,2,1,0:T(8,128)(2,1)}), bf16[4,2,256,128]{3,2,1,0:T(8,128)(2,1)S(1)}, u32[]{:S(2)}, u32[]{:S(2)}) async-start(bf16[4,2,256,128]{3,2,1,0:T(8,128)(2,1)} %shard_map.77), calls=%async_computation.1 | async-start | bytes 1048576 | tf_op jit(solution)/shard_map/all_to_all | solution.py:363
  36.8 0.0 collective-permute-done.refs_1_
  36.8 3.1 %collective-permute-done.1.refs_3_ = s16[784,128]{1,0:T(8,128)(2,1)S(1)} collective-permute-done((s16[784,128]{1,0:T(8,128)(2,1)S(1)}, s16[784,128]{1,0:T(8,128)(2,1)S(1)}, u32[]{:S(2)}, u32[]{:S(2)}) %collective-permute-start.1) | collective-permute-done | bytes 200736 | tf_op jit(solution)/shard_map/ppermute | solution.py:365
  39.9 0.0 copy-done
  39.9 4.1 %shard_map.76.new_ref = bf16[3,128,512]{2,1,0:T(8,128)(2,1)S(1)} custom-call(s32[1]{0:T(128)} %bitcast.2.slot_ref, f32[8]{0:T(128)S(1)} %copy-done, s16[784,128]{1,0:T(8,128)(2,1)S(1)} %shard_map.74.refs_0_, s16[784,128]{1,0:T(8,128)(2,1)S(1)} %collective-permute-done.refs_1_, s16[784,128]{1,0:T(8,128)(2,1)S(1)} %shard_map.75.refs_2_, ...), custom_call_target="tpu_custom_call" | custom-call | flops 8589934592 | bytes 1048576 | tf_op jit(solution)/shard_map/pallas_call | solution.py:274
  44.0 0.0 all-to-all-done.1.query_ref
  44.0 2.2 %shard_map.78 = bf16[8,256,128]{2,1,0:T(8,128)(2,1)S(1)} custom-call(s32[1]{0:T(128)} %bitcast.1.side_ref, bf16[3,128,512]{2,1,0:T(8,128)(2,1)S(1)} %shard_map.76.new_ref, bf16[4,2,256,128]{3,2,1,0:T(8,128)(2,1)S(1)} %all-to-all-done.1.query_ref), custom_call_target="tpu_custom_call" | custom-call | tf_op jit(solution)/shard_map/pallas_call | solution.py:274
  46.2 14.1 %all_to_all.15.read_ref = bf16[8,256,128]{2,1,0:T(8,128)(2,1)S(1)} all-to-all(bf16[8,256,128]{2,1,0:T(8,128)(2,1)S(1)} %shard_map.78), channel_id=1, replica_groups={{8,10,12,14,0,2,4,6},{24,26,28,30,16,18,20,22},{17,19,21,23,1,3,5,7},{2..., dimensions={0} | all-to-all | bytes 1048576 | tf_op jit(solution)/shard_map/all_to_all | solution.py:318
  60.4 0.0 collective-permute-start.3
  60.4 2.3 %shard_map.79 = (f32[256,1024]{1,0:T(8,128)S(1)}, bf16[1024,1024]{1,0:T(8,128)(2,1)S(1)}) custom-call(s32[1]{0:T(128)} %bitcast.column_ref, bf16[8,256,128]{2,1,0:T(8,128)(2,1)S(1)} %all_to_all.15.read_ref, bf16[2048,1024]{1,0:T(8,128)(2,1)} %weight_ref.1), custom_call_target="tpu_custom_call" | custom-call | tf_op jit(solution)/shard_map/pallas_call | solution.py:274
  62.7 0.0 collective-permute-done.3.refs_0_
  62.7 1.6 %shard_map.80 = bf16[256,1024]{1,0:T(8,128)(2,1)} custom-call(f32[256,1024]{1,0:T(8,128)S(1)} %get-tuple-element.7.sum_ref, bf16[8,256,128]{2,1,0:T(8,128)(2,1)S(1)} %collective-permute-done.3.refs_0_, bf16[1024,1024]{1,0:T(8,128)(2,1)S(1)} %get-tuple-element.8.refs_1_), custom_call_target="tpu_custom_call" | custom-call | tf_op jit(solution)/shard_map/pallas_call | solution.py:274
  (1 shorter events, 0.0 us)
Async XLA Ops:
  3.1 21.7 %all-to-all-start = ((bf16[8,2,256,128]{3,2,1,0:T(8,128)(2,1)}), bf16[8,2,256,128]{3,2,1,0:T(8,128)(2,1)S(1)}, u32[]{:S(2)}, u32[]{:S(2)}) async-start(bf16[8,2,256,128]{3,2,1,0:T(8,128)(2,1)} %shard_map.73), calls=%async_computation | async-start | bytes 2097152 | tf_op jit(solution)/shard_map/all_to_all | solution.py:318
  11.4 20.7 %collective-permute-start.2 = (bf16[4,256,128]{2,1,0:T(8,128)(2,1)S(1)}, bf16[4,256,128]{2,1,0:T(8,128)(2,1)S(1)}, u32[]{:S(2)}, u32[]{:S(2)}) collective-permute-start(bf16[4,256,128]{2,1,0:T(8,128)(2,1)S(1)} %bitcast.12), channel_id=1, source_target_pairs={{8,0},{10,2},{12,4},{14,6},{0,8},{2,10},{4,12},{6,14},{24,16},{26,... | collective-permute-start | bytes 786440 | tf_op jit(solution)/shard_map/ppermute | solution.py:341
  26.8 13.1 %copy-start = (f32[8]{0:T(128)S(1)}, f32[8]{0:T(128)}, u32[]{:S(2)}) copy-start(f32[8]{0:T(128)} %rate_ref.1) | copy-start | bytes 100
  26.8 10.0 %collective-permute-start = (s16[784,128]{1,0:T(8,128)(2,1)S(1)}, s16[784,128]{1,0:T(8,128)(2,1)S(1)}, u32[]{:S(2)}, u32[]{:S(2)}) collective-permute-start(s16[784,128]{1,0:T(8,128)(2,1)S(1)} %shard_map.74.refs_0_), channel_id=1, source_target_pairs={{0,16},{2,18},{4,20},{6,22},{8,24},{10,26},{12,28},{14,30},{16,0},... | collective-permute-start | bytes 602120 | tf_op jit(solution)/shard_map/ppermute | solution.py:365
  30.0 10.0 %collective-permute-start.1 = (s16[784,128]{1,0:T(8,128)(2,1)S(1)}, s16[784,128]{1,0:T(8,128)(2,1)S(1)}, u32[]{:S(2)}, u32[]{:S(2)}) collective-permute-start(s16[784,128]{1,0:T(8,128)(2,1)S(1)} %shard_map.75.refs_2_), channel_id=1, source_target_pairs={{0,16},{2,18},{4,20},{6,22},{8,24},{10,26},{12,28},{14,30},{16,0},... | collective-permute-start | bytes 602120 | tf_op jit(solution)/shard_map/ppermute | solution.py:365
  32.9 11.1 %all-to-all-start.1 = ((bf16[4,2,256,128]{3,2,1,0:T(8,128)(2,1)}), bf16[4,2,256,128]{3,2,1,0:T(8,128)(2,1)S(1)}, u32[]{:S(2)}, u32[]{:S(2)}) async-start(bf16[4,2,256,128]{3,2,1,0:T(8,128)(2,1)} %shard_map.77), calls=%async_computation.1 | async-start | bytes 1048576 | tf_op jit(solution)/shard_map/all_to_all | solution.py:363
  60.4 2.3 %collective-permute-start.3 = (bf16[8,256,128]{2,1,0:T(8,128)(2,1)S(1)}, bf16[8,256,128]{2,1,0:T(8,128)(2,1)S(1)}, u32[]{:S(2)}, u32[]{:S(2)}) collective-permute-start(bf16[8,256,128]{2,1,0:T(8,128)(2,1)S(1)} %all_to_all.15.read_ref), channel_id=1, source_target_pairs={{0,1},{1,0},{2,3},{3,2},{4,5},{5,4},{6,7},{7,6},{8,9},{9,8},{10,11... | collective-permute-start | bytes 1572872 | tf_op jit(solution)/shard_map/ppermute | solution.py:386

commit v6 on v5

--- a/solution.py
+++ b/solution.py
@@ -221,22 +221,27 @@
     gate_up = jnp.concatenate([new_ref[0], new_ref[2]], axis=1)
     down = new_ref[1]
 
-    def step(i, _):
-        rows = pl.ds(i * chunk, chunk)
-        pre = dot(query_ref[rows].reshape(chunk * sides * sub, dh), gate_up)
+    for i in range(0, half, chunk):
+        pre = dot(query_ref[pl.ds(i, chunk)].reshape(chunk * sides * sub, dh), gate_up)
         gate, up = pre[:, :ff], pre[:, ff:]
         hidden = (gate * sigmoid(gate) * up).astype(BF16)
         read = dot(hidden, down, NT).astype(BF16).reshape(chunk, sides, sub, dh)
-        for p in range(sides):
-            at = (side_ref[0] if p == 0 else 1 - side_ref[0]) * half + i * chunk
-            read_ref[pl.ds(at, chunk)] = read[:, p]
-        return 0
-
-    lax.fori_loop(0, half // chunk, step, 0)
+        for c in range(chunk):
+            read_ref[spot(side_ref[0], i + c, half)] = read[c, 0]
+            if sides == 2:
+                read_ref[spot(1 - side_ref[0], i + c, half)] = read[c, 1]
+
+
+def spot(side, i, half):
+    if half % 2 == 0:
+        return (half // 2 - 1 - i // 2) * 4 + side * 2 + 1 - i % 2
+    return side * half + half - 1 - i
 
 
 def flat_heads(read_ref):
-    return jnp.concatenate([read_ref[i] for i in range(read_ref.shape[0])], axis=1)
+    heads = read_ref.shape[0]
+    half = max(1, heads // 2)
+    return jnp.concatenate([read_ref[spot(i // half, i % half, half)] for i in range(heads)], axis=1)
 
 
 def project_own_kernel(column_ref, read_ref, weight_ref, sum_ref, *refs):
@@ -314,9 +319,6 @@
     groups = [g[turned:] + g[:turned] for g in groups]
     slot = (slot + heads - turned) % heads
 
-    def shuffle(x):
-        return lax.all_to_all(x, both, 0, 0, tiled=True, axis_index_groups=groups)
-
     pairs = call(
         pack_kernel,
         struct((heads, 2, tokens, dh), BF16),
@@ -331,7 +333,7 @@
             pltpu.SemaphoreType.DMA,
         ],
     )
-    received = shuffle(pairs)
+    received = lax.all_to_all(pairs, both, 0, 0, tiled=True, axis_index_groups=groups)
     packed = queries.reshape(tokens, heads, dh).transpose(1, 0, 2)
     half = max(1, heads // 2)
     side = slot // half
@@ -381,7 +383,10 @@
         limit=16,
     )
 
-    reads = shuffle(read)
+    places = sorted(range(heads), key=lambda i: spot(i // half, i % half, half))
+    reads = lax.all_to_all(
+        read, both, 0, 0, tiled=True, axis_index_groups=[[g[i] for i in places] for g in groups]
+    )
     pieces = [
         lax.ppermute(reads, "head", [(i, (i + s) % head_size) for i in range(head_size)])
         for s in range(1, head_size)

time: 64.8 us -> 61.9 us (0.955)
  blocking collectives: 14.1 us -> 11.4 us
    all_to_all x1, blocking collectives: 14.1 us -> 11.4 us  [on_device(): lax.all_to_all(read, both, 0, 0, tiled=True, axis_index_groups=[[g[i] for...]
  transfers between devices with their start and end apart: 6 -> 6, of which waited for: 2 -> 2; matrix products, arithmetic and copies ran while one was open for 4% -> 5% of each run, Pallas kernels for 17% -> 18%
where the time goes in v6:
time: 61.9 us; the launch traced here: 61.3 us
  Pallas kernels  17.2 us (28%)
  waiting for transfers between devices  15.3 us (25%)
  starting transfers between devices  13.8 us (22%)
  blocking collectives  11.4 us (18%)
  local copies, waits for them, and re-layouts  2.84 us (5%)
  between operations  0.79 us (1%)
    pallas_call x8, Pallas kernels, call(): pl.pallas_call(kernel, out_shape=out_shape, in_specs=specs, out_specs=jax...  17.2 us
    all_to_all x1, waiting for transfers between devices, on_device(): lax.all_to_all(pairs, both, 0, 0, tiled=True, axis_index_groups=groups)  12.2 us
    all_to_all x1, blocking collectives, on_device(): lax.all_to_all(read, both, 0, 0, tiled=True, axis_index_groups=[[g[i] for...  11.4 us
    all_to_all x1, starting transfers between devices, on_device(): lax.all_to_all(pairs, both, 0, 0, tiled=True, axis_index_groups=groups)  6.76 us
    all_to_all x1, starting transfers between devices, on_device(): lax.all_to_all(asked, both, 0, 0, tiled=True, axis_index_groups=halves_of)  3.9 us
    ppermute x2, waiting for transfers between devices, on_device(): lax.ppermute(code, both, turn)  3.11 us
    ppermute x2, starting transfers between devices, on_device(): lax.ppermute(code, both, turn)  3.06 us
    unnamed x5, local copies, waits for them, and re-layouts  1.61 us
  transfers between devices with their start and end apart: 6, of which 2 were waited for; matrix products, arithmetic and copies ran while one was open for 5% of the time, Pallas kernels for 18%

profile of v6, /device:TPU:0, one launch (start us, length us, event | category | flops | bytes accessed | tf_op | source)
XLA Modules:
  0.0 61.3 jit_solution(10125842098474074443)
XLA Ops:
  0.7 2.5 %shard_map.73 = bf16[8,2,256,128]{3,2,1,0:T(8,128)(2,1)} custom-call(s32[1,1]{1,0:T(1,128)} %bitcast.9.mask_ref, bf16[256,1024]{1,0:T(8,128)(2,1)} %keys_ref.1, bf16[256,1024]{1,0:T(8,128)(2,1)} %values_ref.1), custom_call_target="tpu_custom_call" | custom-call | tf_op jit(solution)/shard_map/pallas_call | solution.py:279
  3.1 6.8 %all-to-all-start = ((bf16[8,2,256,128]{3,2,1,0:T(8,128)(2,1)}), bf16[8,2,256,128]{3,2,1,0:T(8,128)(2,1)S(1)}, u32[]{:S(2)}, u32[]{:S(2)}) async-start(bf16[8,2,256,128]{3,2,1,0:T(8,128)(2,1)} %shard_map.73), calls=%async_computation | async-start | bytes 2097152 | tf_op jit(solution)/shard_map/all_to_all | solution.py:336
  9.9 1.2 %copy.8 = bf16[256,1024]{0,1:T(8,128)(2,1)S(1)} copy(bf16[256,1024]{1,0:T(8,128)(2,1)} %param.9) | data formatting | bytes 1048576 | tf_op args[2]
  11.2 0.2 copy.12
  11.4 0.1 collective-permute-start.2
  11.4 1.2 %dynamic-slice_bitcast_fusion.weights_ref.refs_4_ = f32[3,128,512]{2,1,0:T(8,128)S(1)} fusion(f32[3,8,128,512]{3,2,1,0:T(8,128)} %param.10, s32[]{:T(128)S(6)} %select_n.46), kind=kLoop, calls=%fused_computation | loop fusion | bytes 1572868 | tf_op jit(solution)/shard_map/jit(dynamic_index_in_dim)/squeeze | solution.py:346
  12.6 12.2 %all-to-all-done.recv_ref = bf16[8,2,256,128]{3,2,1,0:T(8,128)(2,1)S(1)} async-done(((bf16[8,2,256,128]{3,2,1,0:T(8,128)(2,1)}), bf16[8,2,256,128]{3,2,1,0:T(8,128)(2,1)S(1)}, u32[]{:S(2)}, u32[]{:S(2)}) %all-to-all-start) | async-done | bytes 1048608 | tf_op jit(solution)/shard_map/all_to_all | solution.py:336
  24.8 2.0 %shard_map.74.refs_0_ = s16[784,128]{1,0:T(8,128)(2,1)S(1)} custom-call(bf16[8,2,256,128]{3,2,1,0:T(8,128)(2,1)S(1)} %all-to-all-done.recv_ref, f32[3,128,512]{2,1,0:T(8,128)S(1)} %dynamic-slice_bitcast_fusion.weights_ref.refs_4_), custom_call_target="tpu_custom_call" | custom-call | flops 4294967296 | bytes 1048576 | tf_op jit(solution)/shard_map/pallas_call | solution.py:279
  26.8 0.0 copy-start
  26.8 1.1 %collective-permute-start = (s16[784,128]{1,0:T(8,128)(2,1)S(1)}, s16[784,128]{1,0:T(8,128)(2,1)S(1)}, u32[]{:S(2)}, u32[]{:S(2)}) collective-permute-start(s16[784,128]{1,0:T(8,128)(2,1)S(1)} %shard_map.74.refs_0_), channel_id=1, source_target_pairs={{0,16},{2,18},{4,20},{6,22},{8,24},{10,26},{12,28},{14,30},{16,0},... | collective-permute-start | bytes 602120 | tf_op jit(solution)/shard_map/ppermute | solution.py:367
  28.0 2.0 %shard_map.75.refs_2_ = s16[784,128]{1,0:T(8,128)(2,1)S(1)} custom-call(bf16[8,2,256,128]{3,2,1,0:T(8,128)(2,1)S(1)} %all-to-all-done.recv_ref, f32[3,128,512]{2,1,0:T(8,128)S(1)} %dynamic-slice_bitcast_fusion.weights_ref.refs_4_), custom_call_target="tpu_custom_call" | custom-call | flops 4294967296 | bytes 1048576 | tf_op jit(solution)/shard_map/pallas_call | solution.py:279
  30.0 1.9 %collective-permute-start.1 = (s16[784,128]{1,0:T(8,128)(2,1)S(1)}, s16[784,128]{1,0:T(8,128)(2,1)S(1)}, u32[]{:S(2)}, u32[]{:S(2)}) collective-permute-start(s16[784,128]{1,0:T(8,128)(2,1)S(1)} %shard_map.75.refs_2_), channel_id=1, source_target_pairs={{0,16},{2,18},{4,20},{6,22},{8,24},{10,26},{12,28},{14,30},{16,0},... | collective-permute-start | bytes 602120 | tf_op jit(solution)/shard_map/ppermute | solution.py:367
  31.9 0.2 copy.11
  32.1 0.0 collective-permute-done.2.theirs_ref
  32.1 0.8 %shard_map.77 = bf16[4,2,256,128]{3,2,1,0:T(8,128)(2,1)} custom-call(bf16[4,256,128]{2,1,0:T(8,128)(2,1)S(1)} %bitcast.10, bf16[4,256,128]{2,1,0:T(8,128)(2,1)S(1)} %collective-permute-done.2.theirs_ref), custom_call_target="tpu_custom_call" | custom-call | tf_op jit(solution)/shard_map/pallas_call | solution.py:279
  32.9 3.9 %all-to-all-start.1 = ((bf16[4,2,256,128]{3,2,1,0:T(8,128)(2,1)}), bf16[4,2,256,128]{3,2,1,0:T(8,128)(2,1)S(1)}, u32[]{:S(2)}, u32[]{:S(2)}) async-start(bf16[4,2,256,128]{3,2,1,0:T(8,128)(2,1)} %shard_map.77), calls=%async_computation.1 | async-start | bytes 1048576 | tf_op jit(solution)/shard_map/all_to_all | solution.py:365
  36.8 0.0 collective-permute-done.refs_1_
  36.8 3.1 %collective-permute-done.1.refs_3_ = s16[784,128]{1,0:T(8,128)(2,1)S(1)} collective-permute-done((s16[784,128]{1,0:T(8,128)(2,1)S(1)}, s16[784,128]{1,0:T(8,128)(2,1)S(1)}, u32[]{:S(2)}, u32[]{:S(2)}) %collective-permute-start.1) | collective-permute-done | bytes 200736 | tf_op jit(solution)/shard_map/ppermute | solution.py:367
  39.9 0.0 copy-done
  39.9 4.1 %shard_map.76.new_ref = bf16[3,128,512]{2,1,0:T(8,128)(2,1)S(1)} custom-call(s32[1]{0:T(128)} %bitcast.2.slot_ref, f32[8]{0:T(128)S(1)} %copy-done, s16[784,128]{1,0:T(8,128)(2,1)S(1)} %shard_map.74.refs_0_, s16[784,128]{1,0:T(8,128)(2,1)S(1)} %collective-permute-done.refs_1_, s16[784,128]{1,0:T(8,128)(2,1)S(1)} %shard_map.75.refs_2_, ...), custom_call_target="tpu_custom_call" | custom-call | flops 8589934592 | bytes 1048576 | tf_op jit(solution)/shard_map/pallas_call | solution.py:279
  44.0 0.0 all-to-all-done.1.query_ref
  44.0 1.9 %shard_map.78 = bf16[8,256,128]{2,1,0:T(8,128)(2,1)S(1)} custom-call(s32[1]{0:T(128)} %bitcast.1.side_ref, bf16[3,128,512]{2,1,0:T(8,128)(2,1)S(1)} %shard_map.76.new_ref, bf16[4,2,256,128]{3,2,1,0:T(8,128)(2,1)S(1)} %all-to-all-done.1.query_ref), custom_call_target="tpu_custom_call" | custom-call | tf_op jit(solution)/shard_map/pallas_call | solution.py:279
  45.9 11.4 %all_to_all.15.read_ref = bf16[8,256,128]{2,1,0:T(8,128)(2,1)S(1)} all-to-all(bf16[8,256,128]{2,1,0:T(8,128)(2,1)S(1)} %shard_map.78), channel_id=1, replica_groups={{14,12,6,4,10,8,2,0},{30,28,22,20,26,24,18,16},{23,21,7,5,19,17,3,1},{3..., dimensions={0} | all-to-all | bytes 1048576 | tf_op jit(solution)/shard_map/all_to_all | solution.py:387
  57.4 0.0 collective-permute-start.3
  57.4 2.3 %shard_map.79 = (f32[256,1024]{1,0:T(8,128)S(1)}, bf16[1024,1024]{1,0:T(8,128)(2,1)S(1)}) custom-call(s32[1]{0:T(128)} %bitcast.column_ref, bf16[8,256,128]{2,1,0:T(8,128)(2,1)S(1)} %all_to_all.15.read_ref, bf16[2048,1024]{1,0:T(8,128)(2,1)} %weight_ref.1), custom_call_target="tpu_custom_call" | custom-call | tf_op jit(solution)/shard_map/pallas_call | solution.py:279
  59.7 0.0 collective-permute-done.3.refs_0_
  59.7 1.6 %shard_map.80 = bf16[256,1024]{1,0:T(8,128)(2,1)} custom-call(f32[256,1024]{1,0:T(8,128)S(1)} %get-tuple-element.7.sum_ref, bf16[8,256,128]{2,1,0:T(8,128)(2,1)S(1)} %collective-permute-done.3.refs_0_, bf16[1024,1024]{1,0:T(8,128)(2,1)S(1)} %get-tuple-element.8.refs_1_), custom_call_target="tpu_custom_call" | custom-call | tf_op jit(solution)/shard_map/pallas_call | solution.py:279
  (1 shorter events, 0.0 us)
Async XLA Ops:
  3.1 21.7 %all-to-all-start = ((bf16[8,2,256,128]{3,2,1,0:T(8,128)(2,1)}), bf16[8,2,256,128]{3,2,1,0:T(8,128)(2,1)S(1)}, u32[]{:S(2)}, u32[]{:S(2)}) async-start(bf16[8,2,256,128]{3,2,1,0:T(8,128)(2,1)} %shard_map.73), calls=%async_computation | async-start | bytes 2097152 | tf_op jit(solution)/shard_map/all_to_all | solution.py:336
  11.4 20.7 %collective-permute-start.2 = (bf16[4,256,128]{2,1,0:T(8,128)(2,1)S(1)}, bf16[4,256,128]{2,1,0:T(8,128)(2,1)S(1)}, u32[]{:S(2)}, u32[]{:S(2)}) collective-permute-start(bf16[4,256,128]{2,1,0:T(8,128)(2,1)S(1)} %bitcast.12), channel_id=1, source_target_pairs={{8,0},{10,2},{12,4},{14,6},{0,8},{2,10},{4,12},{6,14},{24,16},{26,... | collective-permute-start | bytes 786440 | tf_op jit(solution)/shard_map/ppermute | solution.py:343
  26.8 13.1 %copy-start = (f32[8]{0:T(128)S(1)}, f32[8]{0:T(128)}, u32[]{:S(2)}) copy-start(f32[8]{0:T(128)} %rate_ref.1) | copy-start | bytes 100
  26.8 10.0 %collective-permute-start = (s16[784,128]{1,0:T(8,128)(2,1)S(1)}, s16[784,128]{1,0:T(8,128)(2,1)S(1)}, u32[]{:S(2)}, u32[]{:S(2)}) collective-permute-start(s16[784,128]{1,0:T(8,128)(2,1)S(1)} %shard_map.74.refs_0_), channel_id=1, source_target_pairs={{0,16},{2,18},{4,20},{6,22},{8,24},{10,26},{12,28},{14,30},{16,0},... | collective-permute-start | bytes 602120 | tf_op jit(solution)/shard_map/ppermute | solution.py:367
  30.0 10.0 %collective-permute-start.1 = (s16[784,128]{1,0:T(8,128)(2,1)S(1)}, s16[784,128]{1,0:T(8,128)(2,1)S(1)}, u32[]{:S(2)}, u32[]{:S(2)}) collective-permute-start(s16[784,128]{1,0:T(8,128)(2,1)S(1)} %shard_map.75.refs_2_), channel_id=1, source_target_pairs={{0,16},{2,18},{4,20},{6,22},{8,24},{10,26},{12,28},{14,30},{16,0},... | collective-permute-start | bytes 602120 | tf_op jit(solution)/shard_map/ppermute | solution.py:367
  32.9 11.1 %all-to-all-start.1 = ((bf16[4,2,256,128]{3,2,1,0:T(8,128)(2,1)}), bf16[4,2,256,128]{3,2,1,0:T(8,128)(2,1)S(1)}, u32[]{:S(2)}, u32[]{:S(2)}) async-start(bf16[4,2,256,128]{3,2,1,0:T(8,128)(2,1)} %shard_map.77), calls=%async_computation.1 | async-start | bytes 1048576 | tf_op jit(solution)/shard_map/all_to_all | solution.py:365
  57.4 2.3 %collective-permute-start.3 = (bf16[8,256,128]{2,1,0:T(8,128)(2,1)S(1)}, bf16[8,256,128]{2,1,0:T(8,128)(2,1)S(1)}, u32[]{:S(2)}, u32[]{:S(2)}) collective-permute-start(bf16[8,256,128]{2,1,0:T(8,128)(2,1)S(1)} %all_to_all.15.read_ref), channel_id=1, source_target_pairs={{0,1},{1,0},{2,3},{3,2},{4,5},{5,4},{6,7},{7,6},{8,9},{9,8},{10,11... | collective-permute-start | bytes 1572872 | tf_op jit(solution)/shard_map/ppermute | solution.py:391

commit v7 on v6

--- a/solution.py
+++ b/solution.py
@@ -33,36 +33,44 @@
     return 0.5 + 0.5 * jnp.tanh(0.5 * x)
 
 
-def pack_kernel(mask_ref, keys_ref, values_ref, pairs_ref, kept_ref, mask_kept, in_sem, out_sem, mask_sem):
+def pack_kernel(mask_ref, keys_ref, values_ref, pairs_ref, wide_ref, kept_ref, mask_kept, in_sem, out_sem, mask_sem):
     heads, _, tokens, dh = pairs_ref.shape
     blocks = mask_ref.shape[1]
-    length = tokens // blocks
+    shares = in_sem.shape[1]
+    length = tokens // shares
     sources = (keys_ref, values_ref)
     mask_copy = pltpu.make_async_copy(mask_ref, mask_kept, mask_sem)
     mask_copy.start()
     loads, stores = [], []
-    for i in range(heads):
+    for r in range(shares):
+        rows = pl.ds(r * length, length)
         for p in range(2):
             loads.append(
+                pltpu.make_async_copy(sources[p].at[rows], wide_ref.at[p, rows], in_sem.at[p, r])
+            )
+            loads[-1].start()
+    mask_copy.wait()
+    for r in range(shares):
+        rows = pl.ds(r * length, length)
+        for p in range(2):
+            loads[2 * r + p].wait()
+            for i in range(heads):
+                columns = pl.ds(i * dh, dh)
+                if p == 0:
+                    kept_ref[i, p, rows] = wide_ref[p, rows, columns]
+                    continue
+                size = min(length, tokens // blocks)
+                for start in range(r * length, (r + 1) * length, size):
+                    some = pl.ds(start, size)
+                    b = start // (tokens // blocks)
+                    kept = wide_ref[p, some, columns].astype(F32) * mask_kept[:, b : b + 1].astype(F32)
+                    kept_ref[i, p, some] = kept.astype(BF16)
+            stores.append(
                 pltpu.make_async_copy(
-                    sources[p].at[:, pl.ds(i * dh, dh)], kept_ref.at[i, p], in_sem.at[i, p]
+                    kept_ref.at[:, p, rows], pairs_ref.at[:, p, rows], out_sem.at[p, r]
                 )
             )
-            stores.append(
-                pltpu.make_async_copy(kept_ref.at[i, p], pairs_ref.at[i, p], out_sem.at[i, p])
-            )
-    for load in loads:
-        load.start()
-    mask_copy.wait()
-    for i in range(heads):
-        for p in range(2):
-            loads[2 * i + p].wait()
-            if p == 1:
-                for b in range(blocks):
-                    rows = pl.ds(b * length, length)
-                    kept = kept_ref[i, 1, rows].astype(F32) * mask_kept[:, b : b + 1].astype(F32)
-                    kept_ref[i, 1, rows] = kept.astype(BF16)
-            stores[2 * i + p].start()
+            stores[-1].start()
     for store in stores:
         store.wait()
 
@@ -260,11 +268,24 @@
 
 
 def project_rest_kernel(sum_ref, *refs):
-    reads, weights, out_ref = refs[: len(refs) // 2], refs[len(refs) // 2 : -1], refs[-1]
-    value = sum_ref[...]
-    for read, weight in zip(reads, weights):
-        value = value + dot(flat_heads(read), weight[...])
-    out_ref[...] = (value * sigmoid(value)).astype(BF16)
+    refs, (out_ref, held_ref, sems) = refs[:-3], refs[-3:]
+    reads, weights = refs[: len(refs) // 2], refs[len(refs) // 2 :]
+    flats = [flat_heads(read) for read in reads]
+    shares = sems.shape[0]
+    width = held_ref.shape[1] // shares
+    copies = []
+    for i in range(shares):
+        columns = pl.ds(i * width, width)
+        value = sum_ref[:, columns]
+        for flat, weight in zip(flats, weights):
+            value = value + dot(flat, weight[:, columns])
+        held_ref[:, columns] = (value * sigmoid(value)).astype(BF16)
+        copies.append(
+            pltpu.make_async_copy(held_ref.at[:, columns], out_ref.at[:, columns], sems.at[i])
+        )
+        copies[-1].start()
+    for copy in copies:
+        copy.wait()
 
 
 def call(kernel, out_shape, args, scalars=0, flops=None, limit=12, hbm=(), scratch=()):
@@ -326,10 +347,11 @@
         hbm=(-1, 0, 1, 2),
         limit=60,
         scratch=[
+            pltpu.VMEM((2, tokens, heads * dh), BF16),
             pltpu.VMEM((heads, 2, tokens, dh), BF16),
             pltpu.VMEM((1, *edit_mask.shape), edit_mask.dtype),
-            pltpu.SemaphoreType.DMA((heads, 2)),
-            pltpu.SemaphoreType.DMA((heads, 2)),
+            pltpu.SemaphoreType.DMA((2, 2)),
+            pltpu.SemaphoreType.DMA((2, 2)),
             pltpu.SemaphoreType.DMA,
         ],
     )
@@ -405,8 +427,13 @@
         limit=49,
         scratch=[pltpu.VMEM((depth, columns), BF16), pltpu.SemaphoreType.DMA((head_size,))],
     )
+    shares = max(c for c in (1, 2, 4) if columns % (c * LANES) == 0)
     return call(
-        project_rest_kernel, struct((tokens, columns), BF16), (own, *pieces, *rest)
+        project_rest_kernel,
+        struct((tokens, columns), BF16),
+        (own, *pieces, *rest),
+        hbm=(-1,),
+        scratch=[pltpu.VMEM((tokens, columns), BF16), pltpu.SemaphoreType.DMA((shares,))],
     )
 
 

time: 61.9 us -> 61.5 us (level)
  no operation moved by 1% of the time
where the time goes in v7:
time: 61.5 us; the launch traced here: 60.9 us
  Pallas kernels  16.8 us (27%)
  waiting for transfers between devices  15.3 us (25%)
  starting transfers between devices  13.8 us (22%)
  blocking collectives  11.4 us (19%)
  local copies, waits for them, and re-layouts  2.84 us (5%)
  between operations  0.79 us (1%)
    pallas_call x8, Pallas kernels, call(): pl.pallas_call(kernel, out_shape=out_shape, in_specs=specs, out_specs=jax...  16.8 us
    all_to_all x1, waiting for transfers between devices, on_device(): lax.all_to_all(pairs, both, 0, 0, tiled=True, axis_index_groups=groups)  12.2 us
    all_to_all x1, blocking collectives, on_device(): lax.all_to_all(read, both, 0, 0, tiled=True, axis_index_groups=[[g[i] for...  11.4 us
    all_to_all x1, starting transfers between devices, on_device(): lax.all_to_all(pairs, both, 0, 0, tiled=True, axis_index_groups=groups)  6.76 us
    all_to_all x1, starting transfers between devices, on_device(): lax.all_to_all(asked, both, 0, 0, tiled=True, axis_index_groups=halves_of)  3.9 us
    ppermute x2, waiting for transfers between devices, on_device(): lax.ppermute(code, both, turn)  3.11 us
    ppermute x2, starting transfers between devices, on_device(): lax.ppermute(code, both, turn)  3.06 us
    unnamed x5, local copies, waits for them, and re-layouts  1.61 us
  transfers between devices with their start and end apart: 6, of which 2 were waited for; matrix products, arithmetic and copies ran while one was open for 5% of the time, Pallas kernels for 18%

profile of v7, /device:TPU:0, one launch (start us, length us, event | category | flops | bytes accessed | tf_op | source)
XLA Modules:
  0.0 60.9 jit_solution(5105204261747420445)
XLA Ops:
  0.7 2.1 %shard_map.73 = bf16[8,2,256,128]{3,2,1,0:T(8,128)(2,1)} custom-call(s32[1,1]{1,0:T(1,128)} %bitcast.9.mask_ref, bf16[256,1024]{1,0:T(8,128)(2,1)} %keys_ref.1, bf16[256,1024]{1,0:T(8,128)(2,1)} %values_ref.1), custom_call_target="tpu_custom_call" | custom-call | tf_op jit(solution)/shard_map/pallas_call | solution.py:300
  2.8 6.8 %all-to-all-start = ((bf16[8,2,256,128]{3,2,1,0:T(8,128)(2,1)}), bf16[8,2,256,128]{3,2,1,0:T(8,128)(2,1)S(1)}, u32[]{:S(2)}, u32[]{:S(2)}) async-start(bf16[8,2,256,128]{3,2,1,0:T(8,128)(2,1)} %shard_map.73), calls=%async_computation | async-start | bytes 2097152 | tf_op jit(solution)/shard_map/all_to_all | solution.py:358
  9.5 1.2 %copy.8 = bf16[256,1024]{0,1:T(8,128)(2,1)S(1)} copy(bf16[256,1024]{1,0:T(8,128)(2,1)} %param.9) | data formatting | bytes 1048576 | tf_op args[2]
  10.8 0.2 copy.12
  11.0 0.1 collective-permute-start.2
  11.1 1.2 %dynamic-slice_bitcast_fusion.weights_ref.refs_4_ = f32[3,128,512]{2,1,0:T(8,128)S(1)} fusion(f32[3,8,128,512]{3,2,1,0:T(8,128)} %param.10, s32[]{:T(128)S(6)} %select_n.46), kind=kLoop, calls=%fused_computation | loop fusion | bytes 1572868 | tf_op jit(solution)/shard_map/jit(dynamic_index_in_dim)/squeeze | solution.py:368
  12.3 12.2 %all-to-all-done.recv_ref = bf16[8,2,256,128]{3,2,1,0:T(8,128)(2,1)S(1)} async-done(((bf16[8,2,256,128]{3,2,1,0:T(8,128)(2,1)}), bf16[8,2,256,128]{3,2,1,0:T(8,128)(2,1)S(1)}, u32[]{:S(2)}, u32[]{:S(2)}) %all-to-all-start) | async-done | bytes 1048608 | tf_op jit(solution)/shard_map/all_to_all | solution.py:358
  24.5 2.0 %shard_map.74.refs_0_ = s16[784,128]{1,0:T(8,128)(2,1)S(1)} custom-call(bf16[8,2,256,128]{3,2,1,0:T(8,128)(2,1)S(1)} %all-to-all-done.recv_ref, f32[3,128,512]{2,1,0:T(8,128)S(1)} %dynamic-slice_bitcast_fusion.weights_ref.refs_4_), custom_call_target="tpu_custom_call" | custom-call | flops 4294967296 | bytes 1048576 | tf_op jit(solution)/shard_map/pallas_call | solution.py:300
  26.5 0.0 copy-start
  26.5 1.1 %collective-permute-start = (s16[784,128]{1,0:T(8,128)(2,1)S(1)}, s16[784,128]{1,0:T(8,128)(2,1)S(1)}, u32[]{:S(2)}, u32[]{:S(2)}) collective-permute-start(s16[784,128]{1,0:T(8,128)(2,1)S(1)} %shard_map.74.refs_0_), channel_id=1, source_target_pairs={{0,16},{2,18},{4,20},{6,22},{8,24},{10,26},{12,28},{14,30},{16,0},... | collective-permute-start | bytes 602120 | tf_op jit(solution)/shard_map/ppermute | solution.py:389
  27.7 2.0 %shard_map.75.refs_2_ = s16[784,128]{1,0:T(8,128)(2,1)S(1)} custom-call(bf16[8,2,256,128]{3,2,1,0:T(8,128)(2,1)S(1)} %all-to-all-done.recv_ref, f32[3,128,512]{2,1,0:T(8,128)S(1)} %dynamic-slice_bitcast_fusion.weights_ref.refs_4_), custom_call_target="tpu_custom_call" | custom-call | flops 4294967296 | bytes 1048576 | tf_op jit(solution)/shard_map/pallas_call | solution.py:300
  29.6 1.9 %collective-permute-start.1 = (s16[784,128]{1,0:T(8,128)(2,1)S(1)}, s16[784,128]{1,0:T(8,128)(2,1)S(1)}, u32[]{:S(2)}, u32[]{:S(2)}) collective-permute-start(s16[784,128]{1,0:T(8,128)(2,1)S(1)} %shard_map.75.refs_2_), channel_id=1, source_target_pairs={{0,16},{2,18},{4,20},{6,22},{8,24},{10,26},{12,28},{14,30},{16,0},... | collective-permute-start | bytes 602120 | tf_op jit(solution)/shard_map/ppermute | solution.py:389
  31.6 0.2 copy.11
  31.7 0.0 collective-permute-done.2.theirs_ref
  31.8 0.8 %shard_map.77 = bf16[4,2,256,128]{3,2,1,0:T(8,128)(2,1)} custom-call(bf16[4,256,128]{2,1,0:T(8,128)(2,1)S(1)} %bitcast.10, bf16[4,256,128]{2,1,0:T(8,128)(2,1)S(1)} %collective-permute-done.2.theirs_ref), custom_call_target="tpu_custom_call" | custom-call | tf_op jit(solution)/shard_map/pallas_call | solution.py:300
  32.6 3.9 %all-to-all-start.1 = ((bf16[4,2,256,128]{3,2,1,0:T(8,128)(2,1)}), bf16[4,2,256,128]{3,2,1,0:T(8,128)(2,1)S(1)}, u32[]{:S(2)}, u32[]{:S(2)}) async-start(bf16[4,2,256,128]{3,2,1,0:T(8,128)(2,1)} %shard_map.77), calls=%async_computation.1 | async-start | bytes 1048576 | tf_op jit(solution)/shard_map/all_to_all | solution.py:387
  36.5 0.0 collective-permute-done.refs_1_
  36.5 3.1 %collective-permute-done.1.refs_3_ = s16[784,128]{1,0:T(8,128)(2,1)S(1)} collective-permute-done((s16[784,128]{1,0:T(8,128)(2,1)S(1)}, s16[784,128]{1,0:T(8,128)(2,1)S(1)}, u32[]{:S(2)}, u32[]{:S(2)}) %collective-permute-start.1) | collective-permute-done | bytes 200736 | tf_op jit(solution)/shard_map/ppermute | solution.py:389
  39.6 0.0 copy-done
  39.6 4.1 %shard_map.76.new_ref = bf16[3,128,512]{2,1,0:T(8,128)(2,1)S(1)} custom-call(s32[1]{0:T(128)} %bitcast.2.slot_ref, f32[8]{0:T(128)S(1)} %copy-done, s16[784,128]{1,0:T(8,128)(2,1)S(1)} %shard_map.74.refs_0_, s16[784,128]{1,0:T(8,128)(2,1)S(1)} %collective-permute-done.refs_1_, s16[784,128]{1,0:T(8,128)(2,1)S(1)} %shard_map.75.refs_2_, ...), custom_call_target="tpu_custom_call" | custom-call | flops 8589934592 | bytes 1048576 | tf_op jit(solution)/shard_map/pallas_call | solution.py:300
  43.7 0.0 all-to-all-done.1.query_ref
  43.7 1.9 %shard_map.78 = bf16[8,256,128]{2,1,0:T(8,128)(2,1)S(1)} custom-call(s32[1]{0:T(128)} %bitcast.1.side_ref, bf16[3,128,512]{2,1,0:T(8,128)(2,1)S(1)} %shard_map.76.new_ref, bf16[4,2,256,128]{3,2,1,0:T(8,128)(2,1)S(1)} %all-to-all-done.1.query_ref), custom_call_target="tpu_custom_call" | custom-call | tf_op jit(solution)/shard_map/pallas_call | solution.py:300
  45.6 11.4 %all_to_all.15.read_ref = bf16[8,256,128]{2,1,0:T(8,128)(2,1)S(1)} all-to-all(bf16[8,256,128]{2,1,0:T(8,128)(2,1)S(1)} %shard_map.78), channel_id=1, replica_groups={{14,12,6,4,10,8,2,0},{30,28,22,20,26,24,18,16},{23,21,7,5,19,17,3,1},{3..., dimensions={0} | all-to-all | bytes 1048576 | tf_op jit(solution)/shard_map/all_to_all | solution.py:409
  57.0 0.0 collective-permute-start.3
  57.0 2.3 %shard_map.79 = (f32[256,1024]{1,0:T(8,128)S(1)}, bf16[1024,1024]{1,0:T(8,128)(2,1)S(1)}) custom-call(s32[1]{0:T(128)} %bitcast.column_ref, bf16[8,256,128]{2,1,0:T(8,128)(2,1)S(1)} %all_to_all.15.read_ref, bf16[2048,1024]{1,0:T(8,128)(2,1)} %weight_ref.1), custom_call_target="tpu_custom_call" | custom-call | tf_op jit(solution)/shard_map/pallas_call | solution.py:300
  59.4 0.0 collective-permute-done.3.refs_0_
  59.4 1.5 %shard_map.80 = bf16[256,1024]{1,0:T(8,128)(2,1)} custom-call(f32[256,1024]{1,0:T(8,128)S(1)} %get-tuple-element.7.sum_ref, bf16[8,256,128]{2,1,0:T(8,128)(2,1)S(1)} %collective-permute-done.3.refs_0_, bf16[1024,1024]{1,0:T(8,128)(2,1)S(1)} %get-tuple-element.8.refs_1_), custom_call_target="tpu_custom_call" | custom-call | tf_op jit(solution)/shard_map/pallas_call | solution.py:300
  (1 shorter events, 0.0 us)
Async XLA Ops:
  2.8 21.7 %all-to-all-start = ((bf16[8,2,256,128]{3,2,1,0:T(8,128)(2,1)}), bf16[8,2,256,128]{3,2,1,0:T(8,128)(2,1)S(1)}, u32[]{:S(2)}, u32[]{:S(2)}) async-start(bf16[8,2,256,128]{3,2,1,0:T(8,128)(2,1)} %shard_map.73), calls=%async_computation | async-start | bytes 2097152 | tf_op jit(solution)/shard_map/all_to_all | solution.py:358
  11.0 20.7 %collective-permute-start.2 = (bf16[4,256,128]{2,1,0:T(8,128)(2,1)S(1)}, bf16[4,256,128]{2,1,0:T(8,128)(2,1)S(1)}, u32[]{:S(2)}, u32[]{:S(2)}) collective-permute-start(bf16[4,256,128]{2,1,0:T(8,128)(2,1)S(1)} %bitcast.12), channel_id=1, source_target_pairs={{8,0},{10,2},{12,4},{14,6},{0,8},{2,10},{4,12},{6,14},{24,16},{26,... | collective-permute-start | bytes 786440 | tf_op jit(solution)/shard_map/ppermute | solution.py:365
  26.5 13.1 %copy-start = (f32[8]{0:T(128)S(1)}, f32[8]{0:T(128)}, u32[]{:S(2)}) copy-start(f32[8]{0:T(128)} %rate_ref.1) | copy-start | bytes 100
  26.5 10.0 %collective-permute-start = (s16[784,128]{1,0:T(8,128)(2,1)S(1)}, s16[784,128]{1,0:T(8,128)(2,1)S(1)}, u32[]{:S(2)}, u32[]{:S(2)}) collective-permute-start(s16[784,128]{1,0:T(8,128)(2,1)S(1)} %shard_map.74.refs_0_), channel_id=1, source_target_pairs={{0,16},{2,18},{4,20},{6,22},{8,24},{10,26},{12,28},{14,30},{16,0},... | collective-permute-start | bytes 602120 | tf_op jit(solution)/shard_map/ppermute | solution.py:389
  29.6 10.0 %collective-permute-start.1 = (s16[784,128]{1,0:T(8,128)(2,1)S(1)}, s16[784,128]{1,0:T(8,128)(2,1)S(1)}, u32[]{:S(2)}, u32[]{:S(2)}) collective-permute-start(s16[784,128]{1,0:T(8,128)(2,1)S(1)} %shard_map.75.refs_2_), channel_id=1, source_target_pairs={{0,16},{2,18},{4,20},{6,22},{8,24},{10,26},{12,28},{14,30},{16,0},... | collective-permute-start | bytes 602120 | tf_op jit(solution)/shard_map/ppermute | solution.py:389
  32.6 11.1 %all-to-all-start.1 = ((bf16[4,2,256,128]{3,2,1,0:T(8,128)(2,1)}), bf16[4,2,256,128]{3,2,1,0:T(8,128)(2,1)S(1)}, u32[]{:S(2)}, u32[]{:S(2)}) async-start(bf16[4,2,256,128]{3,2,1,0:T(8,128)(2,1)} %shard_map.77), calls=%async_computation.1 | async-start | bytes 1048576 | tf_op jit(solution)/shard_map/all_to_all | solution.py:387
  57.0 2.3 %collective-permute-start.3 = (bf16[8,256,128]{2,1,0:T(8,128)(2,1)S(1)}, bf16[8,256,128]{2,1,0:T(8,128)(2,1)S(1)}, u32[]{:S(2)}, u32[]{:S(2)}) collective-permute-start(bf16[8,256,128]{2,1,0:T(8,128)(2,1)S(1)} %all_to_all.15.read_ref), channel_id=1, source_target_pairs={{0,1},{1,0},{2,3},{3,2},{4,5},{5,4},{6,7},{7,6},{8,9},{9,8},{10,11... | collective-permute-start | bytes 1572872 | tf_op jit(solution)/shard_map/ppermute | solution.py:413

commit v8 on v7

--- a/solution.py
+++ b/solution.py
@@ -256,14 +256,23 @@
     rest_refs, (own_ref, sems) = refs[:-2], refs[-2:]
     depth, columns = own_ref.shape
     size = weight_ref.shape[0] // depth
+    shares = sems.shape[1]
+    length = depth // shares
     copies = []
     for s, target in enumerate((own_ref, *rest_refs)):
-        rows = pl.ds(pl.multiple_of(lax.rem(column_ref[0] + size - s, size) * depth, depth), depth)
-        copies.append(pltpu.make_async_copy(weight_ref.at[rows], target, sems.at[s]))
-        copies[-1].start()
-    copies[0].wait()
-    sum_ref[...] = dot(flat_heads(read_ref), own_ref[...])
-    for copy in copies[1:]:
+        base = lax.rem(column_ref[0] + size - s, size) * depth
+        for i in range(shares):
+            rows = pl.ds(pl.multiple_of(base + i * length, length), length)
+            part = target.at[pl.ds(i * length, length)]
+            copies.append(pltpu.make_async_copy(weight_ref.at[rows], part, sems.at[s, i]))
+            copies[-1].start()
+    flat = flat_heads(read_ref)
+    for i in range(shares):
+        copies[i].wait()
+        rows = slice(i * length, (i + 1) * length)
+        value = dot(flat[:, rows], own_ref[rows])
+        sum_ref[...] = value if i == 0 else sum_ref[...] + value
+    for copy in copies[shares:]:
         copy.wait()
 
 
@@ -398,7 +407,7 @@
         flops=2**33,
     )
     read = call(
-        functools.partial(read_kernel, max(1, chunk // 2)),
+        functools.partial(read_kernel, 1),
         struct((heads, tokens, dh), BF16),
         (side.reshape(1), new, asked),
         scalars=1,
@@ -415,6 +424,7 @@
     ]
     columns = out_proj.shape[1]
     depth = heads * dh
+    parts_of = max(c for c in (1, 2, 4) if depth % (c * LANES) == 0)
     own, *rest = call(
         project_own_kernel,
         (
@@ -425,7 +435,7 @@
         scalars=1,
         hbm=(2,),
         limit=49,
-        scratch=[pltpu.VMEM((depth, columns), BF16), pltpu.SemaphoreType.DMA((head_size,))],
+        scratch=[pltpu.VMEM((depth, columns), BF16), pltpu.SemaphoreType.DMA((head_size, parts_of))],
     )
     shares = max(c for c in (1, 2, 4) if columns % (c * LANES) == 0)
     return call(

time: 61.5 us -> 61.4 us (level)
  no operation moved by 1% of the time
where the time goes in v8:
time: 61.4 us; the launch traced here: 60.8 us
  Pallas kernels  16.7 us (27%)
  waiting for transfers between devices  15.3 us (25%)
  starting transfers between devices  13.8 us (22%)
  blocking collectives  11.4 us (19%)
  local copies, waits for them, and re-layouts  2.84 us (5%)
  between operations  0.79 us (1%)
    pallas_call x8, Pallas kernels, call(): pl.pallas_call(kernel, out_shape=out_shape, in_specs=specs, out_specs=jax...  16.7 us
    all_to_all x1, waiting for transfers between devices, on_device(): lax.all_to_all(pairs, both, 0, 0, tiled=True, axis_index_groups=groups)  12.2 us
    all_to_all x1, blocking collectives, on_device(): lax.all_to_all(read, both, 0, 0, tiled=True, axis_index_groups=[[g[i] for...  11.4 us
    all_to_all x1, starting transfers between devices, on_device(): lax.all_to_all(pairs, both, 0, 0, tiled=True, axis_index_groups=groups)  6.76 us
    all_to_all x1, starting transfers between devices, on_device(): lax.all_to_all(asked, both, 0, 0, tiled=True, axis_index_groups=halves_of)  3.9 us
    ppermute x2, waiting for transfers between devices, on_device(): lax.ppermute(code, both, turn)  3.11 us
    ppermute x2, starting transfers between devices, on_device(): lax.ppermute(code, both, turn)  3.06 us
    unnamed x5, local copies, waits for them, and re-layouts  1.61 us
  transfers between devices with their start and end apart: 6, of which 2 were waited for; matrix products, arithmetic and copies ran while one was open for 5% of the time, Pallas kernels for 18%

profile of v8, /device:TPU:0, one launch (start us, length us, event | category | flops | bytes accessed | tf_op | source)
XLA Modules:
  0.0 60.8 jit_solution(12549751877538964502)
XLA Ops:
  0.7 2.1 %shard_map.73 = bf16[8,2,256,128]{3,2,1,0:T(8,128)(2,1)} custom-call(s32[1,1]{1,0:T(1,128)} %bitcast.9.mask_ref, bf16[256,1024]{1,0:T(8,128)(2,1)} %keys_ref.1, bf16[256,1024]{1,0:T(8,128)(2,1)} %values_ref.1), custom_call_target="tpu_custom_call" | custom-call | tf_op jit(solution)/shard_map/pallas_call | solution.py:309
  2.8 6.8 %all-to-all-start = ((bf16[8,2,256,128]{3,2,1,0:T(8,128)(2,1)}), bf16[8,2,256,128]{3,2,1,0:T(8,128)(2,1)S(1)}, u32[]{:S(2)}, u32[]{:S(2)}) async-start(bf16[8,2,256,128]{3,2,1,0:T(8,128)(2,1)} %shard_map.73), calls=%async_computation | async-start | bytes 2097152 | tf_op jit(solution)/shard_map/all_to_all | solution.py:367
  9.5 1.2 %copy.8 = bf16[256,1024]{0,1:T(8,128)(2,1)S(1)} copy(bf16[256,1024]{1,0:T(8,128)(2,1)} %param.9) | data formatting | bytes 1048576 | tf_op args[2]
  10.8 0.2 copy.12
  11.0 0.1 collective-permute-start.2
  11.1 1.2 %dynamic-slice_bitcast_fusion.weights_ref.refs_4_ = f32[3,128,512]{2,1,0:T(8,128)S(1)} fusion(f32[3,8,128,512]{3,2,1,0:T(8,128)} %param.10, s32[]{:T(128)S(6)} %select_n.46), kind=kLoop, calls=%fused_computation | loop fusion | bytes 1572868 | tf_op jit(solution)/shard_map/jit(dynamic_index_in_dim)/squeeze | solution.py:377
  12.3 12.2 %all-to-all-done.recv_ref = bf16[8,2,256,128]{3,2,1,0:T(8,128)(2,1)S(1)} async-done(((bf16[8,2,256,128]{3,2,1,0:T(8,128)(2,1)}), bf16[8,2,256,128]{3,2,1,0:T(8,128)(2,1)S(1)}, u32[]{:S(2)}, u32[]{:S(2)}) %all-to-all-start) | async-done | bytes 1048608 | tf_op jit(solution)/shard_map/all_to_all | solution.py:367
  24.5 2.0 %shard_map.74.refs_0_ = s16[784,128]{1,0:T(8,128)(2,1)S(1)} custom-call(bf16[8,2,256,128]{3,2,1,0:T(8,128)(2,1)S(1)} %all-to-all-done.recv_ref, f32[3,128,512]{2,1,0:T(8,128)S(1)} %dynamic-slice_bitcast_fusion.weights_ref.refs_4_), custom_call_target="tpu_custom_call" | custom-call | flops 4294967296 | bytes 1048576 | tf_op jit(solution)/shard_map/pallas_call | solution.py:309
  26.5 0.0 copy-start
  26.5 1.1 %collective-permute-start = (s16[784,128]{1,0:T(8,128)(2,1)S(1)}, s16[784,128]{1,0:T(8,128)(2,1)S(1)}, u32[]{:S(2)}, u32[]{:S(2)}) collective-permute-start(s16[784,128]{1,0:T(8,128)(2,1)S(1)} %shard_map.74.refs_0_), channel_id=1, source_target_pairs={{0,16},{2,18},{4,20},{6,22},{8,24},{10,26},{12,28},{14,30},{16,0},... | collective-permute-start | bytes 602120 | tf_op jit(solution)/shard_map/ppermute | solution.py:398
  27.7 2.0 %shard_map.75.refs_2_ = s16[784,128]{1,0:T(8,128)(2,1)S(1)} custom-call(bf16[8,2,256,128]{3,2,1,0:T(8,128)(2,1)S(1)} %all-to-all-done.recv_ref, f32[3,128,512]{2,1,0:T(8,128)S(1)} %dynamic-slice_bitcast_fusion.weights_ref.refs_4_), custom_call_target="tpu_custom_call" | custom-call | flops 4294967296 | bytes 1048576 | tf_op jit(solution)/shard_map/pallas_call | solution.py:309
  29.6 1.9 %collective-permute-start.1 = (s16[784,128]{1,0:T(8,128)(2,1)S(1)}, s16[784,128]{1,0:T(8,128)(2,1)S(1)}, u32[]{:S(2)}, u32[]{:S(2)}) collective-permute-start(s16[784,128]{1,0:T(8,128)(2,1)S(1)} %shard_map.75.refs_2_), channel_id=1, source_target_pairs={{0,16},{2,18},{4,20},{6,22},{8,24},{10,26},{12,28},{14,30},{16,0},... | collective-permute-start | bytes 602120 | tf_op jit(solution)/shard_map/ppermute | solution.py:398
  31.6 0.2 copy.11
  31.7 0.0 collective-permute-done.2.theirs_ref
  31.8 0.8 %shard_map.77 = bf16[4,2,256,128]{3,2,1,0:T(8,128)(2,1)} custom-call(bf16[4,256,128]{2,1,0:T(8,128)(2,1)S(1)} %bitcast.10, bf16[4,256,128]{2,1,0:T(8,128)(2,1)S(1)} %collective-permute-done.2.theirs_ref), custom_call_target="tpu_custom_call" | custom-call | tf_op jit(solution)/shard_map/pallas_call | solution.py:309
  32.6 3.9 %all-to-all-start.1 = ((bf16[4,2,256,128]{3,2,1,0:T(8,128)(2,1)}), bf16[4,2,256,128]{3,2,1,0:T(8,128)(2,1)S(1)}, u32[]{:S(2)}, u32[]{:S(2)}) async-start(bf16[4,2,256,128]{3,2,1,0:T(8,128)(2,1)} %shard_map.77), calls=%async_computation.1 | async-start | bytes 1048576 | tf_op jit(solution)/shard_map/all_to_all | solution.py:396
  36.5 0.0 collective-permute-done.refs_1_
  36.5 3.1 %collective-permute-done.1.refs_3_ = s16[784,128]{1,0:T(8,128)(2,1)S(1)} collective-permute-done((s16[784,128]{1,0:T(8,128)(2,1)S(1)}, s16[784,128]{1,0:T(8,128)(2,1)S(1)}, u32[]{:S(2)}, u32[]{:S(2)}) %collective-permute-start.1) | collective-permute-done | bytes 200736 | tf_op jit(solution)/shard_map/ppermute | solution.py:398
  39.6 0.0 copy-done
  39.6 4.1 %shard_map.76.new_ref = bf16[3,128,512]{2,1,0:T(8,128)(2,1)S(1)} custom-call(s32[1]{0:T(128)} %bitcast.2.slot_ref, f32[8]{0:T(128)S(1)} %copy-done, s16[784,128]{1,0:T(8,128)(2,1)S(1)} %shard_map.74.refs_0_, s16[784,128]{1,0:T(8,128)(2,1)S(1)} %collective-permute-done.refs_1_, s16[784,128]{1,0:T(8,128)(2,1)S(1)} %shard_map.75.refs_2_, ...), custom_call_target="tpu_custom_call" | custom-call | flops 8589934592 | bytes 1048576 | tf_op jit(solution)/shard_map/pallas_call | solution.py:309
  43.7 0.0 all-to-all-done.1.query_ref
  43.7 1.9 %shard_map.78 = bf16[8,256,128]{2,1,0:T(8,128)(2,1)S(1)} custom-call(s32[1]{0:T(128)} %bitcast.1.side_ref, bf16[3,128,512]{2,1,0:T(8,128)(2,1)S(1)} %shard_map.76.new_ref, bf16[4,2,256,128]{3,2,1,0:T(8,128)(2,1)S(1)} %all-to-all-done.1.query_ref), custom_call_target="tpu_custom_call" | custom-call | tf_op jit(solution)/shard_map/pallas_call | solution.py:309
  45.6 11.4 %all_to_all.15.read_ref = bf16[8,256,128]{2,1,0:T(8,128)(2,1)S(1)} all-to-all(bf16[8,256,128]{2,1,0:T(8,128)(2,1)S(1)} %shard_map.78), channel_id=1, replica_groups={{14,12,6,4,10,8,2,0},{30,28,22,20,26,24,18,16},{23,21,7,5,19,17,3,1},{3..., dimensions={0} | all-to-all | bytes 1048576 | tf_op jit(solution)/shard_map/all_to_all | solution.py:418
  57.0 0.0 collective-permute-start.3
  57.0 2.2 %shard_map.79 = (f32[256,1024]{1,0:T(8,128)S(1)}, bf16[1024,1024]{1,0:T(8,128)(2,1)S(1)}) custom-call(s32[1]{0:T(128)} %bitcast.column_ref, bf16[8,256,128]{2,1,0:T(8,128)(2,1)S(1)} %all_to_all.15.read_ref, bf16[2048,1024]{1,0:T(8,128)(2,1)} %weight_ref.1), custom_call_target="tpu_custom_call" | custom-call | tf_op jit(solution)/shard_map/pallas_call | solution.py:309
  59.3 0.0 collective-permute-done.3.refs_0_
  59.3 1.5 %shard_map.80 = bf16[256,1024]{1,0:T(8,128)(2,1)} custom-call(f32[256,1024]{1,0:T(8,128)S(1)} %get-tuple-element.7.sum_ref, bf16[8,256,128]{2,1,0:T(8,128)(2,1)S(1)} %collective-permute-done.3.refs_0_, bf16[1024,1024]{1,0:T(8,128)(2,1)S(1)} %get-tuple-element.8.refs_1_), custom_call_target="tpu_custom_call" | custom-call | tf_op jit(solution)/shard_map/pallas_call | solution.py:309
  (1 shorter events, 0.0 us)
Async XLA Ops:
  2.8 21.7 %all-to-all-start = ((bf16[8,2,256,128]{3,2,1,0:T(8,128)(2,1)}), bf16[8,2,256,128]{3,2,1,0:T(8,128)(2,1)S(1)}, u32[]{:S(2)}, u32[]{:S(2)}) async-start(bf16[8,2,256,128]{3,2,1,0:T(8,128)(2,1)} %shard_map.73), calls=%async_computation | async-start | bytes 2097152 | tf_op jit(solution)/shard_map/all_to_all | solution.py:367
  11.0 20.7 %collective-permute-start.2 = (bf16[4,256,128]{2,1,0:T(8,128)(2,1)S(1)}, bf16[4,256,128]{2,1,0:T(8,128)(2,1)S(1)}, u32[]{:S(2)}, u32[]{:S(2)}) collective-permute-start(bf16[4,256,128]{2,1,0:T(8,128)(2,1)S(1)} %bitcast.12), channel_id=1, source_target_pairs={{8,0},{10,2},{12,4},{14,6},{0,8},{2,10},{4,12},{6,14},{24,16},{26,... | collective-permute-start | bytes 786440 | tf_op jit(solution)/shard_map/ppermute | solution.py:374
  26.5 13.1 %copy-start = (f32[8]{0:T(128)S(1)}, f32[8]{0:T(128)}, u32[]{:S(2)}) copy-start(f32[8]{0:T(128)} %rate_ref.1) | copy-start | bytes 100
  26.5 10.0 %collective-permute-start = (s16[784,128]{1,0:T(8,128)(2,1)S(1)}, s16[784,128]{1,0:T(8,128)(2,1)S(1)}, u32[]{:S(2)}, u32[]{:S(2)}) collective-permute-start(s16[784,128]{1,0:T(8,128)(2,1)S(1)} %shard_map.74.refs_0_), channel_id=1, source_target_pairs={{0,16},{2,18},{4,20},{6,22},{8,24},{10,26},{12,28},{14,30},{16,0},... | collective-permute-start | bytes 602120 | tf_op jit(solution)/shard_map/ppermute | solution.py:398
  29.6 10.0 %collective-permute-start.1 = (s16[784,128]{1,0:T(8,128)(2,1)S(1)}, s16[784,128]{1,0:T(8,128)(2,1)S(1)}, u32[]{:S(2)}, u32[]{:S(2)}) collective-permute-start(s16[784,128]{1,0:T(8,128)(2,1)S(1)} %shard_map.75.refs_2_), channel_id=1, source_target_pairs={{0,16},{2,18},{4,20},{6,22},{8,24},{10,26},{12,28},{14,30},{16,0},... | collective-permute-start | bytes 602120 | tf_op jit(solution)/shard_map/ppermute | solution.py:398
  32.6 11.1 %all-to-all-start.1 = ((bf16[4,2,256,128]{3,2,1,0:T(8,128)(2,1)}), bf16[4,2,256,128]{3,2,1,0:T(8,128)(2,1)S(1)}, u32[]{:S(2)}, u32[]{:S(2)}) async-start(bf16[4,2,256,128]{3,2,1,0:T(8,128)(2,1)} %shard_map.77), calls=%async_computation.1 | async-start | bytes 1048576 | tf_op jit(solution)/shard_map/all_to_all | solution.py:396
  57.0 2.2 %collective-permute-start.3 = (bf16[8,256,128]{2,1,0:T(8,128)(2,1)S(1)}, bf16[8,256,128]{2,1,0:T(8,128)(2,1)S(1)}, u32[]{:S(2)}, u32[]{:S(2)}) collective-permute-start(bf16[8,256,128]{2,1,0:T(8,128)(2,1)S(1)} %all_to_all.15.read_ref), channel_id=1, source_target_pairs={{0,1},{1,0},{2,3},{3,2},{4,5},{5,4},{6,7},{7,6},{8,9},{9,8},{10,11... | collective-permute-start | bytes 1572872 | tf_op jit(solution)/shard_map/ppermute | solution.py:422

commit v9 on v8

--- a/solution.py
+++ b/solution.py
@@ -80,8 +80,8 @@
     grads_ref = scratch[0] if scratch else out_ref
     ff = grads_ref.shape[-1]
     units = pl.ds(start, ff)
-    gate_up = jnp.concatenate([weights_ref[0, :, units], weights_ref[2, :, units]], axis=1).astype(BF16)
-    down = weights_ref[1, :, units].astype(BF16)
+    gate_up = jnp.concatenate([weights_ref[0, :, units], weights_ref[2, :, units]], axis=1)
+    down = weights_ref[1, :, units]
     for i in range(0, sources, chunk):
         rows = pl.ds(i, chunk)
         keys = recv_ref[rows, 0].reshape(chunk * sub, dh)
@@ -378,6 +378,7 @@
     chunk = max(c for c in (1, 2, 4) if heads % c == 0)
     split = 2 if ff % (2 * LANES) == 0 else 1
     width = ff // split
+    low = weights.astype(BF16)
     coded = count == 2
     partials = []
     for start in range(0, ff, width):
@@ -386,7 +387,7 @@
         partial = call(
             functools.partial(gradient_kernel, max(1, chunk // 2), start),
             struct((rows, LANES), jnp.int16) if coded else sums,
-            (received, weights),
+            (received, low),
             flops=2**32,
             limit=16,
             scratch=[pltpu.VMEM(sums.shape, F32)] if coded else [],

time: 61.4 us -> 61.4 us (level)
  other arithmetic: 0 us -> 1.26 us
    convert_element_type x0 -> x1, other arithmetic: none -> 1.26 us  [on_device(): low = weights.astype(BF16)]
    squeeze x1 -> x0, local copies, waits for them, and re-layouts: 1.19 us -> none  [on_device(): weights = lax.dynamic_index_in_dim(fast_weights, slot, 1, keepdims=False)]
    unnamed x5, local copies, waits for them, and re-layouts: 1.61 us -> 2.28 us
    all_to_all x1, waiting for transfers between devices: 12.2 us -> 11.6 us  [on_device(): lax.all_to_all(pairs, both, 0, 0, tiled=True, axis_index_groups=groups)]
  transfers between devices with their start and end apart: 6 -> 6, of which waited for: 2 -> 2; matrix products, arithmetic and copies ran while one was open for 5% -> 6% of each run, Pallas kernels for 18% -> 18%
where the time goes in v9:
time: 61.4 us; the launch traced here: 60.8 us
  Pallas kernels  16.6 us (27%)
  waiting for transfers between devices  14.7 us (24%)
  starting transfers between devices  13.7 us (22%)
  blocking collectives  11.4 us (19%)
  local copies, waits for them, and re-layouts  2.32 us (4%)
  other arithmetic  1.26 us (2%)
  between operations  0.77 us (1%)
    pallas_call x8, Pallas kernels, call(): pl.pallas_call(kernel, out_shape=out_shape, in_specs=specs, out_specs=jax...  16.6 us
    all_to_all x1, waiting for transfers between devices, on_device(): lax.all_to_all(pairs, both, 0, 0, tiled=True, axis_index_groups=groups)  11.6 us
    all_to_all x1, blocking collectives, on_device(): lax.all_to_all(read, both, 0, 0, tiled=True, axis_index_groups=[[g[i] for...  11.4 us
    all_to_all x1, starting transfers between devices, on_device(): lax.all_to_all(pairs, both, 0, 0, tiled=True, axis_index_groups=groups)  6.76 us
    all_to_all x1, starting transfers between devices, on_device(): lax.all_to_all(asked, both, 0, 0, tiled=True, axis_index_groups=halves_of)  3.9 us
    ppermute x2, waiting for transfers between devices, on_device(): lax.ppermute(code, both, turn)  3.11 us
    ppermute x2, starting transfers between devices, on_device(): lax.ppermute(code, both, turn)  3.06 us
    unnamed x5, local copies, waits for them, and re-layouts  2.28 us
  transfers between devices with their start and end apart: 6, of which 2 were waited for; matrix products, arithmetic and copies ran while one was open for 6% of the time, Pallas kernels for 18%

profile of v9, /device:TPU:0, one launch (start us, length us, event | category | flops | bytes accessed | tf_op | source)
XLA Modules:
  0.0 60.8 jit_solution(5593729512717259165)
XLA Ops:
  0.7 2.1 %shard_map.73 = bf16[8,2,256,128]{3,2,1,0:T(8,128)(2,1)} custom-call(s32[1,1]{1,0:T(1,128)} %bitcast.10.mask_ref, bf16[256,1024]{1,0:T(8,128)(2,1)} %keys_ref.1, bf16[256,1024]{1,0:T(8,128)(2,1)} %values_ref.1), custom_call_target="tpu_custom_call" | custom-call | tf_op jit(solution)/shard_map/pallas_call | solution.py:309
  2.8 6.8 %all-to-all-start = ((bf16[8,2,256,128]{3,2,1,0:T(8,128)(2,1)}), bf16[8,2,256,128]{3,2,1,0:T(8,128)(2,1)S(1)}, u32[]{:S(2)}, u32[]{:S(2)}) async-start(bf16[8,2,256,128]{3,2,1,0:T(8,128)(2,1)} %shard_map.73), calls=%async_computation | async-start | bytes 2097152 | tf_op jit(solution)/shard_map/all_to_all | solution.py:367
  9.5 1.2 %copy.8 = bf16[256,1024]{0,1:T(8,128)(2,1)S(1)} copy(bf16[256,1024]{1,0:T(8,128)(2,1)} %param.9) | data formatting | bytes 1048576 | tf_op args[2]
  10.8 0.8 %copy.12 = bf16[256,4,128]{2,0,1:T(8,128)(2,1)} copy(bf16[256,4,128]{0,2,1:T(8,128)(2,1)S(1)} %get-tuple-element.11) | data formatting | bytes 524288
  11.7 0.0 collective-permute-start.2
  11.7 1.3 %fusion = (bf16[3,128,512]{2,1,0:T(8,128)(2,1)S(1)}, f32[3,128,512]{2,1,0:T(8,128)S(1)}) fusion(f32[3,8,128,512]{3,2,1,0:T(8,128)} %param.10, s32[]{:T(128)S(6)} %select_n.46), kind=kLoop, calls=%fused_computation.3 | loop fusion | flops 196608 | bytes 1966084 | tf_op jit(solution)/shard_map/convert_element_type | solution.py:381
  12.9 11.6 %all-to-all-done.recv_ref = bf16[8,2,256,128]{3,2,1,0:T(8,128)(2,1)S(1)} async-done(((bf16[8,2,256,128]{3,2,1,0:T(8,128)(2,1)}), bf16[8,2,256,128]{3,2,1,0:T(8,128)(2,1)S(1)}, u32[]{:S(2)}, u32[]{:S(2)}) %all-to-all-start) | async-done | bytes 1048608 | tf_op jit(solution)/shard_map/all_to_all | solution.py:367
  24.5 2.0 %shard_map.74.refs_0_ = s16[784,128]{1,0:T(8,128)(2,1)S(1)} custom-call(bf16[8,2,256,128]{3,2,1,0:T(8,128)(2,1)S(1)} %all-to-all-done.recv_ref, bf16[3,128,512]{2,1,0:T(8,128)(2,1)S(1)} %get-tuple-element.9.weights_ref), custom_call_target="tpu_custom_call" | custom-call | flops 4294967296 | bytes 1048576 | tf_op jit(solution)/shard_map/pallas_call | solution.py:309
  26.5 0.0 copy-start
  26.5 1.1 %collective-permute-start = (s16[784,128]{1,0:T(8,128)(2,1)S(1)}, s16[784,128]{1,0:T(8,128)(2,1)S(1)}, u32[]{:S(2)}, u32[]{:S(2)}) collective-permute-start(s16[784,128]{1,0:T(8,128)(2,1)S(1)} %shard_map.74.refs_0_), channel_id=1, source_target_pairs={{0,16},{2,18},{4,20},{6,22},{8,24},{10,26},{12,28},{14,30},{16,0},... | collective-permute-start | bytes 602120 | tf_op jit(solution)/shard_map/ppermute | solution.py:399
  27.6 2.0 %shard_map.75.refs_2_ = s16[784,128]{1,0:T(8,128)(2,1)S(1)} custom-call(bf16[8,2,256,128]{3,2,1,0:T(8,128)(2,1)S(1)} %all-to-all-done.recv_ref, bf16[3,128,512]{2,1,0:T(8,128)(2,1)S(1)} %get-tuple-element.9.weights_ref), custom_call_target="tpu_custom_call" | custom-call | flops 4294967296 | bytes 1048576 | tf_op jit(solution)/shard_map/pallas_call | solution.py:309
  29.6 1.9 %collective-permute-start.1 = (s16[784,128]{1,0:T(8,128)(2,1)S(1)}, s16[784,128]{1,0:T(8,128)(2,1)S(1)}, u32[]{:S(2)}, u32[]{:S(2)}) collective-permute-start(s16[784,128]{1,0:T(8,128)(2,1)S(1)} %shard_map.75.refs_2_), channel_id=1, source_target_pairs={{0,16},{2,18},{4,20},{6,22},{8,24},{10,26},{12,28},{14,30},{16,0},... | collective-permute-start | bytes 602120 | tf_op jit(solution)/shard_map/ppermute | solution.py:399
  31.5 0.2 copy.11
  31.7 0.0 collective-permute-done.2.theirs_ref
  31.7 0.8 %shard_map.77 = bf16[4,2,256,128]{3,2,1,0:T(8,128)(2,1)} custom-call(bf16[4,256,128]{2,1,0:T(8,128)(2,1)S(1)} %bitcast.11, bf16[4,256,128]{2,1,0:T(8,128)(2,1)S(1)} %collective-permute-done.2.theirs_ref), custom_call_target="tpu_custom_call" | custom-call | tf_op jit(solution)/shard_map/pallas_call | solution.py:309
  32.5 3.9 %all-to-all-start.1 = ((bf16[4,2,256,128]{3,2,1,0:T(8,128)(2,1)}), bf16[4,2,256,128]{3,2,1,0:T(8,128)(2,1)S(1)}, u32[]{:S(2)}, u32[]{:S(2)}) async-start(bf16[4,2,256,128]{3,2,1,0:T(8,128)(2,1)} %shard_map.77), calls=%async_computation.1 | async-start | bytes 1048576 | tf_op jit(solution)/shard_map/all_to_all | solution.py:397
  36.4 0.0 collective-permute-done.refs_1_
  36.5 3.1 %collective-permute-done.1.refs_3_ = s16[784,128]{1,0:T(8,128)(2,1)S(1)} collective-permute-done((s16[784,128]{1,0:T(8,128)(2,1)S(1)}, s16[784,128]{1,0:T(8,128)(2,1)S(1)}, u32[]{:S(2)}, u32[]{:S(2)}) %collective-permute-start.1) | collective-permute-done | bytes 200736 | tf_op jit(solution)/shard_map/ppermute | solution.py:399
  39.6 0.0 copy-done
  39.6 4.1 %shard_map.76.new_ref = bf16[3,128,512]{2,1,0:T(8,128)(2,1)S(1)} custom-call(s32[1]{0:T(128)} %bitcast.2.slot_ref, f32[8]{0:T(128)S(1)} %copy-done, s16[784,128]{1,0:T(8,128)(2,1)S(1)} %shard_map.74.refs_0_, s16[784,128]{1,0:T(8,128)(2,1)S(1)} %collective-permute-done.refs_1_, s16[784,128]{1,0:T(8,128)(2,1)S(1)} %shard_map.75.refs_2_, ...), custom_call_target="tpu_custom_call" | custom-call | flops 8589934592 | bytes 1048576 | tf_op jit(solution)/shard_map/pallas_call | solution.py:309
  43.6 0.0 all-to-all-done.1.query_ref
  43.6 1.9 %shard_map.78 = bf16[8,256,128]{2,1,0:T(8,128)(2,1)S(1)} custom-call(s32[1]{0:T(128)} %bitcast.1.side_ref, bf16[3,128,512]{2,1,0:T(8,128)(2,1)S(1)} %shard_map.76.new_ref, bf16[4,2,256,128]{3,2,1,0:T(8,128)(2,1)S(1)} %all-to-all-done.1.query_ref), custom_call_target="tpu_custom_call" | custom-call | tf_op jit(solution)/shard_map/pallas_call | solution.py:309
  45.6 11.4 %all_to_all.15.read_ref = bf16[8,256,128]{2,1,0:T(8,128)(2,1)S(1)} all-to-all(bf16[8,256,128]{2,1,0:T(8,128)(2,1)S(1)} %shard_map.78), channel_id=1, replica_groups={{14,12,6,4,10,8,2,0},{30,28,22,20,26,24,18,16},{23,21,7,5,19,17,3,1},{3..., dimensions={0} | all-to-all | bytes 1048576 | tf_op jit(solution)/shard_map/all_to_all | solution.py:419
  57.0 0.0 collective-permute-start.3
  57.0 2.2 %shard_map.79 = (f32[256,1024]{1,0:T(8,128)S(1)}, bf16[1024,1024]{1,0:T(8,128)(2,1)S(1)}) custom-call(s32[1]{0:T(128)} %bitcast.column_ref, bf16[8,256,128]{2,1,0:T(8,128)(2,1)S(1)} %all_to_all.15.read_ref, bf16[2048,1024]{1,0:T(8,128)(2,1)} %weight_ref.1), custom_call_target="tpu_custom_call" | custom-call | tf_op jit(solution)/shard_map/pallas_call | solution.py:309
  59.2 0.0 collective-permute-done.3.refs_0_
  59.2 1.5 %shard_map.80 = bf16[256,1024]{1,0:T(8,128)(2,1)} custom-call(f32[256,1024]{1,0:T(8,128)S(1)} %get-tuple-element.7.sum_ref, bf16[8,256,128]{2,1,0:T(8,128)(2,1)S(1)} %collective-permute-done.3.refs_0_, bf16[1024,1024]{1,0:T(8,128)(2,1)S(1)} %get-tuple-element.8.refs_1_), custom_call_target="tpu_custom_call" | custom-call | tf_op jit(solution)/shard_map/pallas_call | solution.py:309
  (1 shorter events, 0.0 us)
Async XLA Ops:
  2.8 21.7 %all-to-all-start = ((bf16[8,2,256,128]{3,2,1,0:T(8,128)(2,1)}), bf16[8,2,256,128]{3,2,1,0:T(8,128)(2,1)S(1)}, u32[]{:S(2)}, u32[]{:S(2)}) async-start(bf16[8,2,256,128]{3,2,1,0:T(8,128)(2,1)} %shard_map.73), calls=%async_computation | async-start | bytes 2097152 | tf_op jit(solution)/shard_map/all_to_all | solution.py:367
  11.7 20.1 %collective-permute-start.2 = (bf16[4,256,128]{2,1,0:T(8,128)(2,1)}, bf16[4,256,128]{2,1,0:T(8,128)(2,1)S(1)}, u32[]{:S(2)}, u32[]{:S(2)}) collective-permute-start(bf16[4,256,128]{2,1,0:T(8,128)(2,1)} %bitcast.7), channel_id=1, source_target_pairs={{8,0},{10,2},{12,4},{14,6},{0,8},{2,10},{4,12},{6,14},{24,16},{26,... | collective-permute-start | bytes 786440 | tf_op jit(solution)/shard_map/ppermute | solution.py:374
  26.5 13.1 %copy-start = (f32[8]{0:T(128)S(1)}, f32[8]{0:T(128)}, u32[]{:S(2)}) copy-start(f32[8]{0:T(128)} %rate_ref.1) | copy-start | bytes 100
  26.5 10.0 %collective-permute-start = (s16[784,128]{1,0:T(8,128)(2,1)S(1)}, s16[784,128]{1,0:T(8,128)(2,1)S(1)}, u32[]{:S(2)}, u32[]{:S(2)}) collective-permute-start(s16[784,128]{1,0:T(8,128)(2,1)S(1)} %shard_map.74.refs_0_), channel_id=1, source_target_pairs={{0,16},{2,18},{4,20},{6,22},{8,24},{10,26},{12,28},{14,30},{16,0},... | collective-permute-start | bytes 602120 | tf_op jit(solution)/shard_map/ppermute | solution.py:399
  29.6 10.0 %collective-permute-start.1 = (s16[784,128]{1,0:T(8,128)(2,1)S(1)}, s16[784,128]{1,0:T(8,128)(2,1)S(1)}, u32[]{:S(2)}, u32[]{:S(2)}) collective-permute-start(s16[784,128]{1,0:T(8,128)(2,1)S(1)} %shard_map.75.refs_2_), channel_id=1, source_target_pairs={{0,16},{2,18},{4,20},{6,22},{8,24},{10,26},{12,28},{14,30},{16,0},... | collective-permute-start | bytes 602120 | tf_op jit(solution)/shard_map/ppermute | solution.py:399
  32.5 11.1 %all-to-all-start.1 = ((bf16[4,2,256,128]{3,2,1,0:T(8,128)(2,1)}), bf16[4,2,256,128]{3,2,1,0:T(8,128)(2,1)S(1)}, u32[]{:S(2)}, u32[]{:S(2)}) async-start(bf16[4,2,256,128]{3,2,1,0:T(8,128)(2,1)} %shard_map.77), calls=%async_computation.1 | async-start | bytes 1048576 | tf_op jit(solution)/shard_map/all_to_all | solution.py:397
  57.0 2.2 %collective-permute-start.3 = (bf16[8,256,128]{2,1,0:T(8,128)(2,1)S(1)}, bf16[8,256,128]{2,1,0:T(8,128)(2,1)S(1)}, u32[]{:S(2)}, u32[]{:S(2)}) collective-permute-start(bf16[8,256,128]{2,1,0:T(8,128)(2,1)S(1)} %all_to_all.15.read_ref), channel_id=1, source_target_pairs={{0,1},{1,0},{2,3},{3,2},{4,5},{5,4},{6,7},{7,6},{8,9},{9,8},{10,11... | collective-permute-start | bytes 1572872 | tf_op jit(solution)/shard_map/ppermute | solution.py:423

commit v10 on v9

--- a/solution.py
+++ b/solution.py
@@ -49,11 +49,12 @@
                 pltpu.make_async_copy(sources[p].at[rows], wide_ref.at[p, rows], in_sem.at[p, r])
             )
             loads[-1].start()
-    mask_copy.wait()
     for r in range(shares):
         rows = pl.ds(r * length, length)
         for p in range(2):
             loads[2 * r + p].wait()
+            if r == 0 and p == 1:
+                mask_copy.wait()
             for i in range(heads):
                 columns = pl.ds(i * dh, dh)
                 if p == 0:

time: 61.4 us -> 61.4 us (level)
  no operation moved by 1% of the time
where the time goes in v10:
time: 61.4 us; the launch traced here: 60.8 us
  Pallas kernels  16.6 us (27%)
  waiting for transfers between devices  14.7 us (24%)
  starting transfers between devices  13.7 us (22%)
  blocking collectives  11.4 us (19%)
  local copies, waits for them, and re-layouts  2.32 us (4%)
  other arithmetic  1.26 us (2%)
  between operations  0.77 us (1%)
    pallas_call x8, Pallas kernels, call(): pl.pallas_call(kernel, out_shape=out_shape, in_specs=specs, out_specs=jax...  16.6 us
    all_to_all x1, waiting for transfers between devices, on_device(): lax.all_to_all(pairs, both, 0, 0, tiled=True, axis_index_groups=groups)  11.6 us
    all_to_all x1, blocking collectives, on_device(): lax.all_to_all(read, both, 0, 0, tiled=True, axis_index_groups=[[g[i] for...  11.4 us
    all_to_all x1, starting transfers between devices, on_device(): lax.all_to_all(pairs, both, 0, 0, tiled=True, axis_index_groups=groups)  6.76 us
    all_to_all x1, starting transfers between devices, on_device(): lax.all_to_all(asked, both, 0, 0, tiled=True, axis_index_groups=halves_of)  3.9 us
    ppermute x2, waiting for transfers between devices, on_device(): lax.ppermute(code, both, turn)  3.11 us
    ppermute x2, starting transfers between devices, on_device(): lax.ppermute(code, both, turn)  3.06 us
    unnamed x5, local copies, waits for them, and re-layouts  2.28 us
  transfers between devices with their start and end apart: 6, of which 2 were waited for; matrix products, arithmetic and copies ran while one was open for 6% of the time, Pallas kernels for 18%

profile of v10, /device:TPU:0, one launch (start us, length us, event | category | flops | bytes accessed | tf_op | source)
XLA Modules:
  0.0 60.8 jit_solution(13014151435604229550)
XLA Ops:
  0.7 2.1 %shard_map.73 = bf16[8,2,256,128]{3,2,1,0:T(8,128)(2,1)} custom-call(s32[1,1]{1,0:T(1,128)} %bitcast.10.mask_ref, bf16[256,1024]{1,0:T(8,128)(2,1)} %keys_ref.1, bf16[256,1024]{1,0:T(8,128)(2,1)} %values_ref.1), custom_call_target="tpu_custom_call" | custom-call | tf_op jit(solution)/shard_map/pallas_call | solution.py:310
  2.8 6.8 %all-to-all-start = ((bf16[8,2,256,128]{3,2,1,0:T(8,128)(2,1)}), bf16[8,2,256,128]{3,2,1,0:T(8,128)(2,1)S(1)}, u32[]{:S(2)}, u32[]{:S(2)}) async-start(bf16[8,2,256,128]{3,2,1,0:T(8,128)(2,1)} %shard_map.73), calls=%async_computation | async-start | bytes 2097152 | tf_op jit(solution)/shard_map/all_to_all | solution.py:368
  9.5 1.2 %copy.8 = bf16[256,1024]{0,1:T(8,128)(2,1)S(1)} copy(bf16[256,1024]{1,0:T(8,128)(2,1)} %param.9) | data formatting | bytes 1048576 | tf_op args[2]
  10.8 0.8 %copy.12 = bf16[256,4,128]{2,0,1:T(8,128)(2,1)} copy(bf16[256,4,128]{0,2,1:T(8,128)(2,1)S(1)} %get-tuple-element.11) | data formatting | bytes 524288
  11.7 0.0 collective-permute-start.2
  11.7 1.3 %fusion = (bf16[3,128,512]{2,1,0:T(8,128)(2,1)S(1)}, f32[3,128,512]{2,1,0:T(8,128)S(1)}) fusion(f32[3,8,128,512]{3,2,1,0:T(8,128)} %param.10, s32[]{:T(128)S(6)} %select_n.46), kind=kLoop, calls=%fused_computation.3 | loop fusion | flops 196608 | bytes 1966084 | tf_op jit(solution)/shard_map/convert_element_type | solution.py:382
  12.9 11.6 %all-to-all-done.recv_ref = bf16[8,2,256,128]{3,2,1,0:T(8,128)(2,1)S(1)} async-done(((bf16[8,2,256,128]{3,2,1,0:T(8,128)(2,1)}), bf16[8,2,256,128]{3,2,1,0:T(8,128)(2,1)S(1)}, u32[]{:S(2)}, u32[]{:S(2)}) %all-to-all-start) | async-done | bytes 1048608 | tf_op jit(solution)/shard_map/all_to_all | solution.py:368
  24.5 2.0 %shard_map.74.refs_0_ = s16[784,128]{1,0:T(8,128)(2,1)S(1)} custom-call(bf16[8,2,256,128]{3,2,1,0:T(8,128)(2,1)S(1)} %all-to-all-done.recv_ref, bf16[3,128,512]{2,1,0:T(8,128)(2,1)S(1)} %get-tuple-element.9.weights_ref), custom_call_target="tpu_custom_call" | custom-call | flops 4294967296 | bytes 1048576 | tf_op jit(solution)/shard_map/pallas_call | solution.py:310
  26.5 0.0 copy-start
  26.5 1.1 %collective-permute-start = (s16[784,128]{1,0:T(8,128)(2,1)S(1)}, s16[784,128]{1,0:T(8,128)(2,1)S(1)}, u32[]{:S(2)}, u32[]{:S(2)}) collective-permute-start(s16[784,128]{1,0:T(8,128)(2,1)S(1)} %shard_map.74.refs_0_), channel_id=1, source_target_pairs={{0,16},{2,18},{4,20},{6,22},{8,24},{10,26},{12,28},{14,30},{16,0},... | collective-permute-start | bytes 602120 | tf_op jit(solution)/shard_map/ppermute | solution.py:400
  27.6 2.0 %shard_map.75.refs_2_ = s16[784,128]{1,0:T(8,128)(2,1)S(1)} custom-call(bf16[8,2,256,128]{3,2,1,0:T(8,128)(2,1)S(1)} %all-to-all-done.recv_ref, bf16[3,128,512]{2,1,0:T(8,128)(2,1)S(1)} %get-tuple-element.9.weights_ref), custom_call_target="tpu_custom_call" | custom-call | flops 4294967296 | bytes 1048576 | tf_op jit(solution)/shard_map/pallas_call | solution.py:310
  29.6 1.9 %collective-permute-start.1 = (s16[784,128]{1,0:T(8,128)(2,1)S(1)}, s16[784,128]{1,0:T(8,128)(2,1)S(1)}, u32[]{:S(2)}, u32[]{:S(2)}) collective-permute-start(s16[784,128]{1,0:T(8,128)(2,1)S(1)} %shard_map.75.refs_2_), channel_id=1, source_target_pairs={{0,16},{2,18},{4,20},{6,22},{8,24},{10,26},{12,28},{14,30},{16,0},... | collective-permute-start | bytes 602120 | tf_op jit(solution)/shard_map/ppermute | solution.py:400
  31.5 0.2 copy.11
  31.7 0.0 collective-permute-done.2.theirs_ref
  31.7 0.8 %shard_map.77 = bf16[4,2,256,128]{3,2,1,0:T(8,128)(2,1)} custom-call(bf16[4,256,128]{2,1,0:T(8,128)(2,1)S(1)} %bitcast.11, bf16[4,256,128]{2,1,0:T(8,128)(2,1)S(1)} %collective-permute-done.2.theirs_ref), custom_call_target="tpu_custom_call" | custom-call | tf_op jit(solution)/shard_map/pallas_call | solution.py:310
  32.5 3.9 %all-to-all-start.1 = ((bf16[4,2,256,128]{3,2,1,0:T(8,128)(2,1)}), bf16[4,2,256,128]{3,2,1,0:T(8,128)(2,1)S(1)}, u32[]{:S(2)}, u32[]{:S(2)}) async-start(bf16[4,2,256,128]{3,2,1,0:T(8,128)(2,1)} %shard_map.77), calls=%async_computation.1 | async-start | bytes 1048576 | tf_op jit(solution)/shard_map/all_to_all | solution.py:398
  36.4 0.0 collective-permute-done.refs_1_
  36.5 3.1 %collective-permute-done.1.refs_3_ = s16[784,128]{1,0:T(8,128)(2,1)S(1)} collective-permute-done((s16[784,128]{1,0:T(8,128)(2,1)S(1)}, s16[784,128]{1,0:T(8,128)(2,1)S(1)}, u32[]{:S(2)}, u32[]{:S(2)}) %collective-permute-start.1) | collective-permute-done | bytes 200736 | tf_op jit(solution)/shard_map/ppermute | solution.py:400
  39.6 0.0 copy-done
  39.6 4.1 %shard_map.76.new_ref = bf16[3,128,512]{2,1,0:T(8,128)(2,1)S(1)} custom-call(s32[1]{0:T(128)} %bitcast.2.slot_ref, f32[8]{0:T(128)S(1)} %copy-done, s16[784,128]{1,0:T(8,128)(2,1)S(1)} %shard_map.74.refs_0_, s16[784,128]{1,0:T(8,128)(2,1)S(1)} %collective-permute-done.refs_1_, s16[784,128]{1,0:T(8,128)(2,1)S(1)} %shard_map.75.refs_2_, ...), custom_call_target="tpu_custom_call" | custom-call | flops 8589934592 | bytes 1048576 | tf_op jit(solution)/shard_map/pallas_call | solution.py:310
  43.6 0.0 all-to-all-done.1.query_ref
  43.6 1.9 %shard_map.78 = bf16[8,256,128]{2,1,0:T(8,128)(2,1)S(1)} custom-call(s32[1]{0:T(128)} %bitcast.1.side_ref, bf16[3,128,512]{2,1,0:T(8,128)(2,1)S(1)} %shard_map.76.new_ref, bf16[4,2,256,128]{3,2,1,0:T(8,128)(2,1)S(1)} %all-to-all-done.1.query_ref), custom_call_target="tpu_custom_call" | custom-call | tf_op jit(solution)/shard_map/pallas_call | solution.py:310
  45.6 11.4 %all_to_all.15.read_ref = bf16[8,256,128]{2,1,0:T(8,128)(2,1)S(1)} all-to-all(bf16[8,256,128]{2,1,0:T(8,128)(2,1)S(1)} %shard_map.78), channel_id=1, replica_groups={{14,12,6,4,10,8,2,0},{30,28,22,20,26,24,18,16},{23,21,7,5,19,17,3,1},{3..., dimensions={0} | all-to-all | bytes 1048576 | tf_op jit(solution)/shard_map/all_to_all | solution.py:420
  57.0 0.0 collective-permute-start.3
  57.0 2.2 %shard_map.79 = (f32[256,1024]{1,0:T(8,128)S(1)}, bf16[1024,1024]{1,0:T(8,128)(2,1)S(1)}) custom-call(s32[1]{0:T(128)} %bitcast.column_ref, bf16[8,256,128]{2,1,0:T(8,128)(2,1)S(1)} %all_to_all.15.read_ref, bf16[2048,1024]{1,0:T(8,128)(2,1)} %weight_ref.1), custom_call_target="tpu_custom_call" | custom-call | tf_op jit(solution)/shard_map/pallas_call | solution.py:310
  59.2 0.0 collective-permute-done.3.refs_0_
  59.2 1.5 %shard_map.80 = bf16[256,1024]{1,0:T(8,128)(2,1)} custom-call(f32[256,1024]{1,0:T(8,128)S(1)} %get-tuple-element.7.sum_ref, bf16[8,256,128]{2,1,0:T(8,128)(2,1)S(1)} %collective-permute-done.3.refs_0_, bf16[1024,1024]{1,0:T(8,128)(2,1)S(1)} %get-tuple-element.8.refs_1_), custom_call_target="tpu_custom_call" | custom-call | tf_op jit(solution)/shard_map/pallas_call | solution.py:310
  (1 shorter events, 0.0 us)
Async XLA Ops:
  2.8 21.7 %all-to-all-start = ((bf16[8,2,256,128]{3,2,1,0:T(8,128)(2,1)}), bf16[8,2,256,128]{3,2,1,0:T(8,128)(2,1)S(1)}, u32[]{:S(2)}, u32[]{:S(2)}) async-start(bf16[8,2,256,128]{3,2,1,0:T(8,128)(2,1)} %shard_map.73), calls=%async_computation | async-start | bytes 2097152 | tf_op jit(solution)/shard_map/all_to_all | solution.py:368
  11.7 20.1 %collective-permute-start.2 = (bf16[4,256,128]{2,1,0:T(8,128)(2,1)}, bf16[4,256,128]{2,1,0:T(8,128)(2,1)S(1)}, u32[]{:S(2)}, u32[]{:S(2)}) collective-permute-start(bf16[4,256,128]{2,1,0:T(8,128)(2,1)} %bitcast.7), channel_id=1, source_target_pairs={{8,0},{10,2},{12,4},{14,6},{0,8},{2,10},{4,12},{6,14},{24,16},{26,... | collective-permute-start | bytes 786440 | tf_op jit(solution)/shard_map/ppermute | solution.py:375
  26.5 13.1 %copy-start = (f32[8]{0:T(128)S(1)}, f32[8]{0:T(128)}, u32[]{:S(2)}) copy-start(f32[8]{0:T(128)} %rate_ref.1) | copy-start | bytes 100
  26.5 10.0 %collective-permute-start = (s16[784,128]{1,0:T(8,128)(2,1)S(1)}, s16[784,128]{1,0:T(8,128)(2,1)S(1)}, u32[]{:S(2)}, u32[]{:S(2)}) collective-permute-start(s16[784,128]{1,0:T(8,128)(2,1)S(1)} %shard_map.74.refs_0_), channel_id=1, source_target_pairs={{0,16},{2,18},{4,20},{6,22},{8,24},{10,26},{12,28},{14,30},{16,0},... | collective-permute-start | bytes 602120 | tf_op jit(solution)/shard_map/ppermute | solution.py:400
  29.6 10.0 %collective-permute-start.1 = (s16[784,128]{1,0:T(8,128)(2,1)S(1)}, s16[784,128]{1,0:T(8,128)(2,1)S(1)}, u32[]{:S(2)}, u32[]{:S(2)}) collective-permute-start(s16[784,128]{1,0:T(8,128)(2,1)S(1)} %shard_map.75.refs_2_), channel_id=1, source_target_pairs={{0,16},{2,18},{4,20},{6,22},{8,24},{10,26},{12,28},{14,30},{16,0},... | collective-permute-start | bytes 602120 | tf_op jit(solution)/shard_map/ppermute | solution.py:400
  32.5 11.1 %all-to-all-start.1 = ((bf16[4,2,256,128]{3,2,1,0:T(8,128)(2,1)}), bf16[4,2,256,128]{3,2,1,0:T(8,128)(2,1)S(1)}, u32[]{:S(2)}, u32[]{:S(2)}) async-start(bf16[4,2,256,128]{3,2,1,0:T(8,128)(2,1)} %shard_map.77), calls=%async_computation.1 | async-start | bytes 1048576 | tf_op jit(solution)/shard_map/all_to_all | solution.py:398
  57.0 2.2 %collective-permute-start.3 = (bf16[8,256,128]{2,1,0:T(8,128)(2,1)S(1)}, bf16[8,256,128]{2,1,0:T(8,128)(2,1)S(1)}, u32[]{:S(2)}, u32[]{:S(2)}) collective-permute-start(bf16[8,256,128]{2,1,0:T(8,128)(2,1)S(1)} %all_to_all.15.read_ref), channel_id=1, source_target_pairs={{0,1},{1,0},{2,3},{3,2},{4,5},{5,4},{6,7},{7,6},{8,9},{9,8},{10,11... | collective-permute-start | bytes 1572872 | tf_op jit(solution)/shard_map/ppermute | solution.py:424
